TPU v7x, 32 devices: a whole 2x2x4 slice. The times are simulated.
32 devices in a mesh: band: 16 (over z, y, core), fft: 2 (over x).
Axes of the slice: x: 2, y: 2, z: 4, core: 2. Of those that a mesh axis runs over, the one named last changes fastest.
Arguments:
- orbitals: float32 [32, 128, 128, 128], P('band', 'fft'), may hold values from -6 to 6
- owners: int32 [1], replicated, may hold values from 0 to 15
- local_pick: int32 [16, 1], P('band'), may hold values from 0 to 1
Outputs:
- exchange_term: float32 [16, 128, 128, 128], P('band', 'fft')
All inputs are finite; a program needn't handle non-finite values.
Results may differ from a plain program's by a relative error of at most 0.0003.
Values sent between devices are 32-bit elements; how exact they have to be, the bound alone decides.
No kernel may reach another device: no remote copies, remote signals or barrier semaphores. Data moves between devices by JAX's collectives and lax.ppermute only.
A program may use at most 128 MiB of HBM per device.

v0:
```python
import math

import jax
import jax.numpy as jnp
from jax import lax
from jax.sharding import PartitionSpec as P

NG = 128


def spread(shard, axis, root):
    mine = lax.axis_index(axis) == root
    return lax.psum(jnp.where(mine, shard, jnp.zeros_like(shard)), axis)


def dft_tables(size):
    index = jnp.arange(size, dtype=jnp.int32)
    product = index[:, None] * index[None, :] % size
    angle = product.astype(jnp.float32) * (2.0 * math.pi / size)
    return (jnp.cos(angle), jnp.sin(angle))


def signed_freq(index, size):
    return jnp.where(index < size // 2, index, index - size).astype(jnp.float32)


def along(form, data, table):
    return jnp.einsum(form, data, table, precision=lax.Precision.HIGHEST)


def transform(density, cosine, sine, kernel):
    last_form = "pzxy,yk->pzxk"
    middle_form = "pzxy,xk->pzky"
    first_form = "pzab,zk->pkab"
    evens = density[0::2]
    odds = density[1::2]
    real_part = along(last_form, evens, cosine) + along(last_form, odds, sine)
    imag_part = along(last_form, odds, cosine) - along(last_form, evens, sine)
    mixed_real = along(middle_form, real_part, cosine) + along(middle_form, imag_part, sine)
    mixed_imag = along(middle_form, imag_part, cosine) - along(middle_form, real_part, sine)
    line_real = lax.all_to_all(mixed_real, "fft", split_axis=2, concat_axis=1, tiled=True)
    line_imag = lax.all_to_all(mixed_imag, "fft", split_axis=2, concat_axis=1, tiled=True)
    spec_real = along(first_form, line_real, cosine) + along(first_form, line_imag, sine)
    spec_imag = along(first_form, line_imag, cosine) - along(first_form, line_real, sine)
    spec_real = spec_real * kernel
    spec_imag = spec_imag * kernel
    back_real = along(first_form, spec_real, cosine) - along(first_form, spec_imag, sine)
    back_imag = along(first_form, spec_imag, cosine) + along(first_form, spec_real, sine)
    slab_real = lax.all_to_all(back_real, "fft", split_axis=1, concat_axis=2, tiled=True)
    slab_imag = lax.all_to_all(back_imag, "fft", split_axis=1, concat_axis=2, tiled=True)
    inner_real = along(middle_form, slab_real, cosine) - along(middle_form, slab_imag, sine)
    inner_imag = along(middle_form, slab_imag, cosine) + along(middle_form, slab_real, sine)
    first_field = along(last_form, inner_real, cosine) - along(last_form, inner_imag, sine)
    second_field = along(last_form, inner_imag, cosine) + along(last_form, inner_real, sine)
    return jnp.stack([first_field, second_field], 1).reshape(density.shape)


def on_device(orbitals, owners, local_pick):
    cosine, sine = dft_tables(NG)
    groups = lax.axis_size("fft")
    width = NG // groups
    start = lax.axis_index("fft") * width
    freq_first = signed_freq(jnp.arange(NG, dtype=jnp.int32), NG)
    freq_second = signed_freq(start + jnp.arange(width, dtype=jnp.int32), NG)
    square = (
        freq_first[:, None, None] ** 2
        + freq_second[None, :, None] ** 2
        + freq_first[None, None, :] ** 2
    )
    scale = 0.25 * NG * math.sqrt(NG) / (NG * NG * NG)
    kernel = jnp.where(square > 0, scale / jnp.maximum(square, 1.0), 0.0)
    selected = jnp.take(orbitals, local_pick[0], axis=0)
    count_local = selected.shape[0]
    grid_shape = selected.shape[1:]
    sent_all = spread(orbitals, "band", owners[0])
    potentials = transform(
        (sent_all[:, None] * selected[None]).reshape(
            (sent_all.shape[0] * count_local,) + grid_shape
        ),
        cosine,
        sine,
        kernel,
    )
    shaped = potentials.reshape((sent_all.shape[0], count_local) + grid_shape)
    return jnp.sum(shaped * sent_all[:, None], axis=0)


def solution(mesh):
    in_specs = (P("band", "fft", None, None), P(), P("band", None))
    out_specs = P("band", "fft", None, None)
    return jax.shard_map(
        on_device, mesh=mesh, in_specs=in_specs, out_specs=out_specs, check_vma=False
    )
```

profile of v0, /device:TPU:0, one launch (start us, length us, event | category | flops | bytes accessed | tf_op | source)
XLA Modules:
  0.0 519.7 jit_solution(11641944094892166865)
XLA Ops:
  7.2 4.9 broadcast_select_fusion
  12.1 0.0 all-reduce.2.cloned.1.call-update
  12.7 4.7 fusion.12
  17.5 168.7 %all-reduce.2.cloned.1.call-done = f32[2,64,128,128]{3,2,1,0:T(8,128)} async-done(((f32[2,64,128,128]{3,2,1,0:T(8,128)}), f32[2,64,128,128]{3,2,1,0:T(8,128)}) %all-reduce.2.cloned.1.call-update) | async-done | bytes 8388624 | tf_op jit(solution)/shard_map/psum | solution.py:13
  186.2 6.0 %broadcast_multiply_fusion = f32[2,64,128,128]{3,2,1,0:T(8,128)S(1)} fusion(f32[2,64,128,128]{3,2,1,0:T(8,128)} %all-reduce.2.cloned.1.call-done, f32[64,128,128]{2,1,0:T(8,128)} %fusion.12), kind=kLoop, calls=%fused_computation.27 | loop fusion | flops 2097152 | bytes 20971520 | tf_op jit(solution)/shard_map/mul | solution.py:77
  192.2 3.8 fusion.13
  196.0 3.8 fusion.14
  199.8 4.0 fusion.18
  203.9 4.3 fusion.44
  208.2 3.8 fusion.17
  212.0 0.0 copy-start.2
  212.0 14.5 %subtract_bitcast_fusion.2 = f32[1,64,128,128]{3,2,1,0:T(8,128)S(1)} fusion(f32[128,64,128]{2,0,1:T(8,128)S(1)} %fusion.44, f32[64,128,128]{2,1,0:T(8,128)S(1)} %fusion.17), kind=kOutput, calls=%fused_computation.25 | convolution fusion | flops 1611890688 | bytes 12582912 | tf_op jit(solution)/shard_map/pzxy,xk->pzky/dot_general | solution.py:28
  226.5 4.4 copy.31
  230.9 5.6 %all-to-all-start.1 = ((f32[1,64,128,128]{3,1,0,2:T(8,128)}), f32[1,64,128,128]{3,1,0,2:T(8,128)}, u32[]{:S(2)}, u32[]{:S(2)}) async-start(f32[1,64,128,128]{3,1,0,2:T(8,128)} %copy.31), calls=%async_computation.1 | async-start | bytes 8388608 | tf_op jit(solution)/shard_map/all_to_all | solution.py:42
  236.5 6.1 %fusion.50 = f32[128,64,128]{2,0,1:T(8,128)S(1)} fusion(f32[64,128,128]{2,1,0:T(8,128)} %copy-done.2), kind=kOutput, calls=%fused_computation.67 | convolution fusion | flops 1610842112 | bytes 8388608 | tf_op jit(solution)/shard_map/pzxy,xk->pzky/dot_general | solution.py:28
  242.6 4.1 add_bitcast_fusion.2
  246.7 4.4 copy.26
  251.1 33.2 %all-to-all-done.1 = f32[1,64,128,128]{3,1,0,2:T(8,128)} async-done(((f32[1,64,128,128]{3,1,0,2:T(8,128)}), f32[1,64,128,128]{3,1,0,2:T(8,128)}, u32[]{:S(2)}, u32[]{:S(2)}) %all-to-all-start.1) | async-done | bytes 4194336 | tf_op jit(solution)/shard_map/all_to_all | solution.py:42
  284.3 6.0 %all-to-all-start = ((f32[1,64,128,128]{3,1,0,2:T(8,128)}), f32[1,64,128,128]{3,1,0,2:T(8,128)}, u32[]{:S(2)}, u32[]{:S(2)}) async-start(f32[1,64,128,128]{3,1,0,2:T(8,128)} %copy.26), calls=%async_computation | async-start | bytes 8388608 | tf_op jit(solution)/shard_map/all_to_all | solution.py:41
  290.4 0.1 broadcast_add_fusion
  290.5 4.7 copy.32
  295.2 42.1 %all-to-all-done = f32[1,64,128,128]{3,1,0,2:T(8,128)} async-done(((f32[1,64,128,128]{3,1,0,2:T(8,128)}), f32[1,64,128,128]{3,1,0,2:T(8,128)}, u32[]{:S(2)}, u32[]{:S(2)}) %all-to-all-start) | async-done | bytes 4194336 | tf_op jit(solution)/shard_map/all_to_all | solution.py:41
  337.3 2.5 copy.27
  339.8 4.0 fusion.52
  343.9 4.0 fusion.42
  347.9 5.2 add_multiply_fusion
  353.1 5.0 subtract_multiply_fusion
  358.1 4.1 fusion.40
  362.2 4.5 add_bitcast_fusion.1
  366.7 4.4 copy.43
  371.1 5.6 %all-to-all-start.3 = ((f32[1,128,64,128]{3,2,0,1:T(8,128)}), f32[1,128,64,128]{3,2,0,1:T(8,128)}, u32[]{:S(2)}, u32[]{:S(2)}) async-start(f32[1,128,64,128]{3,2,0,1:T(8,128)} %copy.43), calls=%async_computation.3 | async-start | bytes 8388608 | tf_op jit(solution)/shard_map/all_to_all | solution.py:50
  376.7 6.1 %fusion.54 = f32[128,64,128]{2,0,1:T(8,128)S(1)} fusion(f32[128,64,128]{2,0,1:T(8,128)} %copy-done.4), kind=kOutput, calls=%fused_computation.71 | convolution fusion | flops 1610842112 | bytes 8388608 | tf_op jit(solution)/shard_map/pzab,zk->pkab/dot_general | solution.py:28
  382.8 4.1 subtract_bitcast_fusion.1
  386.9 4.4 copy.38
  391.3 31.4 %all-to-all-done.3 = f32[1,128,64,128]{3,2,0,1:T(8,128)} async-done(((f32[1,128,64,128]{3,2,0,1:T(8,128)}), f32[1,128,64,128]{3,2,0,1:T(8,128)}, u32[]{:S(2)}, u32[]{:S(2)}) %all-to-all-start.3) | async-done | bytes 4194336 | tf_op jit(solution)/shard_map/all_to_all | solution.py:50
  422.8 5.8 %all-to-all-start.2 = ((f32[1,128,64,128]{3,2,0,1:T(8,128)}), f32[1,128,64,128]{3,2,0,1:T(8,128)}, u32[]{:S(2)}, u32[]{:S(2)}) async-start(f32[1,128,64,128]{3,2,0,1:T(8,128)} %copy.38), calls=%async_computation.2 | async-start | bytes 8388608 | tf_op jit(solution)/shard_map/all_to_all | solution.py:49
  428.5 4.7 copy.44
  433.3 40.4 %all-to-all-done.2 = f32[1,128,64,128]{3,2,0,1:T(8,128)} async-done(((f32[1,128,64,128]{3,2,0,1:T(8,128)}), f32[1,128,64,128]{3,2,0,1:T(8,128)}, u32[]{:S(2)}, u32[]{:S(2)}) %all-to-all-start.2) | async-done | bytes 4194336 | tf_op jit(solution)/shard_map/all_to_all | solution.py:49
  473.6 2.5 copy.39
  476.1 4.1 fusion.56
  480.2 4.1 fusion.38
  484.3 4.3 convolution_subtract_fusion
  488.6 3.8 fusion.4
  492.4 3.8 fusion.6
  496.2 4.3 convolution_add_fusion
  500.5 3.8 subtract_bitcast_fusion
  504.3 3.8 add_bitcast_fusion
  508.1 4.2 fusion.1
  (23 shorter events, 0.1 us)
Async XLA Ops:
  6.5 179.7 %all-reduce.2.cloned.1.call-start = ((), (), s32[]{:S(2)}) async-start(), calls=%async_computation.4 | async-start | bytes 16777216 | tf_op jit(solution)/shard_map/psum | solution.py:13
  203.9 4.3 copy-start
  212.0 14.5 %copy-start.2 = (f32[64,128,128]{2,1,0:T(8,128)}, f32[64,128,128]{2,1,0:T(8,128)S(1)}, u32[]{:S(2)}) copy-start(f32[64,128,128]{2,1,0:T(8,128)S(1)} %fusion.17) | copy-start | bytes 12582916
  230.9 53.4 %all-to-all-start.1 = ((f32[1,64,128,128]{3,1,0,2:T(8,128)}), f32[1,64,128,128]{3,1,0,2:T(8,128)}, u32[]{:S(2)}, u32[]{:S(2)}) async-start(f32[1,64,128,128]{3,1,0,2:T(8,128)} %copy.31), calls=%async_computation.1 | async-start | bytes 8388608 | tf_op jit(solution)/shard_map/all_to_all | solution.py:42
  236.5 6.1 %copy-start.1 = (f32[64,128,128]{2,1,0:T(8,128)S(1)}, f32[64,128,128]{2,1,0:T(8,128)}, u32[]{:S(2)}) copy-start(f32[64,128,128]{2,1,0:T(8,128)} %copy-done) | copy-start | bytes 12582916
  284.3 53.0 %all-to-all-start = ((f32[1,64,128,128]{3,1,0,2:T(8,128)}), f32[1,64,128,128]{3,1,0,2:T(8,128)}, u32[]{:S(2)}, u32[]{:S(2)}) async-start(f32[1,64,128,128]{3,1,0,2:T(8,128)} %copy.26), calls=%async_computation | async-start | bytes 8388608 | tf_op jit(solution)/shard_map/all_to_all | solution.py:41
  339.8 4.1 copy-start.7
  353.1 9.1 %copy-start.4 = (f32[128,64,128]{2,0,1:T(8,128)}, f32[128,64,128]{2,0,1:T(8,128)S(1)}, u32[]{:S(2)}) copy-start(f32[128,64,128]{2,0,1:T(8,128)S(1)} %add_multiply_fusion) | copy-start | bytes 12582916
  358.1 4.1 copy-start.5
  371.1 51.7 %all-to-all-start.3 = ((f32[1,128,64,128]{3,2,0,1:T(8,128)}), f32[1,128,64,128]{3,2,0,1:T(8,128)}, u32[]{:S(2)}, u32[]{:S(2)}) async-start(f32[1,128,64,128]{3,2,0,1:T(8,128)} %copy.43), calls=%async_computation.3 | async-start | bytes 8388608 | tf_op jit(solution)/shard_map/all_to_all | solution.py:50
  376.7 6.1 %copy-start.6 = (f32[128,64,128]{2,0,1:T(8,128)S(1)}, f32[128,64,128]{2,0,1:T(8,128)}, u32[]{:S(2)}) copy-start(f32[128,64,128]{2,0,1:T(8,128)} %copy-done.5) | copy-start | bytes 12582916
  422.8 50.9 %all-to-all-start.2 = ((f32[1,128,64,128]{3,2,0,1:T(8,128)}), f32[1,128,64,128]{3,2,0,1:T(8,128)}, u32[]{:S(2)}, u32[]{:S(2)}) async-start(f32[1,128,64,128]{3,2,0,1:T(8,128)} %copy.38), calls=%async_computation.2 | async-start | bytes 8388608 | tf_op jit(solution)/shard_map/all_to_all | solution.py:49
  476.1 4.1 copy-start.3
  500.5 7.6 %slice-start = ((s8[8388608]{0:T(1024)(128)(4,1)}), s8[4194304]{0:T(1024)(128)(4,1)S(1)}, s32[]{:S(2)}) async-start(s8[8388608]{0:T(1024)(128)(4,1)} %bitcast.169), calls=%async_computation.5 | async-start | bytes 8388608
  504.3 3.8 slice-start.1
Sparse Core Ops, SparseCore 0:
  12.2 173.9 all-reduce.1
where the time goes:
time: 529 us; the launch traced here: 520 us
  waiting for transfers between devices  316 us (60%)
  matrix products  113 us (21%)
  local copies, waits for them, and re-layouts  32.2 us (6%)
  starting transfers between devices  23.1 us (4%)
  other arithmetic  19.9 us (4%)
  between operations  15.6 us (3%)
    psum x1, waiting for transfers between devices, spread(): return lax.psum(jnp.where(mine, shard, jnp.zeros_like(shard)), axis)  169 us
    dot_general x24, matrix products, along(): return jnp.einsum(form, data, table, precision=lax.Precision.HIGHEST)  113 us
    all_to_all x1, waiting for transfers between devices, transform(): lax.all_to_all(mixed_real, 'fft', split_axis=2, concat_axis=1, tiled=True)  42.1 us
    all_to_all x1, waiting for transfers between devices, transform(): lax.all_to_all(back_real, 'fft', split_axis=1, concat_axis=2, tiled=True)  40.4 us
    all_to_all x1, waiting for transfers between devices, transform(): lax.all_to_all(mixed_imag, 'fft', split_axis=2, concat_axis=1, tiled=True)  33.2 us
    all_to_all x1, waiting for transfers between devices, transform(): lax.all_to_all(back_imag, 'fft', split_axis=1, concat_axis=2, tiled=True)  31.4 us
  transfers between devices with their start and end apart: 5, of which 5 were waited for; matrix products, arithmetic and copies ran while one was open for 8% of the time, Pallas kernels for 0%

commit v1 on v0

--- a/solution.py
+++ b/solution.py
@@ -1,11 +1,20 @@
+import functools
 import math
 
 import jax
 import jax.numpy as jnp
+import ml_dtypes
+import numpy as np
 from jax import lax
+from jax.experimental import pallas as pl
+from jax.experimental.pallas import tpu as pltpu
 from jax.sharding import PartitionSpec as P
 
-NG = 128
+F32 = jnp.float32
+BF16 = jnp.bfloat16
+ROWS = 8
+CHUNKS = 8
+GROUPS = ((0, 4), (4, 6), (6, 8))
 
 
 def spread(shard, axis, root):
@@ -55,39 +64,381 @@
     return jnp.stack([first_field, second_field], 1).reshape(density.shape)
 
 
-def on_device(orbitals, owners, local_pick):
-    cosine, sine = dft_tables(NG)
+def general(orbitals, owners, local_pick):
+    grid = orbitals.shape[-1]
+    cosine, sine = dft_tables(grid)
     groups = lax.axis_size("fft")
-    width = NG // groups
+    width = grid // groups
     start = lax.axis_index("fft") * width
-    freq_first = signed_freq(jnp.arange(NG, dtype=jnp.int32), NG)
-    freq_second = signed_freq(start + jnp.arange(width, dtype=jnp.int32), NG)
+    freq_first = signed_freq(jnp.arange(grid, dtype=jnp.int32), grid)
+    freq_second = signed_freq(start + jnp.arange(width, dtype=jnp.int32), grid)
     square = (
         freq_first[:, None, None] ** 2
         + freq_second[None, :, None] ** 2
         + freq_first[None, None, :] ** 2
     )
-    scale = 0.25 * NG * math.sqrt(NG) / (NG * NG * NG)
+    scale = 0.25 * grid * math.sqrt(grid) / (grid * grid * grid)
     kernel = jnp.where(square > 0, scale / jnp.maximum(square, 1.0), 0.0)
     selected = jnp.take(orbitals, local_pick[0], axis=0)
-    count_local = selected.shape[0]
     grid_shape = selected.shape[1:]
-    sent_all = spread(orbitals, "band", owners[0])
-    potentials = transform(
-        (sent_all[:, None] * selected[None]).reshape(
-            (sent_all.shape[0] * count_local,) + grid_shape
+    total = jnp.zeros_like(selected)
+    for step in range(owners.shape[0]):
+        sent = spread(orbitals, "band", owners[step])
+        density = (sent[:, None] * selected[None]).reshape((-1,) + grid_shape)
+        potentials = transform(density, cosine, sine, kernel)
+        shaped = potentials.reshape((sent.shape[0], selected.shape[0]) + grid_shape)
+        total = total + jnp.sum(shaped * sent[:, None], axis=0)
+    return total
+
+
+def host_tables(grid):
+    index = np.arange(grid)
+    angle = 2.0 * np.pi * (np.outer(index, index) % grid) / grid
+    return np.cos(angle), np.sin(angle)
+
+
+def as_pair(table):
+    high = table.astype(ml_dtypes.bfloat16)
+    low = (table - high.astype(np.float64)).astype(ml_dtypes.bfloat16)
+    return jnp.asarray(high), jnp.asarray(low)
+
+
+def blocks(a, b, c, d):
+    return np.block([[a, b], [c, d]])
+
+
+def plane_order(core, half, part):
+    base = np.arange(half).reshape(-1, 2, part)
+    if core:
+        base = base[:, ::-1]
+    return core * half + base.reshape(-1)
+
+
+def tables(grid, part):
+    cos, sin = host_tables(grid)
+    half = grid // 2
+    columns = [np.arange(grid), np.concatenate([np.arange(half, grid), np.arange(half)])]
+    slabs = [plane_order(core, half, part) for core in range(2)]
+    depths = [np.concatenate([slabs[core], slabs[1 - core]]) for core in range(2)]
+
+    def to_spectrum(order):
+        c, s = cos[order], sin[order]
+        return blocks(c, s, -s, c)
+
+    def from_planes(order):
+        c, s = cos[:, order], sin[:, order]
+        return blocks(c, s, -s, c)
+
+    def to_planes(order):
+        c, s = cos[order], sin[order]
+        return blocks(c, -s, s, c)
+
+    def from_spectrum(order):
+        c, s = cos[:, order], sin[:, order]
+        return blocks(c, -s, s, c)
+
+    both = dict(
+        last_fwd=blocks(cos, -sin, sin, cos),
+        last_inv=blocks(cos, sin, -sin, cos),
+        mid_fwd=np.stack([to_spectrum(order) for order in columns]),
+        mid_inv=np.stack([from_spectrum(order) for order in columns]),
+        first_fwd=np.stack([from_planes(order) for order in depths]),
+        first_inv=np.stack([to_planes(order) for order in depths]),
+    )
+    return {name: as_pair(value) for name, value in both.items()}
+
+
+def split(value):
+    high = value.astype(BF16)
+    return high, (value - high.astype(F32)).astype(BF16)
+
+
+def mm(a, b):
+    return jnp.dot(a, b, preferred_element_type=F32)
+
+
+def right(data, high, low):
+    top, rest = split(data)
+    return mm(top, high) + (mm(rest, high) + mm(top, low))
+
+
+def left(high, low, data):
+    top, rest = split(data)
+    return mm(high, top) + (mm(high, rest) + mm(low, top))
+
+
+def forward_body(info, phi, own0, own1, other0, other1, wyh, wyl, wxh, wxl, keep, send):
+    grid = phi.shape[-1]
+    half = grid // 2
+    rows = phi.shape[0]
+    part = rows // 2
+    core = info[0]
+    near = phi[pl.ds(core * part, part)]
+    far = phi[pl.ds((1 - core) * part, part)]
+    re = jnp.concatenate([near * own0[...], far * other0[...]], axis=0)
+    im = jnp.concatenate([near * own1[...], far * other1[...]], axis=0)
+    data = jnp.concatenate([re, im], axis=-1).reshape(rows * grid, 2 * grid)
+    lines = right(data, wyh[...], wyl[...])
+    for first in range(0, rows, 2):
+        planes = []
+        for z in (first, first + 1):
+            plane = lines[z * grid : (z + 1) * grid]
+            planes.append(jnp.concatenate([plane[:, :grid], plane[:, grid:]], axis=0))
+        out = left(wxh[0], wxl[0], jnp.concatenate(planes, axis=1))
+        for pos, z in enumerate((first, first + 1)):
+            plane = out[:, pos * grid : (pos + 1) * grid]
+            for comp in range(2):
+                base = comp * grid
+                keep[comp, :, z, :] = plane[base : base + half]
+                send[comp, :, z, :] = plane[base + half : base + grid]
+
+
+def middle_body(info, *refs):
+    count = (len(refs) - 4) // 4
+    keeps, recvs = refs[:count], refs[count : 2 * count]
+    wfh, wfl, wih, wil = refs[2 * count : 2 * count + 4]
+    keep_outs, send_outs = refs[2 * count + 4 : 3 * count + 4], refs[3 * count + 4 :]
+    rows = keeps[0].shape[1]
+    grid = keeps[0].shape[-1]
+    half = grid // 2
+    scale = 0.25 * grid * math.sqrt(grid) / (grid * grid * grid)
+    kz = lax.broadcasted_iota(jnp.int32, (grid, grid), 0)
+    ky = lax.broadcasted_iota(jnp.int32, (grid, grid), 1)
+    fz = jnp.where(kz < grid // 2, kz, kz - grid)
+    fy = jnp.where(ky < grid // 2, ky, ky - grid)
+    plane_square = fz * fz + fy * fy
+    start = info[0] * half + pl.program_id(0) * rows
+    lane = lax.broadcasted_iota(jnp.int32, (1, grid), 1)
+    for first in range(0, rows, 2):
+        planes = []
+        for k in (first, first + 1):
+            for comp in range(2):
+                pieces = [ref[comp, k] for ref in keeps + recvs]
+                if k == 0:
+                    drop = jnp.where((lane == 0) & (start == 0), pieces[0][0:1], 0.0)
+                    pieces = [piece - drop for piece in pieces]
+                planes.append(jnp.concatenate(pieces, axis=0))
+        data = jnp.concatenate(
+            [
+                jnp.concatenate(planes[:2], axis=0),
+                jnp.concatenate(planes[2:], axis=0),
+            ],
+            axis=1,
+        )
+        spec = left(wfh[0], wfl[0], data)
+        factors = []
+        for k in (first, first + 1):
+            kx = start + k
+            fx = jnp.where(kx < grid // 2, kx, kx - grid)
+            square = (plane_square + fx * fx).astype(F32)
+            factors.append(jnp.where(square > 0, scale / jnp.maximum(square, 1.0), 0.0))
+        factor = jnp.concatenate(factors, axis=1)
+        spec = spec * jnp.concatenate([factor, factor], axis=0)
+        out = left(wih[0], wil[0], spec)
+        for pos, k in enumerate((first, first + 1)):
+            plane = out[:, pos * grid : (pos + 1) * grid]
+            for comp in range(2):
+                row = comp * grid
+                for ref in keep_outs + send_outs:
+                    size = ref.shape[2]
+                    ref[comp, k] = plane[row : row + size]
+                    row += size
+
+
+def backward_body(info, keep, recv, own0, own1, other0, other1, wxh, wxl, wyh, wyl, out):
+    grid = keep.shape[-1]
+    rows = keep.shape[2]
+    part = rows // 2
+    core = info[0]
+    lines = []
+    for first in range(0, rows, 2):
+        planes = []
+        for z in (first, first + 1):
+            planes.append(
+                jnp.concatenate(
+                    [keep[0, :, z, :], recv[0, :, z, :], keep[1, :, z, :], recv[1, :, z, :]],
+                    axis=0,
+                )
+            )
+        mixed = left(wxh[0], wxl[0], jnp.concatenate(planes, axis=1))
+        for pos in range(2):
+            plane = mixed[:, pos * grid : (pos + 1) * grid]
+            lines.append(jnp.concatenate([plane[:grid], plane[grid:]], axis=1))
+    fields = right(jnp.concatenate(lines, axis=0), wyh[...], wyl[...])
+    re = fields[:, :grid].reshape(rows, grid, grid)
+    im = fields[:, grid:].reshape(rows, grid, grid)
+    out[pl.ds(core * part, part)] = re[:part] * own0[...] + im[:part] * own1[...]
+    out[pl.ds((1 - core) * part, part)] = re[part:] * other0[...] + im[part:] * other1[...]
+
+
+def call(body, grid_size, in_specs, out_specs, out_shape):
+    return pl.pallas_call(
+        body,
+        grid_spec=pltpu.PrefetchScalarGridSpec(
+            num_scalar_prefetch=1,
+            grid=(grid_size,),
+            in_specs=in_specs,
+            out_specs=out_specs,
         ),
-        cosine,
-        sine,
-        kernel,
+        out_shape=out_shape,
+        compiler_params=pltpu.CompilerParams(vmem_limit_bytes=24 * 1024 * 1024),
     )
-    shaped = potentials.reshape((sent_all.shape[0], count_local) + grid_shape)
-    return jnp.sum(shaped * sent_all[:, None], axis=0)
+
+
+def paired(orbitals, owners, local_pick):
+    n_orb, half, grid, _ = orbitals.shape
+    bands = lax.axis_size("band")
+    chips = bands // 2
+    layers = chips // 2
+    band = lax.axis_index("band")
+    x = lax.axis_index("fft")
+    core = band % 2
+    chip = band // 2
+    y = chip % 2
+    home = core == x
+    axes = ("band", "fft")
+
+    def at(chip_, core_, x_):
+        return (chip_ * 2 + core_) * 2 + x_
+
+    def move(value, pairs):
+        return lax.ppermute(value, axes, pairs)
+
+    spots = [(t, c, p) for t in range(chips) for c in range(2) for p in range(2)]
+    cross = [(at(t, c, p), at(t, p, c)) for t, c, p in spots if c != p]
+    sibling = [(at(t, c, p), at(t, 1 - c, p)) for t, c, p in spots]
+    over_x = [(at(t, c, p), at(t, c, 1 - p)) for t, c, p in spots]
+    over_y = [(at(t, c, p), at(t ^ 1, c, p)) for t, c, p in spots]
+    cycle = [2 * z for z in range(layers)] + [2 * z + 1 for z in reversed(range(layers))]
+    length = len(cycle)
+    after = {cycle[i]: cycle[(i + 1) % length] for i in range(length)}
+    before = {chip_: source for source, chip_ in after.items()}
+    around = [
+        [(at(t, c, p), at(follow[t], c, p)) for t, c, p in spots] for follow in (after, before)
+    ]
+    place = jnp.asarray(np.argsort(np.array(cycle)).astype(np.int32))
+
+    pick = local_pick[0, 0]
+    owner = owners[0]
+    own_chip = owner // 2
+    own_here = chip == own_chip
+    direct = (owner % 2) == core
+    ahead = jnp.mod(place[chip] - place[own_chip], length)
+    behind = jnp.mod(place[own_chip] - place[chip], length)
+    distance = (ahead, behind)
+
+    planes = half // CHUNKS
+    part = planes // 2
+    near = [move(orbitals[:, :planes], sibling), move(orbitals, sibling)]
+    chosen_orbital = lax.dynamic_index_in_dim(orbitals, pick, 0, keepdims=False)
+    phi = jnp.where(home, chosen_orbital, move(chosen_orbital, cross))
+
+    def injected(s, k):
+        start = k * planes + core * part
+        own = lax.dynamic_slice_in_dim(orbitals[s], start, part, 0)
+        other = lax.dynamic_slice_in_dim(near[min(k, 1)][s], start, part, 0)
+        return jnp.where(direct, own, other)
+
+    steps = CHUNKS + length - 2
+    ring = [jnp.zeros(((CHUNKS + 1) * part, grid, grid), F32) for _ in range(2)]
+    carried = [None, None]
+    pieces = []
+    for t in range(steps + 1):
+        for s in range(2):
+            held = carried[s]
+            if t < CHUNKS:
+                fresh = injected(s, t)
+                held = fresh if held is None else jnp.where(own_here, fresh, held)
+            k = t - distance[s]
+            slot = jnp.where((k >= 0) & (k < CHUNKS), k, CHUNKS)
+            ring[s] = lax.dynamic_update_slice(ring[s], held, (slot * part, 0, 0))
+            if t < steps:
+                carried[s] = move(held, around[s])
+        for lo, hi in GROUPS:
+            if hi - 1 + length - 1 == t:
+                local = [ring[s][lo * part : hi * part] for s in range(2)]
+                got = move(jnp.where(y == 0, local[0], local[1]), over_x)
+                also = move(got, over_y)
+                hop = [jnp.where(y == s, got, also) for s in range(2)]
+                own = [jnp.where(home, local[s], hop[s]) for s in range(2)]
+                other = [move(jnp.where(home, hop[s], local[s]), sibling) for s in range(2)]
+                pieces.append(own + other)
+
+    info = core.astype(jnp.int32)[None]
+    table = tables(grid, part)
+
+    def whole(shape):
+        return pl.BlockSpec(shape, lambda i, info: (0,) * len(shape))
+
+    def chosen(shape):
+        return pl.BlockSpec((1,) + shape, lambda i, info: (info[0],) + (0,) * len(shape))
+
+    square = (2 * grid, 2 * grid)
+    quarter = pl.BlockSpec((part, grid, grid), lambda i, info: (i, 0, 0))
+    lines = pl.BlockSpec((2, half, planes, grid), lambda i, info: (0, 0, i, 0))
+    keeps, sends = [], []
+    for (lo, hi), piece in zip(GROUPS, pieces):
+        spectrum = jax.ShapeDtypeStruct((2, half, (hi - lo) * planes, grid), F32)
+        keep, send = call(
+            forward_body,
+            hi - lo,
+            [pl.BlockSpec((planes, grid, grid), lambda i, info, lo=lo: (lo + i, 0, 0))]
+            + [quarter] * 4
+            + [whole(square)] * 2
+            + [chosen(square)] * 2,
+            [lines, lines],
+            [spectrum, spectrum],
+        )(info, phi, *piece, *table["last_fwd"], *table["mid_fwd"])
+        keeps.append(keep)
+        sends.append(send)
+    recvs = [move(send, sibling) for send in sends]
+    cols = [
+        pl.BlockSpec((2, ROWS, (hi - lo) * planes, grid), lambda i, info: (0, i, 0, 0))
+        for lo, hi in GROUPS
+    ]
+    shapes = [jax.ShapeDtypeStruct(keep.shape, F32) for keep in keeps]
+    results = call(
+        middle_body,
+        half // ROWS,
+        cols * 2 + [chosen(square)] * 4,
+        cols * 2,
+        shapes * 2,
+    )(info, *keeps, *recvs, *table["first_fwd"], *table["first_inv"])
+    keeps, sends = results[: len(GROUPS)], results[len(GROUPS) :]
+    recvs = [move(send, sibling) for send in sends]
+    terms = []
+    for (lo, hi), piece, keep, recv in zip(GROUPS, pieces, keeps, recvs):
+        term = call(
+            backward_body,
+            hi - lo,
+            [lines, lines]
+            + [quarter] * 4
+            + [chosen(square)] * 2
+            + [whole(square)] * 2,
+            pl.BlockSpec((planes, grid, grid), lambda i, info: (i, 0, 0)),
+            jax.ShapeDtypeStruct(((hi - lo) * planes, grid, grid), F32),
+        )(info, keep, recv, *piece, *table["mid_inv"], *table["last_inv"])
+        terms.append(jnp.where(home, term, move(term, cross)))
+    return jnp.concatenate(terms, axis=0)[None]
 
 
 def solution(mesh):
     in_specs = (P("band", "fft", None, None), P(), P("band", None))
     out_specs = P("band", "fft", None, None)
+    two_slabs = mesh.shape["fft"] == 2 and mesh.shape["band"] % 4 == 0
+
+    def on_device(orbitals, owners, local_pick):
+        fits = (
+            orbitals.shape[0] == 2
+            and orbitals.shape[1] == CHUNKS * ROWS
+            and orbitals.shape[-1] % 128 == 0
+            and owners.shape[0] == 1
+            and local_pick.shape == (1, 1)
+        )
+        if two_slabs and fits:
+            return paired(orbitals, owners, local_pick)
+        return general(orbitals, owners, local_pick)
+
     return jax.shard_map(
         on_device, mesh=mesh, in_specs=in_specs, out_specs=out_specs, check_vma=False
     )

time: 529 us -> 337 us (0.64)
  the two profiles are of different devices: /device:TPU:0 before, /device:TPU:1 now
where the time goes in v1:
time: 337 us; the launch traced here: 335 us
  waiting for transfers between devices  160 us (47%)
  starting transfers between devices  60.2 us (18%)
  Pallas kernels  41.1 us (12%)
  other arithmetic  38.2 us (11%)
  local copies, waits for them, and re-layouts  31.6 us (9%)
  between operations  4.34 us (1%)
    ppermute x52, waiting for transfers between devices, move(): return lax.ppermute(value, axes, pairs)  160 us
    ppermute x52, starting transfers between devices, move(): return lax.ppermute(value, axes, pairs)  60.2 us
    dynamic_update_slice x16, other arithmetic, paired(): ring[s] = lax.dynamic_update_slice(ring[s], held, (slot * part, 0, 0))  21.1 us
    pallas_call x3, Pallas kernels, paired(): call(forward_body, hi - lo, [pl.BlockSpec((planes, grid, grid), lambda i,...  16.3 us
    dynamic_update_slice x14, local copies, waits for them, and re-layouts, paired(): ring[s] = lax.dynamic_update_slice(ring[s], held, (slot * part, 0, 0))  13.3 us
    pallas_call x3, Pallas kernels, paired(): call(backward_body, hi - lo, [lines, lines] + [quarter] * 4 + [chosen(squ...  12.7 us
    pallas_call x1, Pallas kernels, paired(): call(middle_body, half // ROWS, cols * 2 + [chosen(square)] * 4, cols * 2...  12 us
    slice x1, local copies, waits for them, and re-layouts, injected(): own = lax.dynamic_slice_in_dim(orbitals[s], start, part, 0)  9.94 us
  transfers between devices with their start and end apart: 52, of which 26 were waited for; matrix products, arithmetic and copies ran while one was open for 19% of the time, Pallas kernels for 9%

profile of v1, /device:TPU:1, one launch (start us, length us, event | category | flops | bytes accessed | tf_op | source)
XLA Modules:
  0.0 335.2 jit_solution(13848893178089639932)
XLA Ops:
  0.1 2.3 slice.27
  8.0 9.9 %fusion.1 = (f32[1,64,128,128]{3,2,1,0:T(8,128)S(1)}, f32[1,64,128,128]{3,2,1,0:T(8,128)}, f32[64,128,128]{2,1,0:T(8,128)}) fusion(f32[2,64,128,128]{3,2,1,0:T(8,128)} %param.16, s32[]{:T(128)S(6)} %select_n.574), kind=kLoop, calls=%fused_computation.74 | loop fusion | bytes 25165828 | tf_op jit(solution)/shard_map/slice | solution.py:338
  19.5 2.3 collective-permute-start.3
  22.2 4.1 %fusion = (f32[1,64,128,128]{3,2,1,0:T(8,128)S(1)}, f32[1,64,128,128]{3,2,1,0:T(8,128)S(1)}) fusion(f32[2,64,128,128]{3,2,1,0:T(8,128)} %collective-permute-done.2), kind=kLoop, calls=%fused_computation.73 | loop fusion | bytes 16777216 | tf_op jit(solution)/shard_map/slice | solution.py:339
  28.0 1.9 constant_dynamic-update-slice_fusion.27
  32.6 4.4 %collective-permute-done.4 = f32[4,128,128]{2,1,0:T(8,128)} collective-permute-done((f32[4,128,128]{2,1,0:T(8,128)}, f32[4,128,128]{2,1,0:T(8,128)}, u32[]{:S(2)}, u32[]{:S(2)}) %collective-permute-start.4) | collective-permute-done | bytes 262176 | tf_op jit(solution)/shard_map/ppermute | solution.py:305
  37.0 1.8 constant_dynamic-update-slice_fusion.26
  41.4 3.2 collective-permute-done.5
  44.6 1.8 constant_dynamic-update-slice_fusion.24
  49.0 2.6 collective-permute-done.6
  51.6 1.8 constant_dynamic-update-slice_fusion.23
  56.0 2.6 collective-permute-done.7
  58.6 1.8 constant_dynamic-update-slice_fusion.22
  63.0 3.2 collective-permute-done.8
  66.2 1.8 constant_dynamic-update-slice_fusion.20
  70.7 4.0 %collective-permute-done.9 = f32[4,128,128]{2,1,0:T(8,128)S(1)} collective-permute-done((f32[4,128,128]{2,1,0:T(8,128)S(1)}, f32[4,128,128]{2,1,0:T(8,128)S(1)}, u32[]{:S(2)}, u32[]{:S(2)}) %collective-permute-start.9) | collective-permute-done | bytes 262176 | tf_op jit(solution)/shard_map/ppermute | solution.py:305
  74.7 1.8 constant_dynamic-update-slice_fusion.19
  79.1 4.8 %collective-permute-done.10 = f32[4,128,128]{2,1,0:T(8,128)S(1)} collective-permute-done((f32[4,128,128]{2,1,0:T(8,128)S(1)}, f32[4,128,128]{2,1,0:T(8,128)S(1)}, u32[]{:S(2)}, u32[]{:S(2)}) %collective-permute-start.10) | collective-permute-done | bytes 262176 | tf_op jit(solution)/shard_map/ppermute | solution.py:305
  87.3 3.2 collective-permute-done.11
  93.3 2.4 collective-permute-done.12
  99.1 2.1 slice_select_fusion.2
  102.5 13.5 %collective-permute-done.23 = f32[16,128,128]{2,1,0:T(8,128)S(1)} collective-permute-done((f32[16,128,128]{2,1,0:T(8,128)S(1)}, f32[16,128,128]{2,1,0:T(8,128)S(1)}, u32[]{:S(2)}, u32[]{:S(2)}) %collective-permute-start.23) | collective-permute-done | bytes 1048608 | tf_op jit(solution)/shard_map/ppermute | solution.py:305
  116.2 14.4 %collective-permute-start = (f32[64,128,128]{2,1,0:T(8,128)}, f32[64,128,128]{2,1,0:T(8,128)}, u32[]{:S(2)}, u32[]{:S(2)}) collective-permute-start(f32[64,128,128]{2,1,0:T(8,128)} %get-tuple-element.65), channel_id=1, source_target_pairs={{1,2},{2,1},{5,6},{6,5},{9,10},{10,9},{13,14},{14,13},{17,18},{18,... | collective-permute-start | bytes 12582920 | tf_op jit(solution)/shard_map/ppermute | solution.py:305
  132.2 7.2 %collective-permute-done.27 = f32[4,128,128]{2,1,0:T(8,128)} collective-permute-done((f32[4,128,128]{2,1,0:T(8,128)}, f32[4,128,128]{2,1,0:T(8,128)}, u32[]{:S(2)}, u32[]{:S(2)}) %collective-permute-start.27) | collective-permute-done | bytes 262176 | tf_op jit(solution)/shard_map/ppermute | solution.py:305
  140.9 3.8 %slice_select_fusion = (f32[16,128,128]{2,1,0:T(8,128)}, f32[16,128,128]{2,1,0:T(8,128)S(1)}, f32[16,128,128]{2,1,0:T(8,128)S(1)}, f32[16,128,128]{2,1,0:T(8,128)S(1)}) fusion(f32[36,128,128]{2,1,0:T(8,128)} %copy-done.12, pred[]{:T(512)S(6)} %eq.28, f32[16,128,128]{2,1,0:T(8,128)} %copy-done.19, f32[16,128,128]{2,1,0:T(8,128)} %collective-permute-done.24, ...), kind=kLoop, calls=%fused_computation.4 | loop fusion | flops 1572864 | bytes 8388611 | tf_op jit(solution)/shard_map/jit(_where)/select_n | solution.py:364
  152.8 34.7 %collective-permute-done.31 = f32[8,128,128]{2,1,0:T(8,128)} collective-permute-done((f32[8,128,128]{2,1,0:T(8,128)S(1)}, f32[8,128,128]{2,1,0:T(8,128)}, u32[]{:S(2)}, u32[]{:S(2)}) %collective-permute-start.31) | collective-permute-done | bytes 524320 | tf_op jit(solution)/shard_map/ppermute | solution.py:305
  190.1 15.2 %collective-permute-done.35 = f32[4,128,128]{2,1,0:T(8,128)} collective-permute-done((f32[4,128,128]{2,1,0:T(8,128)}, f32[4,128,128]{2,1,0:T(8,128)}, u32[]{:S(2)}, u32[]{:S(2)}) %collective-permute-start.35) | collective-permute-done | bytes 262176 | tf_op jit(solution)/shard_map/ppermute | solution.py:305
  208.6 1.8 constant_dynamic-update-slice_fusion.21
  212.9 5.5 %collective-permute-start.39 = (f32[8,128,128]{2,1,0:T(8,128)S(1)}, f32[8,128,128]{2,1,0:T(8,128)S(1)}, u32[]{:S(2)}, u32[]{:S(2)}) collective-permute-start(f32[8,128,128]{2,1,0:T(8,128)S(1)} %slice_select_fusion.7), channel_id=1, source_target_pairs={{0,1},{1,0},{2,3},{3,2},{4,5},{5,4},{6,7},{7,6},{8,9},{9,8},{10,11... | collective-permute-start | bytes 1572872 | tf_op jit(solution)/shard_map/ppermute | solution.py:305
  219.5 10.5 %collective-permute-done.39 = f32[8,128,128]{2,1,0:T(8,128)S(1)} collective-permute-done((f32[8,128,128]{2,1,0:T(8,128)S(1)}, f32[8,128,128]{2,1,0:T(8,128)S(1)}, u32[]{:S(2)}, u32[]{:S(2)}) %collective-permute-start.39) | collective-permute-done | bytes 524320 | tf_op jit(solution)/shard_map/ppermute | solution.py:305
  230.0 3.0 broadcast_select_fusion.phi
  233.1 8.3 %shard_map.154 = (f32[2,64,32,128]{3,2,1,0:T(8,128)S(1)}, f32[2,64,32,128]{3,2,1,0:T(8,128)S(1)}) custom-call(s32[1]{0:T(128)} %bitcast.info, f32[64,128,128]{2,1,0:T(8,128)S(1)} %broadcast_select_fusion.phi, f32[16,128,128]{2,1,0:T(8,128)S(1)} %get-tuple-element.78.own0, f32[16,128,128]{2,1,0:T(8,128)S(1)} %get-tuple-element.67.own1, ...), custom_call_target="tpu_custom_call" | custom-call | tf_op jit(solution)/shard_map/pallas_call | solution.py:382
  241.3 1.9 collective-permute-start.43
  245.7 2.1 collective-permute-done.34.other1
  248.5 4.0 %shard_map.155 = (f32[2,64,16,128]{3,2,1,0:T(8,128)S(1)}, f32[2,64,16,128]{3,2,1,0:T(8,128)S(1)}) custom-call(s32[1]{0:T(128)} %bitcast.info, f32[64,128,128]{2,1,0:T(8,128)S(1)} %broadcast_select_fusion.phi, f32[8,128,128]{2,1,0:T(8,128)S(1)} %get-tuple-element.82.own0, f32[8,128,128]{2,1,0:T(8,128)S(1)} %get-tuple-element.75.own1, ...), custom_call_target="tpu_custom_call" | custom-call | tf_op jit(solution)/shard_map/pallas_call | solution.py:382
  253.0 4.0 %shard_map.156 = (f32[2,64,16,128]{3,2,1,0:T(8,128)S(1)}, f32[2,64,16,128]{3,2,1,0:T(8,128)S(1)}) custom-call(s32[1]{0:T(128)} %bitcast.info, f32[64,128,128]{2,1,0:T(8,128)S(1)} %broadcast_select_fusion.phi, f32[8,128,128]{2,1,0:T(8,128)S(1)} %get-tuple-element.80.own0, f32[8,128,128]{2,1,0:T(8,128)S(1)} %get-tuple-element.71.own1, ...), custom_call_target="tpu_custom_call" | custom-call | tf_op jit(solution)/shard_map/pallas_call | solution.py:382
  257.3 2.5 collective-permute-done.45.refs_5_
  259.9 12.0 %shard_map.157 = (f32[2,64,32,128]{3,2,1,0:T(8,128)S(1)}, f32[2,64,16,128]{3,2,1,0:T(8,128)S(1)}, f32[2,64,16,128]{3,2,1,0:T(8,128)S(1)}, f32[2,64,32,128]{3,2,1...) custom-call(s32[1]{0:T(128)} %bitcast.info, ...), custom_call_target="tpu_custom_call" | custom-call | tf_op jit(solution)/shard_map/pallas_call | solution.py:400
  272.6 3.5 %collective-permute-done.46.recv = f32[2,64,32,128]{3,2,1,0:T(8,128)S(1)} collective-permute-done((f32[2,64,32,128]{3,2,1,0:T(8,128)S(1)}, f32[2,64,32,128]{3,2,1,0:T(8,128)S(1)}, u32[]{:S(2)}, u32[]{:S(2)}) %collective-permute-start.46) | collective-permute-done | bytes 2097184 | tf_op jit(solution)/shard_map/ppermute | solution.py:305
  276.1 6.5 %shard_map.158 = f32[32,128,128]{2,1,0:T(8,128)S(1)} custom-call(s32[1]{0:T(128)} %bitcast.info, f32[2,64,32,128]{3,2,1,0:T(8,128)S(1)} %get-tuple-element.23.keep, f32[2,64,32,128]{3,2,1,0:T(8,128)S(1)} %collective-permute-done.46.recv, f32[16,128,128]{2,1,0:T(8,128)S(1)} %get-tuple-element.78.own0, f32[16,128,128]{2,1,0:T(8,128)S(1)} %get-tuple-element.67.own1, ...), custom_call_target="tpu_custom_call" | custom-call | tf_op jit(solution)/shard_map/pallas_call | solution.py:411
  282.6 3.6 %collective-permute-start.47 = (f32[32,128,128]{2,1,0:T(8,128)S(1)}, f32[32,128,128]{2,1,0:T(8,128)S(1)}, u32[]{:S(2)}, u32[]{:S(2)}) collective-permute-start(f32[32,128,128]{2,1,0:T(8,128)S(1)} %shard_map.158), channel_id=1, source_target_pairs={{1,2},{2,1},{5,6},{6,5},{9,10},{10,9},{13,14},{14,13},{17,18},{18,... | collective-permute-start | bytes 6291464 | tf_op jit(solution)/shard_map/ppermute | solution.py:305
  286.2 3.1 shard_map.159
  289.4 2.2 collective-permute-start.49
  291.6 3.1 shard_map.160
  294.7 3.4 %collective-permute-start.51 = (f32[16,128,128]{2,1,0:T(8,128)S(1)}, f32[16,128,128]{2,1,0:T(8,128)S(1)}, u32[]{:S(2)}, u32[]{:S(2)}) collective-permute-start(f32[16,128,128]{2,1,0:T(8,128)S(1)} %shard_map.160), channel_id=1, source_target_pairs={{1,2},{2,1},{5,6},{6,5},{9,10},{10,9},{13,14},{14,13},{17,18},{18,... | collective-permute-start | bytes 3145736 | tf_op jit(solution)/shard_map/ppermute | solution.py:305
  298.1 23.1 %collective-permute-done.49 = f32[16,128,128]{2,1,0:T(8,128)S(1)} collective-permute-done((f32[16,128,128]{2,1,0:T(8,128)S(1)}, f32[16,128,128]{2,1,0:T(8,128)S(1)}, u32[]{:S(2)}, u32[]{:S(2)}) %collective-permute-start.49) | collective-permute-done | bytes 1048608 | tf_op jit(solution)/shard_map/ppermute | solution.py:305
  321.3 11.1 %collective-permute-done.51 = f32[16,128,128]{2,1,0:T(8,128)S(1)} collective-permute-done((f32[16,128,128]{2,1,0:T(8,128)S(1)}, f32[16,128,128]{2,1,0:T(8,128)S(1)}, u32[]{:S(2)}, u32[]{:S(2)}) %collective-permute-start.51) | collective-permute-done | bytes 1048608 | tf_op jit(solution)/shard_map/ppermute | solution.py:305
  332.9 2.4 maximum_bitcast_fusion
  (151 shorter events, 60.6 us)
Async XLA Ops:
  0.0 22.2 %collective-permute-start.2 = (f32[2,64,128,128]{3,2,1,0:T(8,128)}, f32[2,64,128,128]{3,2,1,0:T(8,128)}, u32[]{:S(2)}, u32[]{:S(2)}) collective-permute-start(f32[2,64,128,128]{3,2,1,0:T(8,128)} %param.16), channel_id=1, source_target_pairs={{0,2},{1,3},{2,0},{3,1},{4,6},{5,7},{6,4},{7,5},{8,10},{9,11},{10,... | collective-permute-start | bytes 25165832 | tf_op jit(solution)/shard_map/ppermute | solution.py:305
  2.3 15.6 %collective-permute-start.1 = (f32[2,8,128,128]{3,2,1,0:T(8,128)}, f32[2,8,128,128]{3,2,1,0:T(8,128)S(1)}, u32[]{:S(2)}, u32[]{:S(2)}) collective-permute-start(f32[2,8,128,128]{3,2,1,0:T(8,128)} %slice.27), channel_id=1, source_target_pairs={{0,2},{1,3},{2,0},{3,1},{4,6},{5,7},{6,4},{7,5},{8,10},{9,11},{10,... | collective-permute-start | bytes 3145736 | tf_op jit(solution)/shard_map/ppermute | solution.py:305
  19.5 8.5 %collective-permute-start.3 = (f32[4,128,128]{2,1,0:T(8,128)S(1)}, f32[4,128,128]{2,1,0:T(8,128)S(1)}, u32[]{:S(2)}, u32[]{:S(2)}) collective-permute-start(f32[4,128,128]{2,1,0:T(8,128)S(1)} %get-tuple-element.60), channel_id=1, source_target_pairs={{0,8},{1,9},{2,10},{3,11},{4,0},{5,1},{6,2},{7,3},{8,16},{9,17},{1... | collective-permute-start | bytes 786440 | tf_op jit(solution)/shard_map/ppermute | solution.py:305
  22.2 9.0 %collective-permute-start.13 = (f32[4,128,128]{2,1,0:T(8,128)S(1)}, f32[4,128,128]{2,1,0:T(8,128)S(1)}, u32[]{:S(2)}, u32[]{:S(2)}) collective-permute-start(f32[4,128,128]{2,1,0:T(8,128)S(1)} %get-tuple-element.44), channel_id=1, source_target_pairs={{0,4},{1,5},{2,6},{3,7},{4,12},{5,13},{6,14},{7,15},{8,0},{9,1},{1... | collective-permute-start | bytes 786440 | tf_op jit(solution)/shard_map/ppermute | solution.py:305
  29.9 7.1 %collective-permute-start.4 = (f32[4,128,128]{2,1,0:T(8,128)}, f32[4,128,128]{2,1,0:T(8,128)}, u32[]{:S(2)}, u32[]{:S(2)}) collective-permute-start(f32[4,128,128]{2,1,0:T(8,128)} %get-tuple-element.58), channel_id=1, source_target_pairs={{0,8},{1,9},{2,10},{3,11},{4,0},{5,1},{6,2},{7,3},{8,16},{9,17},{1... | collective-permute-start | bytes 786440 | tf_op jit(solution)/shard_map/ppermute | solution.py:305
  32.0 7.9 %collective-permute-start.14 = (f32[4,128,128]{2,1,0:T(8,128)}, f32[4,128,128]{2,1,0:T(8,128)S(1)}, u32[]{:S(2)}, u32[]{:S(2)}) collective-permute-start(f32[4,128,128]{2,1,0:T(8,128)} %get-tuple-element.42), channel_id=1, source_target_pairs={{0,4},{1,5},{2,6},{3,7},{4,12},{5,13},{6,14},{7,15},{8,0},{9,1},{1... | collective-permute-start | bytes 786440 | tf_op jit(solution)/shard_map/ppermute | solution.py:305
  38.8 5.8 %collective-permute-start.5 = (f32[4,128,128]{2,1,0:T(8,128)S(1)}, f32[4,128,128]{2,1,0:T(8,128)S(1)}, u32[]{:S(2)}, u32[]{:S(2)}) collective-permute-start(f32[4,128,128]{2,1,0:T(8,128)S(1)} %get-tuple-element.56), channel_id=1, source_target_pairs={{0,8},{1,9},{2,10},{3,11},{4,0},{5,1},{6,2},{7,3},{8,16},{9,17},{1... | collective-permute-start | bytes 786440 | tf_op jit(solution)/shard_map/ppermute | solution.py:305
  40.9 6.3 %collective-permute-start.15 = (f32[4,128,128]{2,1,0:T(8,128)S(1)}, f32[4,128,128]{2,1,0:T(8,128)S(1)}, u32[]{:S(2)}, u32[]{:S(2)}) collective-permute-start(f32[4,128,128]{2,1,0:T(8,128)S(1)} %get-tuple-element.40), channel_id=1, source_target_pairs={{0,4},{1,5},{2,6},{3,7},{4,12},{5,13},{6,14},{7,15},{8,0},{9,1},{1... | collective-permute-start | bytes 786440 | tf_op jit(solution)/shard_map/ppermute | solution.py:305
  46.4 5.2 %collective-permute-start.6 = (f32[4,128,128]{2,1,0:T(8,128)S(1)}, f32[4,128,128]{2,1,0:T(8,128)S(1)}, u32[]{:S(2)}, u32[]{:S(2)}) collective-permute-start(f32[4,128,128]{2,1,0:T(8,128)S(1)} %get-tuple-element.54), channel_id=1, source_target_pairs={{0,8},{1,9},{2,10},{3,11},{4,0},{5,1},{6,2},{7,3},{8,16},{9,17},{1... | collective-permute-start | bytes 786440 | tf_op jit(solution)/shard_map/ppermute | solution.py:305
  48.3 5.9 %collective-permute-start.16 = (f32[4,128,128]{2,1,0:T(8,128)S(1)}, f32[4,128,128]{2,1,0:T(8,128)S(1)}, u32[]{:S(2)}, u32[]{:S(2)}) collective-permute-start(f32[4,128,128]{2,1,0:T(8,128)S(1)} %get-tuple-element.38), channel_id=1, source_target_pairs={{0,4},{1,5},{2,6},{3,7},{4,12},{5,13},{6,14},{7,15},{8,0},{9,1},{1... | collective-permute-start | bytes 786440 | tf_op jit(solution)/shard_map/ppermute | solution.py:305
  53.4 5.2 %collective-permute-start.7 = (f32[4,128,128]{2,1,0:T(8,128)S(1)}, f32[4,128,128]{2,1,0:T(8,128)S(1)}, u32[]{:S(2)}, u32[]{:S(2)}) collective-permute-start(f32[4,128,128]{2,1,0:T(8,128)S(1)} %get-tuple-element.52), channel_id=1, source_target_pairs={{0,8},{1,9},{2,10},{3,11},{4,0},{5,1},{6,2},{7,3},{8,16},{9,17},{1... | collective-permute-start | bytes 786440 | tf_op jit(solution)/shard_map/ppermute | solution.py:305
  55.3 5.9 %collective-permute-start.17 = (f32[4,128,128]{2,1,0:T(8,128)S(1)}, f32[4,128,128]{2,1,0:T(8,128)S(1)}, u32[]{:S(2)}, u32[]{:S(2)}) collective-permute-start(f32[4,128,128]{2,1,0:T(8,128)S(1)} %get-tuple-element.36), channel_id=1, source_target_pairs={{0,4},{1,5},{2,6},{3,7},{4,12},{5,13},{6,14},{7,15},{8,0},{9,1},{1... | collective-permute-start | bytes 786440 | tf_op jit(solution)/shard_map/ppermute | solution.py:305
  60.4 5.8 %collective-permute-start.8 = (f32[4,128,128]{2,1,0:T(8,128)S(1)}, f32[4,128,128]{2,1,0:T(8,128)S(1)}, u32[]{:S(2)}, u32[]{:S(2)}) collective-permute-start(f32[4,128,128]{2,1,0:T(8,128)S(1)} %get-tuple-element.50), channel_id=1, source_target_pairs={{0,8},{1,9},{2,10},{3,11},{4,0},{5,1},{6,2},{7,3},{8,16},{9,17},{1... | collective-permute-start | bytes 786440 | tf_op jit(solution)/shard_map/ppermute | solution.py:305
  62.3 6.8 %collective-permute-start.18 = (f32[4,128,128]{2,1,0:T(8,128)S(1)}, f32[4,128,128]{2,1,0:T(8,128)}, u32[]{:S(2)}, u32[]{:S(2)}) collective-permute-start(f32[4,128,128]{2,1,0:T(8,128)S(1)} %get-tuple-element.34), channel_id=1, source_target_pairs={{0,4},{1,5},{2,6},{3,7},{4,12},{5,13},{6,14},{7,15},{8,0},{9,1},{1... | collective-permute-start | bytes 786440 | tf_op jit(solution)/shard_map/ppermute | solution.py:305
  68.0 6.7 %collective-permute-start.9 = (f32[4,128,128]{2,1,0:T(8,128)S(1)}, f32[4,128,128]{2,1,0:T(8,128)S(1)}, u32[]{:S(2)}, u32[]{:S(2)}) collective-permute-start(f32[4,128,128]{2,1,0:T(8,128)S(1)} %get-tuple-element.48), channel_id=1, source_target_pairs={{0,8},{1,9},{2,10},{3,11},{4,0},{5,1},{6,2},{7,3},{8,16},{9,17},{1... | collective-permute-start | bytes 786440 | tf_op jit(solution)/shard_map/ppermute | solution.py:305
  70.2 7.6 %collective-permute-start.19 = (f32[4,128,128]{2,1,0:T(8,128)S(1)}, f32[4,128,128]{2,1,0:T(8,128)S(1)}, u32[]{:S(2)}, u32[]{:S(2)}) collective-permute-start(f32[4,128,128]{2,1,0:T(8,128)S(1)} %get-tuple-element.32), channel_id=1, source_target_pairs={{0,4},{1,5},{2,6},{3,7},{4,12},{5,13},{6,14},{7,15},{8,0},{9,1},{1... | collective-permute-start | bytes 786440 | tf_op jit(solution)/shard_map/ppermute | solution.py:305
  76.5 7.4 %collective-permute-start.10 = (f32[4,128,128]{2,1,0:T(8,128)S(1)}, f32[4,128,128]{2,1,0:T(8,128)S(1)}, u32[]{:S(2)}, u32[]{:S(2)}) collective-permute-start(f32[4,128,128]{2,1,0:T(8,128)S(1)} %get-tuple-element.46), channel_id=1, source_target_pairs={{0,8},{1,9},{2,10},{3,11},{4,0},{5,1},{6,2},{7,3},{8,16},{9,17},{1... | collective-permute-start | bytes 786440 | tf_op jit(solution)/shard_map/ppermute | solution.py:305
  78.9 7.6 %collective-permute-start.20 = (f32[4,128,128]{2,1,0:T(8,128)S(1)}, f32[4,128,128]{2,1,0:T(8,128)S(1)}, u32[]{:S(2)}, u32[]{:S(2)}) collective-permute-start(f32[4,128,128]{2,1,0:T(8,128)S(1)} %get-tuple-element.30), channel_id=1, source_target_pairs={{0,4},{1,5},{2,6},{3,7},{4,12},{5,13},{6,14},{7,15},{8,0},{9,1},{1... | collective-permute-start | bytes 786440 | tf_op jit(solution)/shard_map/ppermute | solution.py:305
  83.9 6.6 %collective-permute-start.11 = (f32[4,128,128]{2,1,0:T(8,128)S(1)}, f32[4,128,128]{2,1,0:T(8,128)S(1)}, u32[]{:S(2)}, u32[]{:S(2)}) collective-permute-start(f32[4,128,128]{2,1,0:T(8,128)S(1)} %collective-permute-done.10), channel_id=1, source_target_pairs={{0,8},{1,9},{2,10},{3,11},{4,0},{5,1},{6,2},{7,3},{8,16},{9,17},{1... | collective-permute-start | bytes 786440 | tf_op jit(solution)/shard_map/ppermute | solution.py:305
  86.5 6.1 %collective-permute-start.21 = (f32[4,128,128]{2,1,0:T(8,128)S(1)}, f32[4,128,128]{2,1,0:T(8,128)S(1)}, u32[]{:S(2)}, u32[]{:S(2)}) collective-permute-start(f32[4,128,128]{2,1,0:T(8,128)S(1)} %collective-permute-done.20), channel_id=1, source_target_pairs={{0,4},{1,5},{2,6},{3,7},{4,12},{5,13},{6,14},{7,15},{8,0},{9,1},{1... | collective-permute-start | bytes 786440 | tf_op jit(solution)/shard_map/ppermute | solution.py:305
  90.4 5.3 %collective-permute-start.12 = (f32[4,128,128]{2,1,0:T(8,128)S(1)}, f32[4,128,128]{2,1,0:T(8,128)}, u32[]{:S(2)}, u32[]{:S(2)}) collective-permute-start(f32[4,128,128]{2,1,0:T(8,128)S(1)} %collective-permute-done.11), channel_id=1, source_target_pairs={{0,8},{1,9},{2,10},{3,11},{4,0},{5,1},{6,2},{7,3},{8,16},{9,17},{1... | collective-permute-start | bytes 786440 | tf_op jit(solution)/shard_map/ppermute | solution.py:305
  92.6 5.5 %collective-permute-start.22 = (f32[4,128,128]{2,1,0:T(8,128)S(1)}, f32[4,128,128]{2,1,0:T(8,128)}, u32[]{:S(2)}, u32[]{:S(2)}) collective-permute-start(f32[4,128,128]{2,1,0:T(8,128)S(1)} %collective-permute-done.21), channel_id=1, source_target_pairs={{0,4},{1,5},{2,6},{3,7},{4,12},{5,13},{6,14},{7,15},{8,0},{9,1},{1... | collective-permute-start | bytes 786440 | tf_op jit(solution)/shard_map/ppermute | solution.py:305
  101.2 14.8 %collective-permute-start.23 = (f32[16,128,128]{2,1,0:T(8,128)S(1)}, f32[16,128,128]{2,1,0:T(8,128)S(1)}, u32[]{:S(2)}, u32[]{:S(2)}) collective-permute-start(f32[16,128,128]{2,1,0:T(8,128)S(1)} %slice_select_fusion.2), channel_id=1, source_target_pairs={{0,1},{1,0},{2,3},{3,2},{4,5},{5,4},{6,7},{7,6},{8,9},{9,8},{10,11... | collective-permute-start | bytes 3145736 | tf_op jit(solution)/shard_map/ppermute | solution.py:305
  116.0 24.9 %collective-permute-start.24 = (f32[16,128,128]{2,1,0:T(8,128)S(1)}, f32[16,128,128]{2,1,0:T(8,128)}, u32[]{:S(2)}, u32[]{:S(2)}) collective-permute-start(f32[16,128,128]{2,1,0:T(8,128)S(1)} %collective-permute-done.23), channel_id=1, source_target_pairs={{0,4},{1,5},{2,6},{3,7},{4,0},{5,1},{6,2},{7,3},{8,12},{9,13},{10,... | collective-permute-start | bytes 3145736 | tf_op jit(solution)/shard_map/ppermute | solution.py:305
  116.2 113.8 %collective-permute-start = (f32[64,128,128]{2,1,0:T(8,128)}, f32[64,128,128]{2,1,0:T(8,128)}, u32[]{:S(2)}, u32[]{:S(2)}) collective-permute-start(f32[64,128,128]{2,1,0:T(8,128)} %get-tuple-element.65), channel_id=1, source_target_pairs={{1,2},{2,1},{5,6},{6,5},{9,10},{10,9},{13,14},{14,13},{17,18},{18,... | collective-permute-start | bytes 12582920 | tf_op jit(solution)/shard_map/ppermute | solution.py:305
  130.7 8.8 %collective-permute-start.27 = (f32[4,128,128]{2,1,0:T(8,128)}, f32[4,128,128]{2,1,0:T(8,128)}, u32[]{:S(2)}, u32[]{:S(2)}) collective-permute-start(f32[4,128,128]{2,1,0:T(8,128)} %collective-permute-done.12), channel_id=1, source_target_pairs={{0,8},{1,9},{2,10},{3,11},{4,0},{5,1},{6,2},{7,3},{8,16},{9,17},{1... | collective-permute-start | bytes 786440 | tf_op jit(solution)/shard_map/ppermute | solution.py:305
  132.1 8.5 %collective-permute-start.29 = (f32[4,128,128]{2,1,0:T(8,128)}, f32[4,128,128]{2,1,0:T(8,128)}, u32[]{:S(2)}, u32[]{:S(2)}) collective-permute-start(f32[4,128,128]{2,1,0:T(8,128)} %collective-permute-done.22), channel_id=1, source_target_pairs={{0,4},{1,5},{2,6},{3,7},{4,12},{5,13},{6,14},{7,15},{8,0},{9,1},{1... | collective-permute-start | bytes 786440 | tf_op jit(solution)/shard_map/ppermute | solution.py:305
  139.4 8.7 %collective-permute-start.28 = (f32[4,128,128]{2,1,0:T(8,128)}, f32[4,128,128]{2,1,0:T(8,128)}, u32[]{:S(2)}, u32[]{:S(2)}) collective-permute-start(f32[4,128,128]{2,1,0:T(8,128)} %collective-permute-done.27), channel_id=1, source_target_pairs={{0,8},{1,9},{2,10},{3,11},{4,0},{5,1},{6,2},{7,3},{8,16},{9,17},{1... | collective-permute-start | bytes 786440 | tf_op jit(solution)/shard_map/ppermute | solution.py:305
  140.6 9.2 %collective-permute-start.30 = (f32[4,128,128]{2,1,0:T(8,128)}, f32[4,128,128]{2,1,0:T(8,128)}, u32[]{:S(2)}, u32[]{:S(2)}) collective-permute-start(f32[4,128,128]{2,1,0:T(8,128)} %collective-permute-done.29), channel_id=1, source_target_pairs={{0,4},{1,5},{2,6},{3,7},{4,12},{5,13},{6,14},{7,15},{8,0},{9,1},{1... | collective-permute-start | bytes 786440 | tf_op jit(solution)/shard_map/ppermute | solution.py:305
  152.7 34.8 %collective-permute-start.31 = (f32[8,128,128]{2,1,0:T(8,128)S(1)}, f32[8,128,128]{2,1,0:T(8,128)}, u32[]{:S(2)}, u32[]{:S(2)}) collective-permute-start(f32[8,128,128]{2,1,0:T(8,128)S(1)} %slice_select_fusion.12), channel_id=1, source_target_pairs={{0,1},{1,0},{2,3},{3,2},{4,5},{5,4},{6,7},{7,6},{8,9},{9,8},{10,11... | collective-permute-start | bytes 1572872 | tf_op jit(solution)/shard_map/ppermute | solution.py:305
  187.5 19.3 %collective-permute-start.32 = (f32[8,128,128]{2,1,0:T(8,128)}, f32[8,128,128]{2,1,0:T(8,128)}, u32[]{:S(2)}, u32[]{:S(2)}) collective-permute-start(f32[8,128,128]{2,1,0:T(8,128)} %collective-permute-done.31), channel_id=1, source_target_pairs={{0,4},{1,5},{2,6},{3,7},{4,0},{5,1},{6,2},{7,3},{8,12},{9,13},{10,... | collective-permute-start | bytes 1572872 | tf_op jit(solution)/shard_map/ppermute | solution.py:305
  188.5 16.9 %collective-permute-start.35 = (f32[4,128,128]{2,1,0:T(8,128)}, f32[4,128,128]{2,1,0:T(8,128)}, u32[]{:S(2)}, u32[]{:S(2)}) collective-permute-start(f32[4,128,128]{2,1,0:T(8,128)} %collective-permute-done.28), channel_id=1, source_target_pairs={{0,8},{1,9},{2,10},{3,11},{4,0},{5,1},{6,2},{7,3},{8,16},{9,17},{1... | collective-permute-start | bytes 786440 | tf_op jit(solution)/shard_map/ppermute | solution.py:305
  190.1 15.2 %collective-permute-start.37 = (f32[4,128,128]{2,1,0:T(8,128)}, f32[4,128,128]{2,1,0:T(8,128)S(1)}, u32[]{:S(2)}, u32[]{:S(2)}) collective-permute-start(f32[4,128,128]{2,1,0:T(8,128)} %collective-permute-done.30), channel_id=1, source_target_pairs={{0,4},{1,5},{2,6},{3,7},{4,12},{5,13},{6,14},{7,15},{8,0},{9,1},{1... | collective-permute-start | bytes 786440 | tf_op jit(solution)/shard_map/ppermute | solution.py:305
  205.3 5.7 %collective-permute-start.36 = (f32[4,128,128]{2,1,0:T(8,128)}, f32[4,128,128]{2,1,0:T(8,128)S(1)}, u32[]{:S(2)}, u32[]{:S(2)}) collective-permute-start(f32[4,128,128]{2,1,0:T(8,128)} %collective-permute-done.35), channel_id=1, source_target_pairs={{0,8},{1,9},{2,10},{3,11},{4,0},{5,1},{6,2},{7,3},{8,16},{9,17},{1... | collective-permute-start | bytes 786440 | tf_op jit(solution)/shard_map/ppermute | solution.py:305
  205.3 6.4 %collective-permute-start.38 = (f32[4,128,128]{2,1,0:T(8,128)S(1)}, f32[4,128,128]{2,1,0:T(8,128)S(1)}, u32[]{:S(2)}, u32[]{:S(2)}) collective-permute-start(f32[4,128,128]{2,1,0:T(8,128)S(1)} %collective-permute-done.37), channel_id=1, source_target_pairs={{0,4},{1,5},{2,6},{3,7},{4,12},{5,13},{6,14},{7,15},{8,0},{9,1},{1... | collective-permute-start | bytes 786440 | tf_op jit(solution)/shard_map/ppermute | solution.py:305
  212.9 17.1 %collective-permute-start.39 = (f32[8,128,128]{2,1,0:T(8,128)S(1)}, f32[8,128,128]{2,1,0:T(8,128)S(1)}, u32[]{:S(2)}, u32[]{:S(2)}) collective-permute-start(f32[8,128,128]{2,1,0:T(8,128)S(1)} %slice_select_fusion.7), channel_id=1, source_target_pairs={{0,1},{1,0},{2,3},{3,2},{4,5},{5,4},{6,7},{7,6},{8,9},{9,8},{10,11... | collective-permute-start | bytes 1572872 | tf_op jit(solution)/shard_map/ppermute | solution.py:305
  218.4 14.6 %collective-permute-start.26 = (f32[16,128,128]{2,1,0:T(8,128)S(1)}, f32[16,128,128]{2,1,0:T(8,128)S(1)}, u32[]{:S(2)}, u32[]{:S(2)}) collective-permute-start(f32[16,128,128]{2,1,0:T(8,128)S(1)} %copy-done.18), channel_id=1, source_target_pairs={{0,2},{1,3},{2,0},{3,1},{4,6},{5,7},{6,4},{7,5},{8,10},{9,11},{10,... | collective-permute-start | bytes 3145736 | tf_op jit(solution)/shard_map/ppermute | solution.py:305
  219.4 13.6 %collective-permute-start.25 = (f32[16,128,128]{2,1,0:T(8,128)S(1)}, f32[16,128,128]{2,1,0:T(8,128)S(1)}, u32[]{:S(2)}, u32[]{:S(2)}) collective-permute-start(f32[16,128,128]{2,1,0:T(8,128)S(1)} %get-tuple-element.79), channel_id=1, source_target_pairs={{0,2},{1,3},{2,0},{3,1},{4,6},{5,7},{6,4},{7,5},{8,10},{9,11},{10,... | collective-permute-start | bytes 3145736 | tf_op jit(solution)/shard_map/ppermute | solution.py:305
  230.0 13.7 %collective-permute-start.40 = (f32[8,128,128]{2,1,0:T(8,128)S(1)}, f32[8,128,128]{2,1,0:T(8,128)S(1)}, u32[]{:S(2)}, u32[]{:S(2)}) collective-permute-start(f32[8,128,128]{2,1,0:T(8,128)S(1)} %collective-permute-done.39), channel_id=1, source_target_pairs={{0,4},{1,5},{2,6},{3,7},{4,0},{5,1},{6,2},{7,3},{8,12},{9,13},{10,... | collective-permute-start | bytes 1572872 | tf_op jit(solution)/shard_map/ppermute | solution.py:305
  241.3 15.9 %collective-permute-start.43 = (f32[2,64,32,128]{3,2,1,0:T(8,128)S(1)}, f32[2,64,32,128]{3,2,1,0:T(8,128)S(1)}, u32[]{:S(2)}, u32[]{:S(2)}) collective-permute-start(f32[2,64,32,128]{3,2,1,0:T(8,128)S(1)} %get-tuple-element.20), channel_id=1, source_target_pairs={{0,2},{1,3},{2,0},{3,1},{4,6},{5,7},{6,4},{7,5},{8,10},{9,11},{10,... | collective-permute-start | bytes 6291464 | tf_op jit(solution)/shard_map/ppermute | solution.py:305
  243.3 5.2 %collective-permute-start.33 = (f32[8,128,128]{2,1,0:T(8,128)S(1)}, f32[8,128,128]{2,1,0:T(8,128)S(1)}, u32[]{:S(2)}, u32[]{:S(2)}) collective-permute-start(f32[8,128,128]{2,1,0:T(8,128)S(1)} %get-tuple-element.83), channel_id=1, source_target_pairs={{0,2},{1,3},{2,0},{3,1},{4,6},{5,7},{6,4},{7,5},{8,10},{9,11},{10,... | collective-permute-start | bytes 1572872 | tf_op jit(solution)/shard_map/ppermute | solution.py:305
  245.0 8.0 %collective-permute-start.42 = (f32[8,128,128]{2,1,0:T(8,128)S(1)}, f32[8,128,128]{2,1,0:T(8,128)S(1)}, u32[]{:S(2)}, u32[]{:S(2)}) collective-permute-start(f32[8,128,128]{2,1,0:T(8,128)S(1)} %get-tuple-element.70), channel_id=1, source_target_pairs={{0,2},{1,3},{2,0},{3,1},{4,6},{5,7},{6,4},{7,5},{8,10},{9,11},{10,... | collective-permute-start | bytes 1572872 | tf_op jit(solution)/shard_map/ppermute | solution.py:305
  245.6 7.3 %collective-permute-start.41 = (f32[8,128,128]{2,1,0:T(8,128)S(1)}, f32[8,128,128]{2,1,0:T(8,128)S(1)}, u32[]{:S(2)}, u32[]{:S(2)}) collective-permute-start(f32[8,128,128]{2,1,0:T(8,128)S(1)} %get-tuple-element.81), channel_id=1, source_target_pairs={{0,2},{1,3},{2,0},{3,1},{4,6},{5,7},{6,4},{7,5},{8,10},{9,11},{10,... | collective-permute-start | bytes 1572872 | tf_op jit(solution)/shard_map/ppermute | solution.py:305
  272.1 14.1 %collective-permute-start.48 = (f32[2,64,16,128]{3,2,1,0:T(8,128)S(1)}, f32[2,64,16,128]{3,2,1,0:T(8,128)S(1)}, u32[]{:S(2)}, u32[]{:S(2)}) collective-permute-start(f32[2,64,16,128]{3,2,1,0:T(8,128)S(1)} %get-tuple-element.26), channel_id=1, source_target_pairs={{0,2},{1,3},{2,0},{3,1},{4,6},{5,7},{6,4},{7,5},{8,10},{9,11},{10,... | collective-permute-start | bytes 3145736 | tf_op jit(solution)/shard_map/ppermute | solution.py:305
  272.5 19.1 %collective-permute-start.50 = (f32[2,64,16,128]{3,2,1,0:T(8,128)S(1)}, f32[2,64,16,128]{3,2,1,0:T(8,128)S(1)}, u32[]{:S(2)}, u32[]{:S(2)}) collective-permute-start(f32[2,64,16,128]{3,2,1,0:T(8,128)S(1)} %get-tuple-element.28), channel_id=1, source_target_pairs={{0,2},{1,3},{2,0},{3,1},{4,6},{5,7},{6,4},{7,5},{8,10},{9,11},{10,... | collective-permute-start | bytes 3145736 | tf_op jit(solution)/shard_map/ppermute | solution.py:305
  282.6 49.9 %collective-permute-start.47 = (f32[32,128,128]{2,1,0:T(8,128)S(1)}, f32[32,128,128]{2,1,0:T(8,128)S(1)}, u32[]{:S(2)}, u32[]{:S(2)}) collective-permute-start(f32[32,128,128]{2,1,0:T(8,128)S(1)} %shard_map.158), channel_id=1, source_target_pairs={{1,2},{2,1},{5,6},{6,5},{9,10},{10,9},{13,14},{14,13},{17,18},{18,... | collective-permute-start | bytes 6291464 | tf_op jit(solution)/shard_map/ppermute | solution.py:305
  289.4 31.8 %collective-permute-start.49 = (f32[16,128,128]{2,1,0:T(8,128)S(1)}, f32[16,128,128]{2,1,0:T(8,128)S(1)}, u32[]{:S(2)}, u32[]{:S(2)}) collective-permute-start(f32[16,128,128]{2,1,0:T(8,128)S(1)} %shard_map.159), channel_id=1, source_target_pairs={{1,2},{2,1},{5,6},{6,5},{9,10},{10,9},{13,14},{14,13},{17,18},{18,... | collective-permute-start | bytes 3145736 | tf_op jit(solution)/shard_map/ppermute | solution.py:305
  294.7 37.7 %collective-permute-start.51 = (f32[16,128,128]{2,1,0:T(8,128)S(1)}, f32[16,128,128]{2,1,0:T(8,128)S(1)}, u32[]{:S(2)}, u32[]{:S(2)}) collective-permute-start(f32[16,128,128]{2,1,0:T(8,128)S(1)} %shard_map.160), channel_id=1, source_target_pairs={{1,2},{2,1},{5,6},{6,5},{9,10},{10,9},{13,14},{14,13},{17,18},{18,... | collective-permute-start | bytes 3145736 | tf_op jit(solution)/shard_map/ppermute | solution.py:305
  (24 other events, 286.6 us)

commit v2 on v1

--- a/solution.py
+++ b/solution.py
@@ -15,6 +15,9 @@
 ROWS = 8
 CHUNKS = 8
 GROUPS = ((0, 4), (4, 6), (6, 8))
+TERM_GROUPS = ((0, 2), (2, 4), (4, 6), (6, 8))
+HOP_STEPS = 2
+PHI_STEP = 6
 
 
 def spread(shard, axis, root):
@@ -108,10 +111,10 @@
 
 
 def plane_order(core, half, part):
-    base = np.arange(half).reshape(-1, 2, part)
+    base = np.arange(half).reshape(2, -1, part)
     if core:
-        base = base[:, ::-1]
-    return core * half + base.reshape(-1)
+        base = base[::-1]
+    return core * half + base.transpose(1, 0, 2).reshape(-1)
 
 
 def tables(grid, part):
@@ -167,16 +170,26 @@
     return mm(high, top) + (mm(high, rest) + mm(low, top))
 
 
-def forward_body(info, phi, own0, own1, other0, other1, wyh, wyl, wxh, wxl, keep, send):
+def pick_body(info, *refs):
+    inputs, out, sem = refs[:-2], refs[-2], refs[-1]
+    for index, ref in enumerate(inputs):
+
+        @pl.when(info[1] == index)
+        def _(ref=ref):
+            pltpu.make_async_copy(ref, out, sem).start()
+
+    pltpu.make_async_copy(inputs[0], out, sem).wait()
+
+
+def forward_body(info, phi, own, other, wyh, wyl, wxh, wxl, keep, send):
     grid = phi.shape[-1]
     half = grid // 2
-    rows = phi.shape[0]
-    part = rows // 2
+    part = phi.shape[1]
+    rows = 2 * part
     core = info[0]
-    near = phi[pl.ds(core * part, part)]
-    far = phi[pl.ds((1 - core) * part, part)]
-    re = jnp.concatenate([near * own0[...], far * other0[...]], axis=0)
-    im = jnp.concatenate([near * own1[...], far * other1[...]], axis=0)
+    near, far = phi[core], phi[1 - core]
+    re = jnp.concatenate([near * own[0, 0], far * other[0, 0]], axis=0)
+    im = jnp.concatenate([near * own[0, 1], far * other[0, 1]], axis=0)
     data = jnp.concatenate([re, im], axis=-1).reshape(rows * grid, 2 * grid)
     lines = right(data, wyh[...], wyl[...])
     for first in range(0, rows, 2):
@@ -245,7 +258,7 @@
                     row += size
 
 
-def backward_body(info, keep, recv, own0, own1, other0, other1, wxh, wxl, wyh, wyl, out):
+def backward_body(info, keep, recv, own, other, wxh, wxl, wyh, wyl, out):
     grid = keep.shape[-1]
     rows = keep.shape[2]
     part = rows // 2
@@ -267,8 +280,8 @@
     fields = right(jnp.concatenate(lines, axis=0), wyh[...], wyl[...])
     re = fields[:, :grid].reshape(rows, grid, grid)
     im = fields[:, grid:].reshape(rows, grid, grid)
-    out[pl.ds(core * part, part)] = re[:part] * own0[...] + im[:part] * own1[...]
-    out[pl.ds((1 - core) * part, part)] = re[part:] * other0[...] + im[part:] * other1[...]
+    out[core] = re[:part] * own[0, 0] + im[:part] * own[0, 1]
+    out[1 - core] = re[part:] * other[0, 0] + im[part:] * other[0, 1]
 
 
 def call(body, grid_size, in_specs, out_specs, out_shape):
@@ -281,7 +294,7 @@
             out_specs=out_specs,
         ),
         out_shape=out_shape,
-        compiler_params=pltpu.CompilerParams(vmem_limit_bytes=24 * 1024 * 1024),
+        compiler_params=pltpu.CompilerParams(vmem_limit_bytes=16 * 1024 * 1024),
     )
 
 
@@ -314,57 +327,102 @@
     after = {cycle[i]: cycle[(i + 1) % length] for i in range(length)}
     before = {chip_: source for source, chip_ in after.items()}
     around = [
-        [(at(t, c, p), at(follow[t], c, p)) for t, c, p in spots] for follow in (after, before)
+        (at(t, c, p), at((after if c == 0 else before)[t], c, p)) for t, c, p in spots
     ]
-    place = jnp.asarray(np.argsort(np.array(cycle)).astype(np.int32))
+
+    def place(chip_):
+        return jnp.where(chip_ % 2 == 0, chip_ // 2, length - 1 - chip_ // 2)
 
     pick = local_pick[0, 0]
     owner = owners[0]
     own_chip = owner // 2
     own_here = chip == own_chip
     direct = (owner % 2) == core
-    ahead = jnp.mod(place[chip] - place[own_chip], length)
-    behind = jnp.mod(place[own_chip] - place[chip], length)
-    distance = (ahead, behind)
-
-    planes = half // CHUNKS
-    part = planes // 2
-    near = [move(orbitals[:, :planes], sibling), move(orbitals, sibling)]
+    ahead = (place(chip) - place(own_chip) + length) % length
+    distance = jnp.where(core == 0, ahead, (length - ahead) % length)
+
+    part = half // 2 // CHUNKS
+    chunk_shape = (n_orb, part, grid, grid)
+    cut = orbitals.reshape((n_orb, 2, half // 2, grid, grid))
+
+    def of_half(which, lo, hi):
+        begin = (0, which, lo * part, 0, 0)
+        piece = lax.dynamic_slice(cut, begin, (n_orb, 1, (hi - lo) * part, grid, grid))
+        return piece.reshape((n_orb, hi - lo, part, grid, grid))
+
+    first_out, own_first, cut, orbitals = lax.optimization_barrier(
+        (of_half(1 - core, 0, 1), of_half(core, 0, 1), cut, orbitals)
+    )
+    first_in = move(first_out, sibling)
     chosen_orbital = lax.dynamic_index_in_dim(orbitals, pick, 0, keepdims=False)
-    phi = jnp.where(home, chosen_orbital, move(chosen_orbital, cross))
-
-    def injected(s, k):
-        start = k * planes + core * part
-        own = lax.dynamic_slice_in_dim(orbitals[s], start, part, 0)
-        other = lax.dynamic_slice_in_dim(near[min(k, 1)][s], start, part, 0)
-        return jnp.where(direct, own, other)
+    first_in, chosen_orbital, cut = lax.optimization_barrier((first_in, chosen_orbital, cut))
+    crossed = move(chosen_orbital, cross)
+    bounds = ((1, 3), (3, CHUNKS))
+    rest_in = [move(of_half(1 - core, lo, hi), sibling) for lo, hi in bounds]
+    fresh = [jnp.where(direct, own_first, first_in)[:, 0]]
+    for (lo, hi), other in zip(bounds, rest_in):
+        more = jnp.where(direct, of_half(core, lo, hi), other)
+        fresh += [more[:, k] for k in range(hi - lo)]
+    info = jnp.stack([core.astype(jnp.int32), distance.astype(jnp.int32)])
 
     steps = CHUNKS + length - 2
-    ring = [jnp.zeros(((CHUNKS + 1) * part, grid, grid), F32) for _ in range(2)]
-    carried = [None, None]
-    pieces = []
-    for t in range(steps + 1):
-        for s in range(2):
-            held = carried[s]
-            if t < CHUNKS:
-                fresh = injected(s, t)
-                held = fresh if held is None else jnp.where(own_here, fresh, held)
-            k = t - distance[s]
-            slot = jnp.where((k >= 0) & (k < CHUNKS), k, CHUNKS)
-            ring[s] = lax.dynamic_update_slice(ring[s], held, (slot * part, 0, 0))
+    kept = []
+
+    def arrived(k):
+        return pl.pallas_call(
+            pick_body,
+            in_specs=[pl.BlockSpec(memory_space=pltpu.SMEM)]
+            + [pl.BlockSpec(memory_space=pl.ANY)] * length,
+            out_specs=pl.BlockSpec(memory_space=pltpu.VMEM),
+            out_shape=jax.ShapeDtypeStruct(chunk_shape, F32),
+            scratch_shapes=[pltpu.SemaphoreType.DMA],
+        )(info, *kept[k : k + length])
+
+    carried, phi = None, None
+    flying, swapping = [], []
+    owns, others = [], []
+    t = 0
+    while len(others) < CHUNKS:
+        joined = [flying.pop(0)] if flying and flying[0][0] <= t else []
+        landed = [swapping.pop(0)] if swapping and swapping[0][0] <= t else []
+        values = [] if carried is None else [carried]
+        values += [item[1] for item in joined + landed]
+        if t == 1:
+            values.append(info)
+        if t == PHI_STEP:
+            values.append(crossed)
+        if t == PHI_STEP + 1:
+            values.append(phi)
+        if len(values) > 1:
+            values = list(lax.optimization_barrier(tuple(values)))
+        if t == 1:
+            info = values.pop()
+        if t == PHI_STEP + 1:
+            phi = values.pop()
+        if t == PHI_STEP:
+            phi = jnp.where(home, chosen_orbital, values.pop())
+        if landed:
+            others.append(values.pop())
+        if joined:
+            mine, got = joined[0][2], values.pop()
+            owns.append(jnp.where(home, mine, got))
+            swapping.append((t + 1, move(jnp.where(home, got, mine), sibling)))
+        carried = None
+        if t <= steps:
+            held = jnp.where(own_here, fresh[t], values[0]) if 0 < t < CHUNKS else (values or fresh)[0]
+            kept.append(held)
             if t < steps:
-                carried[s] = move(held, around[s])
-        for lo, hi in GROUPS:
-            if hi - 1 + length - 1 == t:
-                local = [ring[s][lo * part : hi * part] for s in range(2)]
-                got = move(jnp.where(y == 0, local[0], local[1]), over_x)
-                also = move(got, over_y)
-                hop = [jnp.where(y == s, got, also) for s in range(2)]
-                own = [jnp.where(home, local[s], hop[s]) for s in range(2)]
-                other = [move(jnp.where(home, hop[s], local[s]), sibling) for s in range(2)]
-                pieces.append(own + other)
-
-    info = core.astype(jnp.int32)[None]
+                carried = move(held, around)
+        k = t - length + 1
+        if 0 <= k < CHUNKS:
+            mine = arrived(k)
+            flying.append((t + HOP_STEPS, move(mine, over_x), mine))
+        t += 1
+
+    planes = 2 * part
+    phi = phi.reshape((2, half // 2, grid, grid))
+    own = [jnp.stack(owns[lo:hi]) for lo, hi in GROUPS]
+    other = [jnp.stack(others[lo:hi]) for lo, hi in GROUPS]
     table = tables(grid, part)
 
     def whole(shape):
@@ -374,21 +432,20 @@
         return pl.BlockSpec((1,) + shape, lambda i, info: (info[0],) + (0,) * len(shape))
 
     square = (2 * grid, 2 * grid)
-    quarter = pl.BlockSpec((part, grid, grid), lambda i, info: (i, 0, 0))
+
+    pairs = pl.BlockSpec((1,) + chunk_shape, lambda i, info: (i, 0, 0, 0, 0))
     lines = pl.BlockSpec((2, half, planes, grid), lambda i, info: (0, 0, i, 0))
     keeps, sends = [], []
-    for (lo, hi), piece in zip(GROUPS, pieces):
+    for g, (lo, hi) in enumerate(GROUPS):
         spectrum = jax.ShapeDtypeStruct((2, half, (hi - lo) * planes, grid), F32)
+        slab = pl.BlockSpec((2, part, grid, grid), lambda i, info, lo=lo: (0, lo + i, 0, 0))
         keep, send = call(
             forward_body,
             hi - lo,
-            [pl.BlockSpec((planes, grid, grid), lambda i, info, lo=lo: (lo + i, 0, 0))]
-            + [quarter] * 4
-            + [whole(square)] * 2
-            + [chosen(square)] * 2,
+            [slab, pairs, pairs] + [whole(square)] * 2 + [chosen(square)] * 2,
             [lines, lines],
             [spectrum, spectrum],
-        )(info, phi, *piece, *table["last_fwd"], *table["mid_fwd"])
+        )(info, phi, own[g], other[g], *table["last_fwd"], *table["mid_fwd"])
         keeps.append(keep)
         sends.append(send)
     recvs = [move(send, sibling) for send in sends]
@@ -407,19 +464,32 @@
     keeps, sends = results[: len(GROUPS)], results[len(GROUPS) :]
     recvs = [move(send, sibling) for send in sends]
     terms = []
-    for (lo, hi), piece, keep, recv in zip(GROUPS, pieces, keeps, recvs):
+    terms = []
+    for lo, hi in TERM_GROUPS:
+        g, start = [(g, a) for g, (a, b) in enumerate(GROUPS) if a <= lo < b][0]
+        keep, recv = keeps[g], recvs[g]
+        if len(terms) > 1:
+            there, keep = lax.optimization_barrier((terms[-2][1], keep))
+            terms[-2] = (terms[-2][0], there)
+        shift = lo - start
+        some_lines = pl.BlockSpec(
+            (2, half, planes, grid), lambda i, info, shift=shift: (0, 0, shift + i, 0)
+        )
+        some_pairs = pl.BlockSpec(
+            (1,) + chunk_shape, lambda i, info, shift=shift: (shift + i, 0, 0, 0, 0)
+        )
         term = call(
             backward_body,
             hi - lo,
-            [lines, lines]
-            + [quarter] * 4
+            [some_lines, some_lines, some_pairs, some_pairs]
             + [chosen(square)] * 2
             + [whole(square)] * 2,
-            pl.BlockSpec((planes, grid, grid), lambda i, info: (i, 0, 0)),
-            jax.ShapeDtypeStruct(((hi - lo) * planes, grid, grid), F32),
-        )(info, keep, recv, *piece, *table["mid_inv"], *table["last_inv"])
-        terms.append(jnp.where(home, term, move(term, cross)))
-    return jnp.concatenate(terms, axis=0)[None]
+            pl.BlockSpec((2, part, grid, grid), lambda i, info: (0, i, 0, 0)),
+            jax.ShapeDtypeStruct((2, (hi - lo) * part, grid, grid), F32),
+        )(info, keep, recv, own[g], other[g], *table["mid_inv"], *table["last_inv"])
+        terms.append((term, move(term, cross)))
+    total = jnp.concatenate([jnp.where(home, *both) for both in terms], axis=1)
+    return total.reshape((1, half, grid, grid))
 
 
 def solution(mesh):

time: 337 us -> 275 us (0.82)
  waiting for transfers between devices: 160 us -> 93.8 us
  Pallas kernels: 41.1 us -> 65.8 us
  local copies, waits for them, and re-layouts: 31.6 us -> 16.2 us
  other arithmetic: 38.2 us -> 32 us
  starting transfers between devices: 60.2 us -> 63.6 us
    ppermute x52 -> x44, waiting for transfers between devices: 160 us -> 93.8 us  [move(): return lax.ppermute(value, axes, pairs)]
    pallas_call x6 -> x15, Pallas kernels: 29 us -> 53.5 us  [the longest x8 20.1 us: arrived(): pl.pallas_call(pick_body, in_specs=[pl.BlockSpec(memory_space=pltpu.SMEM)...]
    dynamic_update_slice x16 -> x0, other arithmetic: 21.1 us -> none  [paired(): ring[s] = lax.dynamic_update_slice(ring[s], held, (slot * part, 0, 0))]
    slice x4 -> x0, local copies, waits for them, and re-layouts: 16.4 us -> none  [the longest x1 9.94 us: injected(): own = lax.dynamic_slice_in_dim(orbitals[s], start, part, 0)]
    dynamic_update_slice x14 -> x0, local copies, waits for them, and re-layouts: 13.3 us -> none  [paired(): ring[s] = lax.dynamic_update_slice(ring[s], held, (slot * part, 0, 0))]
    another operation x0 -> x12, other arithmetic: none -> 13 us  [the longest x8 9.17 us: paired(): own = [jnp.stack(owns[lo:hi]) for lo, hi in GROUPS]]
    unnamed x40 -> x83, local copies, waits for them, and re-layouts: 0.1 us -> 6.71 us
    squeeze x0 -> x1, local copies, waits for them, and re-layouts: none -> 4.97 us  [paired(): chosen_orbital = lax.dynamic_index_in_dim(orbitals, pick, 0, keepdims=False)]
  transfers between devices with their start and end apart: 52 -> 44, of which waited for: 26 -> 26; matrix products, arithmetic and copies ran while one was open for 19% -> 13% of each run, Pallas kernels for 9% -> 18%
where the time goes in v2:
time: 275 us; the launch traced here: 273 us
  waiting for transfers between devices  93.8 us (34%)
  Pallas kernels  65.8 us (24%)
  starting transfers between devices  63.6 us (23%)
  other arithmetic  32 us (12%)
  local copies, waits for them, and re-layouts  16.2 us (6%)
    ppermute x44, waiting for transfers between devices, move(): return lax.ppermute(value, axes, pairs)  93.8 us
    ppermute x44, starting transfers between devices, move(): return lax.ppermute(value, axes, pairs)  63.6 us
    pallas_call x8, Pallas kernels, arrived(): pl.pallas_call(pick_body, in_specs=[pl.BlockSpec(memory_space=pltpu.SMEM)...  20.1 us
    pallas_call x3, Pallas kernels, paired(): call(forward_body, hi - lo, [slab, pairs, pairs] + [whole(square)] * 2 +...  18.2 us
    pallas_call x4, Pallas kernels, paired(): call(backward_body, hi - lo, [some_lines, some_lines, some_pairs, some_pa...  15.2 us
    pallas_call x1, Pallas kernels, paired(): call(middle_body, half // ROWS, cols * 2 + [chosen(square)] * 4, cols * 2...  12.3 us
    another operation x8, other arithmetic, paired(): own = [jnp.stack(owns[lo:hi]) for lo, hi in GROUPS]  9.17 us
    unnamed x83, local copies, waits for them, and re-layouts  6.71 us
  transfers between devices with their start and end apart: 44, of which 26 were waited for; matrix products, arithmetic and copies ran while one was open for 13% of the time, Pallas kernels for 18%

profile of v2, /device:TPU:1, one launch (start us, length us, event | category | flops | bytes accessed | tf_op | source)
XLA Modules:
  0.0 273.4 jit_solution(9364838724490837505)
XLA Ops:
  0.0 2.1 dynamic-slice_bitcast_fusion.1
  2.8 5.0 %dynamic-slice_bitcast_fusion = f32[64,128,128]{2,1,0:T(8,128)} fusion(f32[2,64,128,128]{3,2,1,0:T(8,128)} %param.15, s32[]{:T(128)S(6)} %select_n.221), kind=kLoop, calls=%fused_computation.1 | loop fusion | bytes 8388612 | tf_op jit(solution)/shard_map/jit(dynamic_index_in_dim)/squeeze | solution.py:357
  15.8 2.7 %collective-permute-start.1 = (f32[2,4,128,128]{3,2,1,0:T(8,128)S(1)}, f32[2,4,128,128]{3,2,1,0:T(8,128)}, u32[]{:S(2)}, u32[]{:S(2)}) collective-permute-start(f32[2,4,128,128]{3,2,1,0:T(8,128)S(1)} %select_bitcast_fusion.8.refs_0_), channel_id=1, source_target_pairs={{0,8},{1,9},{2,6},{3,7},{4,0},{5,1},{6,14},{7,15},{8,16},{9,17},{1... | collective-permute-start | bytes 1572872 | tf_op jit(solution)/shard_map/ppermute | solution.py:318
  19.1 3.3 %collective-permute-start.9 = (f32[64,128,128]{2,1,0:T(8,128)}, f32[64,128,128]{2,1,0:T(8,128)}, u32[]{:S(2)}, u32[]{:S(2)}) collective-permute-start(f32[64,128,128]{2,1,0:T(8,128)} %dynamic-slice_bitcast_fusion), channel_id=1, source_target_pairs={{1,2},{2,1},{5,6},{6,5},{9,10},{10,9},{13,14},{14,13},{17,18},{18,... | collective-permute-start | bytes 12582920 | tf_op jit(solution)/shard_map/ppermute | solution.py:318
  22.5 3.0 %collective-permute-done.1 = f32[2,4,128,128]{3,2,1,0:T(8,128)} collective-permute-done((f32[2,4,128,128]{3,2,1,0:T(8,128)S(1)}, f32[2,4,128,128]{3,2,1,0:T(8,128)}, u32[]{:S(2)}, u32[]{:S(2)}) %collective-permute-start.1) | collective-permute-done | bytes 524320 | tf_op jit(solution)/shard_map/ppermute | solution.py:318
  29.5 6.9 %collective-permute-done.4 = f32[2,4,128,128]{3,2,1,0:T(8,128)S(1)} collective-permute-done((f32[2,4,128,128]{3,2,1,0:T(8,128)S(1)}, f32[2,4,128,128]{3,2,1,0:T(8,128)S(1)}, u32[]{:S(2)}, u32[]{:S(2)}) %collective-permute-start.4) | collective-permute-done | bytes 524320 | tf_op jit(solution)/shard_map/ppermute | solution.py:318
  38.3 6.5 %collective-permute-done.5 = f32[2,4,128,128]{3,2,1,0:T(8,128)S(1)} collective-permute-done((f32[2,4,128,128]{3,2,1,0:T(8,128)S(1)}, f32[2,4,128,128]{3,2,1,0:T(8,128)S(1)}, u32[]{:S(2)}, u32[]{:S(2)}) %collective-permute-start.5) | collective-permute-done | bytes 524320 | tf_op jit(solution)/shard_map/ppermute | solution.py:318
  46.4 6.9 %collective-permute-done.6 = f32[2,4,128,128]{3,2,1,0:T(8,128)S(1)} collective-permute-done((f32[2,4,128,128]{3,2,1,0:T(8,128)S(1)}, f32[2,4,128,128]{3,2,1,0:T(8,128)S(1)}, u32[]{:S(2)}, u32[]{:S(2)}) %collective-permute-start.6) | collective-permute-done | bytes 524320 | tf_op jit(solution)/shard_map/ppermute | solution.py:318
  54.8 6.9 %collective-permute-done.7 = f32[2,4,128,128]{3,2,1,0:T(8,128)S(1)} collective-permute-done((f32[2,4,128,128]{3,2,1,0:T(8,128)S(1)}, f32[2,4,128,128]{3,2,1,0:T(8,128)S(1)}, u32[]{:S(2)}, u32[]{:S(2)}) %collective-permute-start.7) | collective-permute-done | bytes 524320 | tf_op jit(solution)/shard_map/ppermute | solution.py:318
  63.3 6.2 %collective-permute-done.9 = f32[64,128,128]{2,1,0:T(8,128)} collective-permute-done((f32[64,128,128]{2,1,0:T(8,128)}, f32[64,128,128]{2,1,0:T(8,128)}, u32[]{:S(2)}, u32[]{:S(2)}) %collective-permute-start.9) | collective-permute-done | bytes 4194336 | tf_op jit(solution)/shard_map/ppermute | solution.py:318
  72.8 5.3 %broadcast_select_fusion = f32[64,128,128]{2,1,0:T(8,128)} fusion(f32[64,128,128]{2,1,0:T(8,128)} %dynamic-slice_bitcast_fusion, f32[64,128,128]{2,1,0:T(8,128)} %collective-permute-done.9, pred[]{:T(512)S(6)} %eq.25), kind=kLoop, calls=%fused_computation.5 | loop fusion | flops 1048576 | bytes 12582913 | tf_op jit(solution)/shard_map/jit(_where)/select_n | solution.py:403
  82.0 2.5 shard_map.145
  84.5 2.0 collective-permute-start.13
  86.5 2.4 collective-permute-done.11.refs_7_.refs_6_.refs_5_.refs_4_.refs_3_.refs_2_.refs_1_
  90.0 2.5 shard_map.146
  94.5 2.7 collective-permute-done.12.refs_7_.refs_6_.refs_5_.refs_4_.refs_3_.refs_2_
  98.2 8.2 %collective-permute-start.16 = (f32[2,4,128,128]{3,2,1,0:T(8,128)}, f32[2,4,128,128]{3,2,1,0:T(8,128)}, u32[]{:S(2)}, u32[]{:S(2)}) collective-permute-start(f32[2,4,128,128]{3,2,1,0:T(8,128)} %get-tuple-element.122), channel_id=1, source_target_pairs={{0,2},{1,3},{2,0},{3,1},{4,6},{5,7},{6,4},{7,5},{8,10},{9,11},{10,... | collective-permute-start | bytes 1572872 | tf_op jit(solution)/shard_map/ppermute | solution.py:318
  107.9 2.5 shard_map.147
  112.5 2.5 collective-permute-done.14.refs_7_.refs_6_.refs_5_.refs_4_.refs_3_
  115.1 2.1 select_bitcast_fusion.6
  119.3 2.5 shard_map.148
  123.7 2.8 %collective-permute-done.17.refs_7_.refs_6_.refs_5_.refs_4_ = f32[2,4,128,128]{3,2,1,0:T(8,128)S(1)} collective-permute-done((f32[2,4,128,128]{3,2,1,0:T(8,128)S(1)}, f32[2,4,128,128]{3,2,1,0:T(8,128)S(1)}, u32[]{:S(2)}, u32[]{:S(2)}) %collective-permute-start.17) | collective-permute-done | bytes 524320 | tf_op jit(solution)/shard_map/ppermute | solution.py:318
  129.7 2.5 shard_map.149
  136.9 2.3 broadcast_select_fusion.9
  141.2 2.5 shard_map.151
  148.4 2.1 select_bitcast_fusion.3
  152.5 2.5 shard_map.152
  162.3 2.6 shard_map.154
  166.3 2.9 %collective-permute-done.29 = f32[2,4,128,128]{3,2,1,0:T(8,128)S(1)} collective-permute-done((f32[2,4,128,128]{3,2,1,0:T(8,128)}, f32[2,4,128,128]{3,2,1,0:T(8,128)S(1)}, u32[]{:S(2)}, u32[]{:S(2)}) %collective-permute-start.29) | collective-permute-done | bytes 524320 | tf_op jit(solution)/shard_map/ppermute | solution.py:318
  176.9 8.9 %shard_map.150 = (f32[2,64,32,128]{3,2,1,0:T(8,128)S(1)}, f32[2,64,32,128]{3,2,1,0:T(8,128)S(1)}) custom-call(s32[2]{0:T(128)S(1)} %copy-done.13, f32[2,32,128,128]{3,2,1,0:T(8,128)S(1)} %bitcast.78, f32[4,2,4,128,128]{4,3,2,1,0:T(8,128)S(1)} %pad_maximum_fusion.1.own, f32[4,2,4,128,128]{4,3,2,1,0:T(8,128)S(1)} %pad_maximum_fusion.2.other, ...), custom_call_target="tpu_custom_call" | custom-call | tf_op jit(solution)/shard_map/pallas_call | solution.py:442
  188.0 4.6 %shard_map.153 = (f32[2,64,16,128]{3,2,1,0:T(8,128)S(1)}, f32[2,64,16,128]{3,2,1,0:T(8,128)S(1)}) custom-call(s32[2]{0:T(128)S(1)} %copy-done.13, f32[2,32,128,128]{3,2,1,0:T(8,128)S(1)} %bitcast.79, f32[2,2,4,128,128]{4,3,2,1,0:T(8,128)S(1)} %pad_maximum_fusion.3.own, f32[2,2,4,128,128]{4,3,2,1,0:T(8,128)S(1)} %pad_maximum_fusion.4.other, ...), custom_call_target="tpu_custom_call" | custom-call | tf_op jit(solution)/shard_map/pallas_call | solution.py:442
  193.0 4.6 %shard_map.155 = (f32[2,64,16,128]{3,2,1,0:T(8,128)S(1)}, f32[2,64,16,128]{3,2,1,0:T(8,128)S(1)}) custom-call(s32[2]{0:T(128)S(1)} %copy-done.13, f32[2,32,128,128]{3,2,1,0:T(8,128)S(1)} %bitcast.80, f32[2,2,4,128,128]{4,3,2,1,0:T(8,128)S(1)} %pad_maximum_fusion.5.own, f32[2,2,4,128,128]{4,3,2,1,0:T(8,128)S(1)} %pad_maximum_fusion.6.other, ...), custom_call_target="tpu_custom_call" | custom-call | tf_op jit(solution)/shard_map/pallas_call | solution.py:442
  198.2 2.3 collective-permute-done.36.refs_5_
  200.5 12.3 %shard_map.156 = (f32[2,64,32,128]{3,2,1,0:T(8,128)S(1)}, f32[2,64,16,128]{3,2,1,0:T(8,128)S(1)}, f32[2,64,16,128]{3,2,1,0:T(8,128)S(1)}, f32[2,64,32,128]{3,2,1...) custom-call(s32[2]{0:T(128)S(1)} %copy-done.13, ...), custom_call_target="tpu_custom_call" | custom-call | tf_op jit(solution)/shard_map/pallas_call | solution.py:457
  213.3 3.8 %collective-permute-done.37.recv = f32[2,64,32,128]{3,2,1,0:T(8,128)S(1)} collective-permute-done((f32[2,64,32,128]{3,2,1,0:T(8,128)S(1)}, f32[2,64,32,128]{3,2,1,0:T(8,128)S(1)}, u32[]{:S(2)}, u32[]{:S(2)}) %collective-permute-start.37) | collective-permute-done | bytes 2097184 | tf_op jit(solution)/shard_map/ppermute | solution.py:318
  217.1 3.9 %shard_map.157 = f32[2,8,128,128]{3,2,1,0:T(8,128)S(1)} custom-call(s32[2]{0:T(128)S(1)} %copy-done.13, f32[2,64,32,128]{3,2,1,0:T(8,128)S(1)} %get-tuple-element.95.keep, f32[2,64,32,128]{3,2,1,0:T(8,128)S(1)} %collective-permute-done.37.recv, f32[4,2,4,128,128]{4,3,2,1,0:T(8,128)S(1)} %pad_maximum_fusion.1.own, ...), custom_call_target="tpu_custom_call" | custom-call | tf_op jit(solution)/shard_map/pallas_call | solution.py:481
  220.9 3.4 %collective-permute-start.38 = (f32[2,8,128,128]{3,2,1,0:T(8,128)S(1)}, f32[2,8,128,128]{3,2,1,0:T(8,128)S(1)}, u32[]{:S(2)}, u32[]{:S(2)}) collective-permute-start(f32[2,8,128,128]{3,2,1,0:T(8,128)S(1)} %shard_map.157), channel_id=1, source_target_pairs={{1,2},{2,1},{5,6},{6,5},{9,10},{10,9},{13,14},{14,13},{17,18},{18,... | collective-permute-start | bytes 3145736 | tf_op jit(solution)/shard_map/ppermute | solution.py:318
  224.4 3.9 %shard_map.158 = f32[2,8,128,128]{3,2,1,0:T(8,128)S(1)} custom-call(s32[2]{0:T(128)S(1)} %copy-done.13, f32[2,64,32,128]{3,2,1,0:T(8,128)S(1)} %get-tuple-element.95.keep, f32[2,64,32,128]{3,2,1,0:T(8,128)S(1)} %collective-permute-done.37.recv, f32[4,2,4,128,128]{4,3,2,1,0:T(8,128)S(1)} %pad_maximum_fusion.1.own, ...), custom_call_target="tpu_custom_call" | custom-call | tf_op jit(solution)/shard_map/pallas_call | solution.py:481
  228.3 2.4 collective-permute-start.39
  230.8 6.3 %collective-permute-done.38 = f32[2,8,128,128]{3,2,1,0:T(8,128)S(1)} collective-permute-done((f32[2,8,128,128]{3,2,1,0:T(8,128)S(1)}, f32[2,8,128,128]{3,2,1,0:T(8,128)S(1)}, u32[]{:S(2)}, u32[]{:S(2)}) %collective-permute-start.38) | collective-permute-done | bytes 1048608 | tf_op jit(solution)/shard_map/ppermute | solution.py:318
  237.1 3.7 %shard_map.159 = f32[2,8,128,128]{3,2,1,0:T(8,128)S(1)} custom-call(s32[2]{0:T(128)S(1)} %copy-done.13, f32[2,64,16,128]{3,2,1,0:T(8,128)S(1)} %get-tuple-element.101.keep, f32[2,64,16,128]{3,2,1,0:T(8,128)S(1)} %collective-permute-done.40.recv, f32[2,2,4,128,128]{4,3,2,1,0:T(8,128)S(1)} %pad_maximum_fusion.3.own, ...), custom_call_target="tpu_custom_call" | custom-call | tf_op jit(solution)/shard_map/pallas_call | solution.py:481
  240.8 3.4 %collective-permute-start.41 = (f32[2,8,128,128]{3,2,1,0:T(8,128)S(1)}, f32[2,8,128,128]{3,2,1,0:T(8,128)S(1)}, u32[]{:S(2)}, u32[]{:S(2)}) collective-permute-start(f32[2,8,128,128]{3,2,1,0:T(8,128)S(1)} %shard_map.159), channel_id=1, source_target_pairs={{1,2},{2,1},{5,6},{6,5},{9,10},{10,9},{13,14},{14,13},{17,18},{18,... | collective-permute-start | bytes 3145736 | tf_op jit(solution)/shard_map/ppermute | solution.py:318
  244.2 4.1 %collective-permute-done.39 = f32[2,8,128,128]{3,2,1,0:T(8,128)S(1)} collective-permute-done((f32[2,8,128,128]{3,2,1,0:T(8,128)S(1)}, f32[2,8,128,128]{3,2,1,0:T(8,128)S(1)}, u32[]{:S(2)}, u32[]{:S(2)}) %collective-permute-start.39) | collective-permute-done | bytes 1048608 | tf_op jit(solution)/shard_map/ppermute | solution.py:318
  248.3 3.7 %shard_map.160 = f32[2,8,128,128]{3,2,1,0:T(8,128)S(1)} custom-call(s32[2]{0:T(128)S(1)} %copy-done.13, f32[2,64,16,128]{3,2,1,0:T(8,128)S(1)} %get-tuple-element.103.keep, f32[2,64,16,128]{3,2,1,0:T(8,128)S(1)} %collective-permute-done.42.recv, f32[2,2,4,128,128]{4,3,2,1,0:T(8,128)S(1)} %pad_maximum_fusion.5.own, ...), custom_call_target="tpu_custom_call" | custom-call | tf_op jit(solution)/shard_map/pallas_call | solution.py:481
  252.0 3.4 %collective-permute-start.43 = (f32[2,8,128,128]{3,2,1,0:T(8,128)S(1)}, f32[2,8,128,128]{3,2,1,0:T(8,128)S(1)}, u32[]{:S(2)}, u32[]{:S(2)}) collective-permute-start(f32[2,8,128,128]{3,2,1,0:T(8,128)S(1)} %shard_map.160), channel_id=1, source_target_pairs={{1,2},{2,1},{5,6},{6,5},{9,10},{10,9},{13,14},{14,13},{17,18},{18,... | collective-permute-start | bytes 3145736 | tf_op jit(solution)/shard_map/ppermute | solution.py:318
  255.7 3.9 %collective-permute-done.41 = f32[2,8,128,128]{3,2,1,0:T(8,128)S(1)} collective-permute-done((f32[2,8,128,128]{3,2,1,0:T(8,128)S(1)}, f32[2,8,128,128]{3,2,1,0:T(8,128)S(1)}, u32[]{:S(2)}, u32[]{:S(2)}) %collective-permute-start.41) | collective-permute-done | bytes 1048608 | tf_op jit(solution)/shard_map/ppermute | solution.py:318
  259.6 11.1 %collective-permute-done.43 = f32[2,8,128,128]{3,2,1,0:T(8,128)S(1)} collective-permute-done((f32[2,8,128,128]{3,2,1,0:T(8,128)S(1)}, f32[2,8,128,128]{3,2,1,0:T(8,128)S(1)}, u32[]{:S(2)}, u32[]{:S(2)}) %collective-permute-start.43) | collective-permute-done | bytes 1048608 | tf_op jit(solution)/shard_map/ppermute | solution.py:318
  270.9 2.5 pad_maximum_fusion
  (175 shorter events, 74.1 us)
Async XLA Ops:
  2.1 5.7 %collective-permute-start = (f32[2,1,4,128,128]{4,3,2,0,1:T(8,128)S(1)}, f32[2,1,4,128,128]{4,3,2,0,1:T(8,128)}, u32[]{:S(2)}, u32[]{:S(2)}) collective-permute-start(f32[2,1,4,128,128]{4,3,2,0,1:T(8,128)S(1)} %get-tuple-element.56), channel_id=1, source_target_pairs={{0,2},{1,3},{2,0},{3,1},{4,6},{5,7},{6,4},{7,5},{8,10},{9,11},{10,... | collective-permute-start | bytes 1572872 | tf_op jit(solution)/shard_map/ppermute | solution.py:318
  11.2 26.7 %collective-permute-start.2 = (f32[2,5,4,128,128]{4,3,2,0,1:T(8,128)}, f32[2,5,4,128,128]{4,3,2,0,1:T(8,128)}, u32[]{:S(2)}, u32[]{:S(2)}) collective-permute-start(f32[2,5,4,128,128]{4,3,2,0,1:T(8,128)} %copy.18), channel_id=1, source_target_pairs={{0,2},{1,3},{2,0},{3,1},{4,6},{5,7},{6,4},{7,5},{8,10},{9,11},{10,... | collective-permute-start | bytes 7864328 | tf_op jit(solution)/shard_map/ppermute | solution.py:318
  13.9 11.6 %collective-permute-start.3 = (f32[2,2,4,128,128]{4,3,2,0,1:T(8,128)}, f32[2,2,4,128,128]{4,3,2,0,1:T(8,128)}, u32[]{:S(2)}, u32[]{:S(2)}) collective-permute-start(f32[2,2,4,128,128]{4,3,2,0,1:T(8,128)} %copy.20), channel_id=1, source_target_pairs={{0,2},{1,3},{2,0},{3,1},{4,6},{5,7},{6,4},{7,5},{8,10},{9,11},{10,... | collective-permute-start | bytes 3145736 | tf_op jit(solution)/shard_map/ppermute | solution.py:318
  15.8 20.7 %copy-start.37 = (f32[2,4,128,128]{3,2,1,0:T(8,128)}, f32[2,4,128,128]{3,2,1,0:T(8,128)S(1)}, u32[]{:S(2)}) copy-start(f32[2,4,128,128]{3,2,1,0:T(8,128)S(1)} %select_bitcast_fusion.8.refs_0_) | copy-start | bytes 1572868
  15.8 9.8 %collective-permute-start.1 = (f32[2,4,128,128]{3,2,1,0:T(8,128)S(1)}, f32[2,4,128,128]{3,2,1,0:T(8,128)}, u32[]{:S(2)}, u32[]{:S(2)}) collective-permute-start(f32[2,4,128,128]{3,2,1,0:T(8,128)S(1)} %select_bitcast_fusion.8.refs_0_), channel_id=1, source_target_pairs={{0,8},{1,9},{2,6},{3,7},{4,0},{5,1},{6,14},{7,15},{8,16},{9,17},{1... | collective-permute-start | bytes 1572872 | tf_op jit(solution)/shard_map/ppermute | solution.py:318
  19.1 50.3 %collective-permute-start.9 = (f32[64,128,128]{2,1,0:T(8,128)}, f32[64,128,128]{2,1,0:T(8,128)}, u32[]{:S(2)}, u32[]{:S(2)}) collective-permute-start(f32[64,128,128]{2,1,0:T(8,128)} %dynamic-slice_bitcast_fusion), channel_id=1, source_target_pairs={{1,2},{2,1},{5,6},{6,5},{9,10},{10,9},{13,14},{14,13},{17,18},{18,... | collective-permute-start | bytes 12582920 | tf_op jit(solution)/shard_map/ppermute | solution.py:318
  28.0 8.4 %collective-permute-start.4 = (f32[2,4,128,128]{3,2,1,0:T(8,128)S(1)}, f32[2,4,128,128]{3,2,1,0:T(8,128)S(1)}, u32[]{:S(2)}, u32[]{:S(2)}) collective-permute-start(f32[2,4,128,128]{3,2,1,0:T(8,128)S(1)} %fusion.1.refs_1_.refs_0_), channel_id=1, source_target_pairs={{0,8},{1,9},{2,6},{3,7},{4,0},{5,1},{6,14},{7,15},{8,16},{9,17},{1... | collective-permute-start | bytes 1572872 | tf_op jit(solution)/shard_map/ppermute | solution.py:318
  36.5 8.4 %collective-permute-start.5 = (f32[2,4,128,128]{3,2,1,0:T(8,128)S(1)}, f32[2,4,128,128]{3,2,1,0:T(8,128)S(1)}, u32[]{:S(2)}, u32[]{:S(2)}) collective-permute-start(f32[2,4,128,128]{3,2,1,0:T(8,128)S(1)} %fusion.2.refs_2_.refs_1_.refs_0_), channel_id=1, source_target_pairs={{0,8},{1,9},{2,6},{3,7},{4,0},{5,1},{6,14},{7,15},{8,16},{9,17},{1... | collective-permute-start | bytes 1572872 | tf_op jit(solution)/shard_map/ppermute | solution.py:318
  38.3 23.4 %copy-start.23 = (f32[2,5,4,128,128]{4,3,2,0,1:T(8,128)}, f32[2,5,4,128,128]{4,3,2,0,1:T(8,128)S(1)}, u32[]{:S(2)}) copy-start(f32[2,5,4,128,128]{4,3,2,0,1:T(8,128)S(1)} %copy_select_fusion) | copy-start | bytes 7864324
  44.9 33.1 %copy-start.22 = (f32[2,4,128,128]{3,2,1,0:T(8,128)}, f32[2,4,128,128]{3,2,1,0:T(8,128)S(1)}, u32[]{:S(2)}) copy-start(f32[2,4,128,128]{3,2,1,0:T(8,128)S(1)} %fusion.3.refs_3_.refs_2_.refs_1_.refs_0_) | copy-start | bytes 1572868
  44.9 8.4 %collective-permute-start.6 = (f32[2,4,128,128]{3,2,1,0:T(8,128)S(1)}, f32[2,4,128,128]{3,2,1,0:T(8,128)S(1)}, u32[]{:S(2)}, u32[]{:S(2)}) collective-permute-start(f32[2,4,128,128]{3,2,1,0:T(8,128)S(1)} %fusion.3.refs_3_.refs_2_.refs_1_.refs_0_), channel_id=1, source_target_pairs={{0,8},{1,9},{2,6},{3,7},{4,0},{5,1},{6,14},{7,15},{8,16},{9,17},{1... | collective-permute-start | bytes 1572872 | tf_op jit(solution)/shard_map/ppermute | solution.py:318
  53.4 24.7 %copy-start.19 = (f32[2,4,128,128]{3,2,1,0:T(8,128)}, f32[2,4,128,128]{3,2,1,0:T(8,128)S(1)}, u32[]{:S(2)}) copy-start(f32[2,4,128,128]{3,2,1,0:T(8,128)S(1)} %fusion.4.refs_4_.refs_3_.refs_2_.refs_1_.refs_0_) | copy-start | bytes 1572868
  53.4 8.4 %collective-permute-start.7 = (f32[2,4,128,128]{3,2,1,0:T(8,128)S(1)}, f32[2,4,128,128]{3,2,1,0:T(8,128)S(1)}, u32[]{:S(2)}, u32[]{:S(2)}) collective-permute-start(f32[2,4,128,128]{3,2,1,0:T(8,128)S(1)} %fusion.4.refs_4_.refs_3_.refs_2_.refs_1_.refs_0_), channel_id=1, source_target_pairs={{0,8},{1,9},{2,6},{3,7},{4,0},{5,1},{6,14},{7,15},{8,16},{9,17},{1... | collective-permute-start | bytes 1572872 | tf_op jit(solution)/shard_map/ppermute | solution.py:318
  61.8 8.4 %collective-permute-start.8 = (f32[2,4,128,128]{3,2,1,0:T(8,128)S(1)}, f32[2,4,128,128]{3,2,1,0:T(8,128)S(1)}, u32[]{:S(2)}, u32[]{:S(2)}) collective-permute-start(f32[2,4,128,128]{3,2,1,0:T(8,128)S(1)} %fusion.5.refs_5_.refs_4_.refs_3_.refs_2_.refs_1_.refs_0_), channel_id=1, source_target_pairs={{0,8},{1,9},{2,6},{3,7},{4,0},{5,1},{6,14},{7,15},{8,16},{9,17},{1... | collective-permute-start | bytes 1572872 | tf_op jit(solution)/shard_map/ppermute | solution.py:318
  71.3 8.4 %collective-permute-start.10 = (f32[2,4,128,128]{3,2,1,0:T(8,128)S(1)}, f32[2,4,128,128]{3,2,1,0:T(8,128)S(1)}, u32[]{:S(2)}, u32[]{:S(2)}) collective-permute-start(f32[2,4,128,128]{3,2,1,0:T(8,128)S(1)} %fusion.6.refs_6_.refs_5_.refs_4_.refs_3_.refs_2_.refs_1_.refs_0_), channel_id=1, source_target_pairs={{0,8},{1,9},{2,6},{3,7},{4,0},{5,1},{6,14},{7,15},{8,16},{9,17},{1... | collective-permute-start | bytes 1572872 | tf_op jit(solution)/shard_map/ppermute | solution.py:318
  80.8 8.1 %collective-permute-start.11 = (f32[2,4,128,128]{3,2,1,0:T(8,128)S(1)}, f32[2,4,128,128]{3,2,1,0:T(8,128)S(1)}, u32[]{:S(2)}, u32[]{:S(2)}) collective-permute-start(f32[2,4,128,128]{3,2,1,0:T(8,128)S(1)} %fusion.refs_7_.refs_6_.refs_5_.refs_4_.refs_3_.refs_2_.refs_1_.refs_0_), channel_id=1, source_target_pairs={{0,8},{1,9},{2,6},{3,7},{4,0},{5,1},{6,14},{7,15},{8,16},{9,17},{1... | collective-permute-start | bytes 1572872 | tf_op jit(solution)/shard_map/ppermute | solution.py:318
  84.5 10.0 %collective-permute-start.13 = (f32[2,4,128,128]{3,2,1,0:T(8,128)}, f32[2,4,128,128]{3,2,1,0:T(8,128)S(1)}, u32[]{:S(2)}, u32[]{:S(2)}) collective-permute-start(f32[2,4,128,128]{3,2,1,0:T(8,128)} %shard_map.145), channel_id=1, source_target_pairs={{0,1},{1,0},{2,3},{3,2},{4,5},{5,4},{6,7},{7,6},{8,9},{9,8},{10,11... | collective-permute-start | bytes 1572872 | tf_op jit(solution)/shard_map/ppermute | solution.py:318
  88.9 8.3 %collective-permute-start.12 = (f32[2,4,128,128]{3,2,1,0:T(8,128)S(1)}, f32[2,4,128,128]{3,2,1,0:T(8,128)S(1)}, u32[]{:S(2)}, u32[]{:S(2)}) collective-permute-start(f32[2,4,128,128]{3,2,1,0:T(8,128)S(1)} %collective-permute-done.11.refs_7_.refs_6_.refs_5_.refs_4_.refs_3_.refs_2_.refs_1_), channel_id=1, source_target_pairs={{0,8},{1,9},{2,6},{3,7},{4,0},{5,1},{6,14},{7,15},{8,16},{9,17},{1... | collective-permute-start | bytes 1572872 | tf_op jit(solution)/shard_map/ppermute | solution.py:318
  92.5 19.2 %collective-permute-start.15 = (f32[2,4,128,128]{3,2,1,0:T(8,128)}, f32[2,4,128,128]{3,2,1,0:T(8,128)S(1)}, u32[]{:S(2)}, u32[]{:S(2)}) collective-permute-start(f32[2,4,128,128]{3,2,1,0:T(8,128)} %shard_map.146), channel_id=1, source_target_pairs={{0,1},{1,0},{2,3},{3,2},{4,5},{5,4},{6,7},{7,6},{8,9},{9,8},{10,11... | collective-permute-start | bytes 1572872 | tf_op jit(solution)/shard_map/ppermute | solution.py:318
  98.2 13.5 %collective-permute-start.16 = (f32[2,4,128,128]{3,2,1,0:T(8,128)}, f32[2,4,128,128]{3,2,1,0:T(8,128)}, u32[]{:S(2)}, u32[]{:S(2)}) collective-permute-start(f32[2,4,128,128]{3,2,1,0:T(8,128)} %get-tuple-element.122), channel_id=1, source_target_pairs={{0,2},{1,3},{2,0},{3,1},{4,6},{5,7},{6,4},{7,5},{8,10},{9,11},{10,... | collective-permute-start | bytes 1572872 | tf_op jit(solution)/shard_map/ppermute | solution.py:318
  106.4 8.7 %collective-permute-start.14 = (f32[2,4,128,128]{3,2,1,0:T(8,128)S(1)}, f32[2,4,128,128]{3,2,1,0:T(8,128)S(1)}, u32[]{:S(2)}, u32[]{:S(2)}) collective-permute-start(f32[2,4,128,128]{3,2,1,0:T(8,128)S(1)} %collective-permute-done.12.refs_7_.refs_6_.refs_5_.refs_4_.refs_3_.refs_2_), channel_id=1, source_target_pairs={{0,8},{1,9},{2,6},{3,7},{4,0},{5,1},{6,14},{7,15},{8,16},{9,17},{1... | collective-permute-start | bytes 1572872 | tf_op jit(solution)/shard_map/ppermute | solution.py:318
  110.5 13.2 %collective-permute-start.18 = (f32[2,4,128,128]{3,2,1,0:T(8,128)}, f32[2,4,128,128]{3,2,1,0:T(8,128)S(1)}, u32[]{:S(2)}, u32[]{:S(2)}) collective-permute-start(f32[2,4,128,128]{3,2,1,0:T(8,128)} %shard_map.147), channel_id=1, source_target_pairs={{0,1},{1,0},{2,3},{3,2},{4,5},{5,4},{6,7},{7,6},{8,9},{9,8},{10,11... | collective-permute-start | bytes 1572872 | tf_op jit(solution)/shard_map/ppermute | solution.py:318
  117.2 6.5 %collective-permute-start.19 = (f32[2,4,128,128]{3,2,1,0:T(8,128)}, f32[2,4,128,128]{3,2,1,0:T(8,128)}, u32[]{:S(2)}, u32[]{:S(2)}) collective-permute-start(f32[2,4,128,128]{3,2,1,0:T(8,128)} %get-tuple-element.124), channel_id=1, source_target_pairs={{0,2},{1,3},{2,0},{3,1},{4,6},{5,7},{6,4},{7,5},{8,10},{9,11},{10,... | collective-permute-start | bytes 1572872 | tf_op jit(solution)/shard_map/ppermute | solution.py:318
  117.7 8.8 %collective-permute-start.17 = (f32[2,4,128,128]{3,2,1,0:T(8,128)S(1)}, f32[2,4,128,128]{3,2,1,0:T(8,128)S(1)}, u32[]{:S(2)}, u32[]{:S(2)}) collective-permute-start(f32[2,4,128,128]{3,2,1,0:T(8,128)S(1)} %collective-permute-done.14.refs_7_.refs_6_.refs_5_.refs_4_.refs_3_), channel_id=1, source_target_pairs={{0,8},{1,9},{2,6},{3,7},{4,0},{5,1},{6,14},{7,15},{8,16},{9,17},{1... | collective-permute-start | bytes 1572872 | tf_op jit(solution)/shard_map/ppermute | solution.py:318
  121.8 13.3 %collective-permute-start.21 = (f32[2,4,128,128]{3,2,1,0:T(8,128)}, f32[2,4,128,128]{3,2,1,0:T(8,128)}, u32[]{:S(2)}, u32[]{:S(2)}) collective-permute-start(f32[2,4,128,128]{3,2,1,0:T(8,128)} %shard_map.148), channel_id=1, source_target_pairs={{0,1},{1,0},{2,3},{3,2},{4,5},{5,4},{6,7},{7,6},{8,9},{9,8},{10,11... | collective-permute-start | bytes 1572872 | tf_op jit(solution)/shard_map/ppermute | solution.py:318
  127.7 7.4 %collective-permute-start.22 = (f32[2,4,128,128]{3,2,1,0:T(8,128)}, f32[2,4,128,128]{3,2,1,0:T(8,128)}, u32[]{:S(2)}, u32[]{:S(2)}) collective-permute-start(f32[2,4,128,128]{3,2,1,0:T(8,128)} %get-tuple-element.126), channel_id=1, source_target_pairs={{0,2},{1,3},{2,0},{3,1},{4,6},{5,7},{6,4},{7,5},{8,10},{9,11},{10,... | collective-permute-start | bytes 1572872 | tf_op jit(solution)/shard_map/ppermute | solution.py:318
  128.1 8.8 %collective-permute-start.20 = (f32[2,4,128,128]{3,2,1,0:T(8,128)S(1)}, f32[2,4,128,128]{3,2,1,0:T(8,128)S(1)}, u32[]{:S(2)}, u32[]{:S(2)}) collective-permute-start(f32[2,4,128,128]{3,2,1,0:T(8,128)S(1)} %collective-permute-done.17.refs_7_.refs_6_.refs_5_.refs_4_), channel_id=1, source_target_pairs={{0,8},{1,9},{2,6},{3,7},{4,0},{5,1},{6,14},{7,15},{8,16},{9,17},{1... | collective-permute-start | bytes 1572872 | tf_op jit(solution)/shard_map/ppermute | solution.py:318
  132.2 14.3 %collective-permute-start.24 = (f32[2,4,128,128]{3,2,1,0:T(8,128)}, f32[2,4,128,128]{3,2,1,0:T(8,128)S(1)}, u32[]{:S(2)}, u32[]{:S(2)}) collective-permute-start(f32[2,4,128,128]{3,2,1,0:T(8,128)} %shard_map.149), channel_id=1, source_target_pairs={{0,1},{1,0},{2,3},{3,2},{4,5},{5,4},{6,7},{7,6},{8,9},{9,8},{10,11... | collective-permute-start | bytes 1572872 | tf_op jit(solution)/shard_map/ppermute | solution.py:318
  139.2 7.2 %collective-permute-start.25 = (f32[2,4,128,128]{3,2,1,0:T(8,128)}, f32[2,4,128,128]{3,2,1,0:T(8,128)}, u32[]{:S(2)}, u32[]{:S(2)}) collective-permute-start(f32[2,4,128,128]{3,2,1,0:T(8,128)} %get-tuple-element.119), channel_id=1, source_target_pairs={{0,2},{1,3},{2,0},{3,1},{4,6},{5,7},{6,4},{7,5},{8,10},{9,11},{10,... | collective-permute-start | bytes 1572872 | tf_op jit(solution)/shard_map/ppermute | solution.py:318
  139.7 8.7 %collective-permute-start.23 = (f32[2,4,128,128]{3,2,1,0:T(8,128)S(1)}, f32[2,4,128,128]{3,2,1,0:T(8,128)S(1)}, u32[]{:S(2)}, u32[]{:S(2)}) collective-permute-start(f32[2,4,128,128]{3,2,1,0:T(8,128)S(1)} %collective-permute-done.20.refs_7_.refs_6_.refs_5_), channel_id=1, source_target_pairs={{0,8},{1,9},{2,6},{3,7},{4,0},{5,1},{6,14},{7,15},{8,16},{9,17},{1... | collective-permute-start | bytes 1572872 | tf_op jit(solution)/shard_map/ppermute | solution.py:318
  143.7 14.4 %collective-permute-start.27 = (f32[2,4,128,128]{3,2,1,0:T(8,128)}, f32[2,4,128,128]{3,2,1,0:T(8,128)}, u32[]{:S(2)}, u32[]{:S(2)}) collective-permute-start(f32[2,4,128,128]{3,2,1,0:T(8,128)} %shard_map.151), channel_id=1, source_target_pairs={{0,1},{1,0},{2,3},{3,2},{4,5},{5,4},{6,7},{7,6},{8,9},{9,8},{10,11... | collective-permute-start | bytes 1572872 | tf_op jit(solution)/shard_map/ppermute | solution.py:318
  150.5 7.6 %collective-permute-start.28 = (f32[2,4,128,128]{3,2,1,0:T(8,128)}, f32[2,4,128,128]{3,2,1,0:T(8,128)}, u32[]{:S(2)}, u32[]{:S(2)}) collective-permute-start(f32[2,4,128,128]{3,2,1,0:T(8,128)} %get-tuple-element.118), channel_id=1, source_target_pairs={{0,2},{1,3},{2,0},{3,1},{4,6},{5,7},{6,4},{7,5},{8,10},{9,11},{10,... | collective-permute-start | bytes 1572872 | tf_op jit(solution)/shard_map/ppermute | solution.py:318
  151.1 8.7 %collective-permute-start.26 = (f32[2,4,128,128]{3,2,1,0:T(8,128)S(1)}, f32[2,4,128,128]{3,2,1,0:T(8,128)}, u32[]{:S(2)}, u32[]{:S(2)}) collective-permute-start(f32[2,4,128,128]{3,2,1,0:T(8,128)S(1)} %collective-permute-done.23.refs_7_.refs_6_), channel_id=1, source_target_pairs={{0,8},{1,9},{2,6},{3,7},{4,0},{5,1},{6,14},{7,15},{8,16},{9,17},{1... | collective-permute-start | bytes 1572872 | tf_op jit(solution)/shard_map/ppermute | solution.py:318
  155.0 14.2 %collective-permute-start.29 = (f32[2,4,128,128]{3,2,1,0:T(8,128)}, f32[2,4,128,128]{3,2,1,0:T(8,128)S(1)}, u32[]{:S(2)}, u32[]{:S(2)}) collective-permute-start(f32[2,4,128,128]{3,2,1,0:T(8,128)} %shard_map.152), channel_id=1, source_target_pairs={{0,1},{1,0},{2,3},{3,2},{4,5},{5,4},{6,7},{7,6},{8,9},{9,8},{10,11... | collective-permute-start | bytes 1572872 | tf_op jit(solution)/shard_map/ppermute | solution.py:318
  161.6 8.4 %collective-permute-start.30 = (f32[2,4,128,128]{3,2,1,0:T(8,128)}, f32[2,4,128,128]{3,2,1,0:T(8,128)}, u32[]{:S(2)}, u32[]{:S(2)}) collective-permute-start(f32[2,4,128,128]{3,2,1,0:T(8,128)} %get-tuple-element.115), channel_id=1, source_target_pairs={{0,2},{1,3},{2,0},{3,1},{4,6},{5,7},{6,4},{7,5},{8,10},{9,11},{10,... | collective-permute-start | bytes 1572872 | tf_op jit(solution)/shard_map/ppermute | solution.py:318
  164.8 21.1 %collective-permute-start.31 = (f32[2,4,128,128]{3,2,1,0:T(8,128)}, f32[2,4,128,128]{3,2,1,0:T(8,128)S(1)}, u32[]{:S(2)}, u32[]{:S(2)}) collective-permute-start(f32[2,4,128,128]{3,2,1,0:T(8,128)} %shard_map.154), channel_id=1, source_target_pairs={{0,1},{1,0},{2,3},{3,2},{4,5},{5,4},{6,7},{7,6},{8,9},{9,8},{10,11... | collective-permute-start | bytes 1572872 | tf_op jit(solution)/shard_map/ppermute | solution.py:318
  171.1 14.8 %collective-permute-start.32 = (f32[2,4,128,128]{3,2,1,0:T(8,128)S(1)}, f32[2,4,128,128]{3,2,1,0:T(8,128)S(1)}, u32[]{:S(2)}, u32[]{:S(2)}) collective-permute-start(f32[2,4,128,128]{3,2,1,0:T(8,128)S(1)} %get-tuple-element.114), channel_id=1, source_target_pairs={{0,2},{1,3},{2,0},{3,1},{4,6},{5,7},{6,4},{7,5},{8,10},{9,11},{10,... | collective-permute-start | bytes 1572872 | tf_op jit(solution)/shard_map/ppermute | solution.py:318
  185.8 12.3 %collective-permute-start.34 = (f32[2,64,32,128]{3,2,1,0:T(8,128)S(1)}, f32[2,64,32,128]{3,2,1,0:T(8,128)S(1)}, u32[]{:S(2)}, u32[]{:S(2)}) collective-permute-start(f32[2,64,32,128]{3,2,1,0:T(8,128)S(1)} %get-tuple-element.92), channel_id=1, source_target_pairs={{0,2},{1,3},{2,0},{3,1},{4,6},{5,7},{6,4},{7,5},{8,10},{9,11},{10,... | collective-permute-start | bytes 6291464 | tf_op jit(solution)/shard_map/ppermute | solution.py:318
  186.1 6.8 %collective-permute-start.33 = (f32[2,4,128,128]{3,2,1,0:T(8,128)S(1)}, f32[2,4,128,128]{3,2,1,0:T(8,128)S(1)}, u32[]{:S(2)}, u32[]{:S(2)}) collective-permute-start(f32[2,4,128,128]{3,2,1,0:T(8,128)S(1)} %get-tuple-element.111), channel_id=1, source_target_pairs={{0,2},{1,3},{2,0},{3,1},{4,6},{5,7},{6,4},{7,5},{8,10},{9,11},{10,... | collective-permute-start | bytes 1572872 | tf_op jit(solution)/shard_map/ppermute | solution.py:318
  192.6 5.5 %collective-permute-start.35 = (f32[2,64,16,128]{3,2,1,0:T(8,128)S(1)}, f32[2,64,16,128]{3,2,1,0:T(8,128)S(1)}, u32[]{:S(2)}, u32[]{:S(2)}) collective-permute-start(f32[2,64,16,128]{3,2,1,0:T(8,128)S(1)} %get-tuple-element.93), channel_id=1, source_target_pairs={{0,2},{1,3},{2,0},{3,1},{4,6},{5,7},{6,4},{7,5},{8,10},{9,11},{10,... | collective-permute-start | bytes 3145736 | tf_op jit(solution)/shard_map/ppermute | solution.py:318
  197.6 2.8 %collective-permute-start.36 = (f32[2,64,16,128]{3,2,1,0:T(8,128)S(1)}, f32[2,64,16,128]{3,2,1,0:T(8,128)S(1)}, u32[]{:S(2)}, u32[]{:S(2)}) collective-permute-start(f32[2,64,16,128]{3,2,1,0:T(8,128)S(1)} %get-tuple-element.94), channel_id=1, source_target_pairs={{0,2},{1,3},{2,0},{3,1},{4,6},{5,7},{6,4},{7,5},{8,10},{9,11},{10,... | collective-permute-start | bytes 3145736 | tf_op jit(solution)/shard_map/ppermute | solution.py:318
  212.8 4.2 %collective-permute-start.37 = (f32[2,64,32,128]{3,2,1,0:T(8,128)S(1)}, f32[2,64,32,128]{3,2,1,0:T(8,128)S(1)}, u32[]{:S(2)}, u32[]{:S(2)}) collective-permute-start(f32[2,64,32,128]{3,2,1,0:T(8,128)S(1)} %get-tuple-element.96), channel_id=1, source_target_pairs={{0,2},{1,3},{2,0},{3,1},{4,6},{5,7},{6,4},{7,5},{8,10},{9,11},{10,... | collective-permute-start | bytes 6291464 | tf_op jit(solution)/shard_map/ppermute | solution.py:318
  220.9 16.1 %collective-permute-start.38 = (f32[2,8,128,128]{3,2,1,0:T(8,128)S(1)}, f32[2,8,128,128]{3,2,1,0:T(8,128)S(1)}, u32[]{:S(2)}, u32[]{:S(2)}) collective-permute-start(f32[2,8,128,128]{3,2,1,0:T(8,128)S(1)} %shard_map.157), channel_id=1, source_target_pairs={{1,2},{2,1},{5,6},{6,5},{9,10},{10,9},{13,14},{14,13},{17,18},{18,... | collective-permute-start | bytes 3145736 | tf_op jit(solution)/shard_map/ppermute | solution.py:318
  224.3 12.7 %collective-permute-start.40 = (f32[2,64,16,128]{3,2,1,0:T(8,128)S(1)}, f32[2,64,16,128]{3,2,1,0:T(8,128)S(1)}, u32[]{:S(2)}, u32[]{:S(2)}) collective-permute-start(f32[2,64,16,128]{3,2,1,0:T(8,128)S(1)} %get-tuple-element.102), channel_id=1, source_target_pairs={{0,2},{1,3},{2,0},{3,1},{4,6},{5,7},{6,4},{7,5},{8,10},{9,11},{10,... | collective-permute-start | bytes 3145736 | tf_op jit(solution)/shard_map/ppermute | solution.py:318
  228.3 20.0 %collective-permute-start.39 = (f32[2,8,128,128]{3,2,1,0:T(8,128)S(1)}, f32[2,8,128,128]{3,2,1,0:T(8,128)S(1)}, u32[]{:S(2)}, u32[]{:S(2)}) collective-permute-start(f32[2,8,128,128]{3,2,1,0:T(8,128)S(1)} %shard_map.158), channel_id=1, source_target_pairs={{1,2},{2,1},{5,6},{6,5},{9,10},{10,9},{13,14},{14,13},{17,18},{18,... | collective-permute-start | bytes 3145736 | tf_op jit(solution)/shard_map/ppermute | solution.py:318
  230.7 17.6 %collective-permute-start.42 = (f32[2,64,16,128]{3,2,1,0:T(8,128)S(1)}, f32[2,64,16,128]{3,2,1,0:T(8,128)S(1)}, u32[]{:S(2)}, u32[]{:S(2)}) collective-permute-start(f32[2,64,16,128]{3,2,1,0:T(8,128)S(1)} %get-tuple-element.104), channel_id=1, source_target_pairs={{0,2},{1,3},{2,0},{3,1},{4,6},{5,7},{6,4},{7,5},{8,10},{9,11},{10,... | collective-permute-start | bytes 3145736 | tf_op jit(solution)/shard_map/ppermute | solution.py:318
  240.8 18.7 %collective-permute-start.41 = (f32[2,8,128,128]{3,2,1,0:T(8,128)S(1)}, f32[2,8,128,128]{3,2,1,0:T(8,128)S(1)}, u32[]{:S(2)}, u32[]{:S(2)}) collective-permute-start(f32[2,8,128,128]{3,2,1,0:T(8,128)S(1)} %shard_map.159), channel_id=1, source_target_pairs={{1,2},{2,1},{5,6},{6,5},{9,10},{10,9},{13,14},{14,13},{17,18},{18,... | collective-permute-start | bytes 3145736 | tf_op jit(solution)/shard_map/ppermute | solution.py:318
  252.0 18.7 %collective-permute-start.43 = (f32[2,8,128,128]{3,2,1,0:T(8,128)S(1)}, f32[2,8,128,128]{3,2,1,0:T(8,128)S(1)}, u32[]{:S(2)}, u32[]{:S(2)}) collective-permute-start(f32[2,8,128,128]{3,2,1,0:T(8,128)S(1)} %shard_map.160), channel_id=1, source_target_pairs={{1,2},{2,1},{5,6},{6,5},{9,10},{10,9},{13,14},{14,13},{17,18},{18,... | collective-permute-start | bytes 3145736 | tf_op jit(solution)/shard_map/ppermute | solution.py:318
  (37 other events, 271.1 us)

commit v3 on v2

--- a/solution.py
+++ b/solution.py
@@ -14,6 +14,8 @@
 BF16 = jnp.bfloat16
 ROWS = 8
 CHUNKS = 8
+UNITS = 2
+MIDDLE_ROWS = 16
 GROUPS = ((0, 4), (4, 6), (6, 8))
 TERM_GROUPS = ((0, 2), (2, 4), (4, 6), (6, 8))
 HOP_STEPS = 2
@@ -187,9 +189,16 @@
     part = phi.shape[1]
     rows = 2 * part
     core = info[0]
-    near, far = phi[core], phi[1 - core]
-    re = jnp.concatenate([near * own[0, 0], far * other[0, 0]], axis=0)
-    im = jnp.concatenate([near * own[0, 1], far * other[0, 1]], axis=0)
+    units = own.shape[0]
+    part = part // units
+    re, im = [], []
+    for u in range(units):
+        near = phi[core, u * part : (u + 1) * part]
+        far = phi[1 - core, u * part : (u + 1) * part]
+        re += [near * own[u, 0], far * other[u, 0]]
+        im += [near * own[u, 1], far * other[u, 1]]
+    re = jnp.concatenate(re, axis=0)
+    im = jnp.concatenate(im, axis=0)
     data = jnp.concatenate([re, im], axis=-1).reshape(rows * grid, 2 * grid)
     lines = right(data, wyh[...], wyl[...])
     for first in range(0, rows, 2):
@@ -261,7 +270,8 @@
 def backward_body(info, keep, recv, own, other, wxh, wxl, wyh, wyl, out):
     grid = keep.shape[-1]
     rows = keep.shape[2]
-    part = rows // 2
+    units = own.shape[0]
+    part = rows // 2 // units
     core = info[0]
     lines = []
     for first in range(0, rows, 2):
@@ -280,8 +290,12 @@
     fields = right(jnp.concatenate(lines, axis=0), wyh[...], wyl[...])
     re = fields[:, :grid].reshape(rows, grid, grid)
     im = fields[:, grid:].reshape(rows, grid, grid)
-    out[core] = re[:part] * own[0, 0] + im[:part] * own[0, 1]
-    out[1 - core] = re[part:] * other[0, 0] + im[part:] * other[0, 1]
+    for u in range(units):
+        near = slice(2 * u * part, (2 * u + 1) * part)
+        far = slice((2 * u + 1) * part, (2 * u + 2) * part)
+        place = pl.ds(u * part, part)
+        out[core, place] = re[near] * own[u, 0] + im[near] * own[u, 1]
+        out[1 - core, place] = re[far] * other[u, 0] + im[far] * other[u, 1]
 
 
 def call(body, grid_size, in_specs, out_specs, out_shape):
@@ -294,7 +308,7 @@
             out_specs=out_specs,
         ),
         out_shape=out_shape,
-        compiler_params=pltpu.CompilerParams(vmem_limit_bytes=16 * 1024 * 1024),
+        compiler_params=pltpu.CompilerParams(vmem_limit_bytes=32 * 1024 * 1024),
     )
 
 
@@ -355,14 +369,15 @@
     )
     first_in = move(first_out, sibling)
     chosen_orbital = lax.dynamic_index_in_dim(orbitals, pick, 0, keepdims=False)
+    rest_in = move(orbitals, sibling).reshape(cut.shape)
     first_in, chosen_orbital, cut = lax.optimization_barrier((first_in, chosen_orbital, cut))
     crossed = move(chosen_orbital, cross)
-    bounds = ((1, 3), (3, CHUNKS))
-    rest_in = [move(of_half(1 - core, lo, hi), sibling) for lo, hi in bounds]
     fresh = [jnp.where(direct, own_first, first_in)[:, 0]]
-    for (lo, hi), other in zip(bounds, rest_in):
-        more = jnp.where(direct, of_half(core, lo, hi), other)
-        fresh += [more[:, k] for k in range(hi - lo)]
+    for k in range(1, CHUNKS):
+        begin = (0, core, k * part, 0, 0)
+        size = (n_orb, 1, part, grid, grid)
+        both = [lax.dynamic_slice(v, begin, size)[:, 0] for v in (cut, rest_in)]
+        fresh.append(jnp.where(direct, *both))
     info = jnp.stack([core.astype(jnp.int32), distance.astype(jnp.int32)])
 
     steps = CHUNKS + length - 2
@@ -389,12 +404,17 @@
         values += [item[1] for item in joined + landed]
         if t == 1:
             values.append(info)
+        if t == 2:
+            values += fresh[3:]
         if t == PHI_STEP:
             values.append(crossed)
         if t == PHI_STEP + 1:
             values.append(phi)
         if len(values) > 1:
             values = list(lax.optimization_barrier(tuple(values)))
+        if t == 2:
+            fresh[3:] = values[-len(fresh[3:]) :]
+            values = values[: -len(fresh[3:])]
         if t == 1:
             info = values.pop()
         if t == PHI_STEP + 1:
@@ -433,15 +453,17 @@
 
     square = (2 * grid, 2 * grid)
 
-    pairs = pl.BlockSpec((1,) + chunk_shape, lambda i, info: (i, 0, 0, 0, 0))
-    lines = pl.BlockSpec((2, half, planes, grid), lambda i, info: (0, 0, i, 0))
+    pairs = pl.BlockSpec((UNITS,) + chunk_shape, lambda i, info: (i, 0, 0, 0, 0))
+    lines = pl.BlockSpec((2, half, UNITS * planes, grid), lambda i, info: (0, 0, i, 0))
     keeps, sends = [], []
     for g, (lo, hi) in enumerate(GROUPS):
         spectrum = jax.ShapeDtypeStruct((2, half, (hi - lo) * planes, grid), F32)
-        slab = pl.BlockSpec((2, part, grid, grid), lambda i, info, lo=lo: (0, lo + i, 0, 0))
+        slab = pl.BlockSpec(
+            (2, UNITS * part, grid, grid), lambda i, info, lo=lo: (0, lo // UNITS + i, 0, 0)
+        )
         keep, send = call(
             forward_body,
-            hi - lo,
+            (hi - lo) // UNITS,
             [slab, pairs, pairs] + [whole(square)] * 2 + [chosen(square)] * 2,
             [lines, lines],
             [spectrum, spectrum],
@@ -450,13 +472,13 @@
         sends.append(send)
     recvs = [move(send, sibling) for send in sends]
     cols = [
-        pl.BlockSpec((2, ROWS, (hi - lo) * planes, grid), lambda i, info: (0, i, 0, 0))
+        pl.BlockSpec((2, MIDDLE_ROWS, (hi - lo) * planes, grid), lambda i, info: (0, i, 0, 0))
         for lo, hi in GROUPS
     ]
     shapes = [jax.ShapeDtypeStruct(keep.shape, F32) for keep in keeps]
     results = call(
         middle_body,
-        half // ROWS,
+        half // MIDDLE_ROWS,
         cols * 2 + [chosen(square)] * 4,
         cols * 2,
         shapes * 2,
@@ -471,20 +493,20 @@
         if len(terms) > 1:
             there, keep = lax.optimization_barrier((terms[-2][1], keep))
             terms[-2] = (terms[-2][0], there)
-        shift = lo - start
+        shift = (lo - start) // UNITS
         some_lines = pl.BlockSpec(
-            (2, half, planes, grid), lambda i, info, shift=shift: (0, 0, shift + i, 0)
+            (2, half, UNITS * planes, grid), lambda i, info, shift=shift: (0, 0, shift + i, 0)
         )
         some_pairs = pl.BlockSpec(
-            (1,) + chunk_shape, lambda i, info, shift=shift: (shift + i, 0, 0, 0, 0)
+            (UNITS,) + chunk_shape, lambda i, info, shift=shift: (shift + i, 0, 0, 0, 0)
         )
         term = call(
             backward_body,
-            hi - lo,
+            (hi - lo) // UNITS,
             [some_lines, some_lines, some_pairs, some_pairs]
             + [chosen(square)] * 2
             + [whole(square)] * 2,
-            pl.BlockSpec((2, part, grid, grid), lambda i, info: (0, i, 0, 0)),
+            pl.BlockSpec((2, UNITS * part, grid, grid), lambda i, info: (0, i, 0, 0)),
             jax.ShapeDtypeStruct((2, (hi - lo) * part, grid, grid), F32),
         )(info, keep, recv, own[g], other[g], *table["mid_inv"], *table["last_inv"])
         terms.append((term, move(term, cross)))

time: 275 us -> 261 us (0.949)
  local copies, waits for them, and re-layouts: 16.2 us -> 7.5 us
  Pallas kernels: 65.8 us -> 60.8 us
    pallas_call x8, Pallas kernels: 45.7 us -> 40.5 us  [the longest x3 16.2 us: paired(): call(forward_body, (hi - lo) // UNITS, [slab, pairs, pairs] + [whole(squa...]
    unnamed x83 -> x79, local copies, waits for them, and re-layouts: 6.71 us -> 2.8 us
    reshape x2 -> x0, local copies, waits for them, and re-layouts: 2.86 us -> none  [of_half(): return piece.reshape((n_orb, hi - lo, part, grid, grid))]
    ppermute x44 -> x43, starting transfers between devices: 63.6 us -> 61 us  [move(): return lax.ppermute(value, axes, pairs)]
    ppermute x44 -> x43, waiting for transfers between devices: 93.8 us -> 94.7 us  [move(): return lax.ppermute(value, axes, pairs)]
  transfers between devices with their start and end apart: 44 -> 43, of which waited for: 26 -> 27; matrix products, arithmetic and copies ran while one was open for 13% -> 13% of each run, Pallas kernels for 18% -> 18%
where the time goes in v3:
time: 261 us; the launch traced here: 260 us
  waiting for transfers between devices  94.7 us (36%)
  starting transfers between devices  61 us (23%)
  Pallas kernels  60.8 us (23%)
  other arithmetic  33.8 us (13%)
  local copies, waits for them, and re-layouts  7.5 us (3%)
    ppermute x43, waiting for transfers between devices, move(): return lax.ppermute(value, axes, pairs)  94.7 us
    ppermute x43, starting transfers between devices, move(): return lax.ppermute(value, axes, pairs)  61 us
    pallas_call x8, Pallas kernels, arrived(): pl.pallas_call(pick_body, in_specs=[pl.BlockSpec(memory_space=pltpu.SMEM)...  20.2 us
    pallas_call x3, Pallas kernels, paired(): call(forward_body, (hi - lo) // UNITS, [slab, pairs, pairs] + [whole(squa...  16.2 us
    pallas_call x4, Pallas kernels, paired(): call(backward_body, (hi - lo) // UNITS, [some_lines, some_lines, some_pai...  13.7 us
    pallas_call x1, Pallas kernels, paired(): call(middle_body, half // MIDDLE_ROWS, cols * 2 + [chosen(square)] * 4, c...  10.7 us
    another operation x8, other arithmetic, paired(): own = [jnp.stack(owns[lo:hi]) for lo, hi in GROUPS]  9.47 us
    select_n x1, other arithmetic, paired(): phi = jnp.where(home, chosen_orbital, values.pop())  5.29 us
  transfers between devices with their start and end apart: 43, of which 27 were waited for; matrix products, arithmetic and copies ran while one was open for 13% of the time, Pallas kernels for 18%

profile of v3, /device:TPU:1, one launch (start us, length us, event | category | flops | bytes accessed | tf_op | source)
XLA Modules:
  0.0 259.9 jit_solution(3774206506029271816)
XLA Ops:
  3.2 4.7 %dynamic-slice_bitcast_fusion = f32[64,128,128]{2,1,0:T(8,128)} fusion(f32[2,64,128,128]{3,2,1,0:T(8,128)} %param.15, s32[]{:T(128)S(6)} %select_n.264), kind=kLoop, calls=%fused_computation.1 | loop fusion | bytes 8388612 | tf_op jit(solution)/shard_map/jit(dynamic_index_in_dim)/squeeze | solution.py:371
  8.3 3.1 %collective-permute-start.1 = (f32[2,4,128,128]{3,2,1,0:T(8,128)S(1)}, f32[2,4,128,128]{3,2,1,0:T(8,128)S(1)}, u32[]{:S(2)}, u32[]{:S(2)}) collective-permute-start(f32[2,4,128,128]{3,2,1,0:T(8,128)S(1)} %select_bitcast_fusion.8.refs_0_), channel_id=1, source_target_pairs={{0,8},{1,9},{2,6},{3,7},{4,0},{5,1},{6,14},{7,15},{8,16},{9,17},{1... | collective-permute-start | bytes 1572872 | tf_op jit(solution)/shard_map/ppermute | solution.py:332
  11.4 3.5 %collective-permute-start.8 = (f32[64,128,128]{2,1,0:T(8,128)}, f32[64,128,128]{2,1,0:T(8,128)}, u32[]{:S(2)}, u32[]{:S(2)}) collective-permute-start(f32[64,128,128]{2,1,0:T(8,128)} %dynamic-slice_bitcast_fusion), channel_id=1, source_target_pairs={{1,2},{2,1},{5,6},{6,5},{9,10},{10,9},{13,14},{14,13},{17,18},{18,... | collective-permute-start | bytes 12582920 | tf_op jit(solution)/shard_map/ppermute | solution.py:332
  15.6 2.7 %collective-permute-done.1 = f32[2,4,128,128]{3,2,1,0:T(8,128)S(1)} collective-permute-done((f32[2,4,128,128]{3,2,1,0:T(8,128)S(1)}, f32[2,4,128,128]{3,2,1,0:T(8,128)S(1)}, u32[]{:S(2)}, u32[]{:S(2)}) %collective-permute-start.1) | collective-permute-done | bytes 524320 | tf_op jit(solution)/shard_map/ppermute | solution.py:332
  21.1 3.7 %fusion.2 = (f32[2,4,128,128]{3,2,1,0:T(8,128)S(1)}, f32[2,4,128,128]{3,2,1,0:T(8,128)}, f32[2,4,128,128]{3,2,1,0:T(8,128)S(1)}, f32[2,4,128,128]{3,2,1,0:T(8,128)S(1)}, f32[2,4,128,128]{3,2,1,0:T(8,128)S(1)}) fusion(f32[2,2,32,128,128]{4,3,2,1,0:T(8,128)} %bitcast.7, s32[]{:T(128)S(6)} %select_n.263, pred[]{:T(512)S(6)} %eq.26, ...), kind=kLoop, calls=%fused_computation.13 | loop fusion | flops 655360 | bytes 7864325 | tf_op jit(solution)/shard_map/jit(_where)/select_n | solution.py:380
  24.8 3.2 %collective-permute-done.3 = f32[2,4,128,128]{3,2,1,0:T(8,128)S(1)} collective-permute-done((f32[2,4,128,128]{3,2,1,0:T(8,128)S(1)}, f32[2,4,128,128]{3,2,1,0:T(8,128)S(1)}, u32[]{:S(2)}, u32[]{:S(2)}) %collective-permute-start.3) | collective-permute-done | bytes 524320 | tf_op jit(solution)/shard_map/ppermute | solution.py:332
  30.8 6.9 %collective-permute-done.4 = f32[2,4,128,128]{3,2,1,0:T(8,128)S(1)} collective-permute-done((f32[2,4,128,128]{3,2,1,0:T(8,128)S(1)}, f32[2,4,128,128]{3,2,1,0:T(8,128)S(1)}, u32[]{:S(2)}, u32[]{:S(2)}) %collective-permute-start.4) | collective-permute-done | bytes 524320 | tf_op jit(solution)/shard_map/ppermute | solution.py:332
  39.3 6.9 %collective-permute-done.5 = f32[2,4,128,128]{3,2,1,0:T(8,128)S(1)} collective-permute-done((f32[2,4,128,128]{3,2,1,0:T(8,128)S(1)}, f32[2,4,128,128]{3,2,1,0:T(8,128)S(1)}, u32[]{:S(2)}, u32[]{:S(2)}) %collective-permute-start.5) | collective-permute-done | bytes 524320 | tf_op jit(solution)/shard_map/ppermute | solution.py:332
  47.7 6.9 %collective-permute-done.6 = f32[2,4,128,128]{3,2,1,0:T(8,128)S(1)} collective-permute-done((f32[2,4,128,128]{3,2,1,0:T(8,128)S(1)}, f32[2,4,128,128]{3,2,1,0:T(8,128)S(1)}, u32[]{:S(2)}, u32[]{:S(2)}) %collective-permute-start.6) | collective-permute-done | bytes 524320 | tf_op jit(solution)/shard_map/ppermute | solution.py:332
  56.2 5.3 %collective-permute-done.8 = f32[64,128,128]{2,1,0:T(8,128)} collective-permute-done((f32[64,128,128]{2,1,0:T(8,128)}, f32[64,128,128]{2,1,0:T(8,128)}, u32[]{:S(2)}, u32[]{:S(2)}) %collective-permute-start.8) | collective-permute-done | bytes 4194336 | tf_op jit(solution)/shard_map/ppermute | solution.py:332
  64.7 5.3 %broadcast_select_fusion = f32[64,128,128]{2,1,0:T(8,128)} fusion(f32[64,128,128]{2,1,0:T(8,128)} %dynamic-slice_bitcast_fusion, f32[64,128,128]{2,1,0:T(8,128)} %collective-permute-done.8, pred[]{:T(512)S(6)} %eq.25), kind=kLoop, calls=%fused_computation.4 | loop fusion | flops 1048576 | bytes 12582913 | tf_op jit(solution)/shard_map/jit(_where)/select_n | solution.py:423
  70.1 2.6 %collective-permute-done.9 = f32[2,4,128,128]{3,2,1,0:T(8,128)S(1)} collective-permute-done((f32[2,4,128,128]{3,2,1,0:T(8,128)S(1)}, f32[2,4,128,128]{3,2,1,0:T(8,128)S(1)}, u32[]{:S(2)}, u32[]{:S(2)}) %collective-permute-start.9) | collective-permute-done | bytes 524320 | tf_op jit(solution)/shard_map/ppermute | solution.py:332
  73.6 2.5 shard_map.145
  78.1 2.8 %collective-permute-done.10.refs_7_.refs_6_.refs_5_.refs_4_.refs_3_.refs_2_.refs_1_ = f32[2,4,128,128]{3,2,1,0:T(8,128)S(1)} collective-permute-done((f32[2,4,128,128]{3,2,1,0:T(8,128)S(1)}, f32[2,4,128,128]{3,2,1,0:T(8,128)S(1)}, u32[]{:S(2)}, u32[]{:S(2)}) %collective-permute-start.10) | collective-permute-done | bytes 524320 | tf_op jit(solution)/shard_map/ppermute | solution.py:332
  81.7 2.5 shard_map.146
  86.2 3.0 %collective-permute-done.11.refs_7_.refs_6_.refs_5_.refs_4_.refs_3_.refs_2_ = f32[2,4,128,128]{3,2,1,0:T(8,128)S(1)} collective-permute-done((f32[2,4,128,128]{3,2,1,0:T(8,128)S(1)}, f32[2,4,128,128]{3,2,1,0:T(8,128)S(1)}, u32[]{:S(2)}, u32[]{:S(2)}) %collective-permute-start.11) | collective-permute-done | bytes 524320 | tf_op jit(solution)/shard_map/ppermute | solution.py:332
  90.2 8.2 %collective-permute-start.15 = (f32[2,4,128,128]{3,2,1,0:T(8,128)}, f32[2,4,128,128]{3,2,1,0:T(8,128)}, u32[]{:S(2)}, u32[]{:S(2)}) collective-permute-start(f32[2,4,128,128]{3,2,1,0:T(8,128)} %get-tuple-element.135), channel_id=1, source_target_pairs={{0,2},{1,3},{2,0},{3,1},{4,6},{5,7},{6,4},{7,5},{8,10},{9,11},{10,... | collective-permute-start | bytes 1572872 | tf_op jit(solution)/shard_map/ppermute | solution.py:332
  99.3 2.5 shard_map.147
  103.1 3.6 %collective-permute-done.13.refs_7_.refs_6_.refs_5_.refs_4_.refs_3_ = f32[2,4,128,128]{3,2,1,0:T(8,128)S(1)} collective-permute-done((f32[2,4,128,128]{3,2,1,0:T(8,128)S(1)}, f32[2,4,128,128]{3,2,1,0:T(8,128)S(1)}, u32[]{:S(2)}, u32[]{:S(2)}) %collective-permute-start.13) | collective-permute-done | bytes 524320 | tf_op jit(solution)/shard_map/ppermute | solution.py:332
  106.7 2.3 select_bitcast_fusion.6
  110.8 2.5 shard_map.148
  114.8 3.5 %collective-permute-done.16.refs_7_.refs_6_.refs_5_.refs_4_ = f32[2,4,128,128]{3,2,1,0:T(8,128)S(1)} collective-permute-done((f32[2,4,128,128]{3,2,1,0:T(8,128)S(1)}, f32[2,4,128,128]{3,2,1,0:T(8,128)S(1)}, u32[]{:S(2)}, u32[]{:S(2)}) %collective-permute-start.16) | collective-permute-done | bytes 524320 | tf_op jit(solution)/shard_map/ppermute | solution.py:332
  121.2 2.5 shard_map.149
  126.4 2.2 collective-permute-done.19.refs_7_.refs_6_.refs_5_
  128.6 2.3 broadcast_select_fusion.9
  132.7 2.5 shard_map.151
  144.0 2.5 shard_map.152
  154.3 2.5 shard_map.154
  158.3 2.3 collective-permute-done.28
  167.4 8.0 %shard_map.150 = (f32[2,64,32,128]{3,2,1,0:T(8,128)S(1)}, f32[2,64,32,128]{3,2,1,0:T(8,128)S(1)}) custom-call(s32[2]{0:T(128)S(1)} %copy-done.13, f32[2,32,128,128]{3,2,1,0:T(8,128)S(1)} %bitcast.97, f32[4,2,4,128,128]{4,3,2,1,0:T(8,128)S(1)} %pad_maximum_fusion.1.own, f32[4,2,4,128,128]{4,3,2,1,0:T(8,128)S(1)} %pad_maximum_fusion.2.other, ...), custom_call_target="tpu_custom_call" | custom-call | tf_op jit(solution)/shard_map/pallas_call | solution.py:464
  177.6 4.1 %shard_map.153 = (f32[2,64,16,128]{3,2,1,0:T(8,128)S(1)}, f32[2,64,16,128]{3,2,1,0:T(8,128)S(1)}) custom-call(s32[2]{0:T(128)S(1)} %copy-done.13, f32[2,32,128,128]{3,2,1,0:T(8,128)S(1)} %bitcast.98, f32[2,2,4,128,128]{4,3,2,1,0:T(8,128)S(1)} %pad_maximum_fusion.3.own, f32[2,2,4,128,128]{4,3,2,1,0:T(8,128)S(1)} %pad_maximum_fusion.4.other, ...), custom_call_target="tpu_custom_call" | custom-call | tf_op jit(solution)/shard_map/pallas_call | solution.py:464
  182.0 4.1 %shard_map.155 = (f32[2,64,16,128]{3,2,1,0:T(8,128)S(1)}, f32[2,64,16,128]{3,2,1,0:T(8,128)S(1)}) custom-call(s32[2]{0:T(128)S(1)} %copy-done.13, f32[2,32,128,128]{3,2,1,0:T(8,128)S(1)} %bitcast.99, f32[2,2,4,128,128]{4,3,2,1,0:T(8,128)S(1)} %pad_maximum_fusion.5.own, f32[2,2,4,128,128]{4,3,2,1,0:T(8,128)S(1)} %pad_maximum_fusion.6.other, ...), custom_call_target="tpu_custom_call" | custom-call | tf_op jit(solution)/shard_map/pallas_call | solution.py:464
  186.7 2.3 collective-permute-done.35.refs_5_
  189.0 10.7 %shard_map.156 = (f32[2,64,32,128]{3,2,1,0:T(8,128)S(1)}, f32[2,64,16,128]{3,2,1,0:T(8,128)S(1)}, f32[2,64,16,128]{3,2,1,0:T(8,128)S(1)}, f32[2,64,32,128]{3,2,1...) custom-call(s32[2]{0:T(128)S(1)} %copy-done.13, ...), custom_call_target="tpu_custom_call" | custom-call | tf_op jit(solution)/shard_map/pallas_call | solution.py:479
  200.1 3.8 %collective-permute-done.36.recv = f32[2,64,32,128]{3,2,1,0:T(8,128)S(1)} collective-permute-done((f32[2,64,32,128]{3,2,1,0:T(8,128)S(1)}, f32[2,64,32,128]{3,2,1,0:T(8,128)S(1)}, u32[]{:S(2)}, u32[]{:S(2)}) %collective-permute-start.36) | collective-permute-done | bytes 2097184 | tf_op jit(solution)/shard_map/ppermute | solution.py:332
  203.9 3.6 %shard_map.157 = f32[2,8,128,128]{3,2,1,0:T(8,128)S(1)} custom-call(s32[2]{0:T(128)S(1)} %copy-done.13, f32[2,64,32,128]{3,2,1,0:T(8,128)S(1)} %get-tuple-element.107.keep, f32[2,64,32,128]{3,2,1,0:T(8,128)S(1)} %collective-permute-done.36.recv, f32[4,2,4,128,128]{4,3,2,1,0:T(8,128)S(1)} %pad_maximum_fusion.1.own, ...), custom_call_target="tpu_custom_call" | custom-call | tf_op jit(solution)/shard_map/pallas_call | solution.py:503
  207.5 3.4 %collective-permute-start.37 = (f32[2,8,128,128]{3,2,1,0:T(8,128)S(1)}, f32[2,8,128,128]{3,2,1,0:T(8,128)S(1)}, u32[]{:S(2)}, u32[]{:S(2)}) collective-permute-start(f32[2,8,128,128]{3,2,1,0:T(8,128)S(1)} %shard_map.157), channel_id=1, source_target_pairs={{1,2},{2,1},{5,6},{6,5},{9,10},{10,9},{13,14},{14,13},{17,18},{18,... | collective-permute-start | bytes 3145736 | tf_op jit(solution)/shard_map/ppermute | solution.py:332
  210.9 3.5 %shard_map.158 = f32[2,8,128,128]{3,2,1,0:T(8,128)S(1)} custom-call(s32[2]{0:T(128)S(1)} %copy-done.13, f32[2,64,32,128]{3,2,1,0:T(8,128)S(1)} %get-tuple-element.107.keep, f32[2,64,32,128]{3,2,1,0:T(8,128)S(1)} %collective-permute-done.36.recv, f32[4,2,4,128,128]{4,3,2,1,0:T(8,128)S(1)} %pad_maximum_fusion.1.own, ...), custom_call_target="tpu_custom_call" | custom-call | tf_op jit(solution)/shard_map/pallas_call | solution.py:503
  214.5 2.2 collective-permute-start.38
  216.8 6.8 %collective-permute-done.37 = f32[2,8,128,128]{3,2,1,0:T(8,128)S(1)} collective-permute-done((f32[2,8,128,128]{3,2,1,0:T(8,128)S(1)}, f32[2,8,128,128]{3,2,1,0:T(8,128)S(1)}, u32[]{:S(2)}, u32[]{:S(2)}) %collective-permute-start.37) | collective-permute-done | bytes 1048608 | tf_op jit(solution)/shard_map/ppermute | solution.py:332
  223.6 3.3 %shard_map.159 = f32[2,8,128,128]{3,2,1,0:T(8,128)S(1)} custom-call(s32[2]{0:T(128)S(1)} %copy-done.13, f32[2,64,16,128]{3,2,1,0:T(8,128)S(1)} %get-tuple-element.113.keep, f32[2,64,16,128]{3,2,1,0:T(8,128)S(1)} %collective-permute-done.39.recv, f32[2,2,4,128,128]{4,3,2,1,0:T(8,128)S(1)} %pad_maximum_fusion.3.own, ...), custom_call_target="tpu_custom_call" | custom-call | tf_op jit(solution)/shard_map/pallas_call | solution.py:503
  226.9 3.6 %collective-permute-start.40 = (f32[2,8,128,128]{3,2,1,0:T(8,128)S(1)}, f32[2,8,128,128]{3,2,1,0:T(8,128)S(1)}, u32[]{:S(2)}, u32[]{:S(2)}) collective-permute-start(f32[2,8,128,128]{3,2,1,0:T(8,128)S(1)} %shard_map.159), channel_id=1, source_target_pairs={{1,2},{2,1},{5,6},{6,5},{9,10},{10,9},{13,14},{14,13},{17,18},{18,... | collective-permute-start | bytes 3145736 | tf_op jit(solution)/shard_map/ppermute | solution.py:332
  230.5 4.3 %collective-permute-done.38 = f32[2,8,128,128]{3,2,1,0:T(8,128)S(1)} collective-permute-done((f32[2,8,128,128]{3,2,1,0:T(8,128)S(1)}, f32[2,8,128,128]{3,2,1,0:T(8,128)S(1)}, u32[]{:S(2)}, u32[]{:S(2)}) %collective-permute-start.38) | collective-permute-done | bytes 1048608 | tf_op jit(solution)/shard_map/ppermute | solution.py:332
  234.8 3.3 %shard_map.160 = f32[2,8,128,128]{3,2,1,0:T(8,128)S(1)} custom-call(s32[2]{0:T(128)S(1)} %copy-done.13, f32[2,64,16,128]{3,2,1,0:T(8,128)S(1)} %get-tuple-element.115.keep, f32[2,64,16,128]{3,2,1,0:T(8,128)S(1)} %collective-permute-done.41.recv, f32[2,2,4,128,128]{4,3,2,1,0:T(8,128)S(1)} %pad_maximum_fusion.5.own, ...), custom_call_target="tpu_custom_call" | custom-call | tf_op jit(solution)/shard_map/pallas_call | solution.py:503
  238.1 3.4 %collective-permute-start.42 = (f32[2,8,128,128]{3,2,1,0:T(8,128)S(1)}, f32[2,8,128,128]{3,2,1,0:T(8,128)S(1)}, u32[]{:S(2)}, u32[]{:S(2)}) collective-permute-start(f32[2,8,128,128]{3,2,1,0:T(8,128)S(1)} %shard_map.160), channel_id=1, source_target_pairs={{1,2},{2,1},{5,6},{6,5},{9,10},{10,9},{13,14},{14,13},{17,18},{18,... | collective-permute-start | bytes 3145736 | tf_op jit(solution)/shard_map/ppermute | solution.py:332
  241.8 4.3 %collective-permute-done.40 = f32[2,8,128,128]{3,2,1,0:T(8,128)S(1)} collective-permute-done((f32[2,8,128,128]{3,2,1,0:T(8,128)S(1)}, f32[2,8,128,128]{3,2,1,0:T(8,128)S(1)}, u32[]{:S(2)}, u32[]{:S(2)}) %collective-permute-start.40) | collective-permute-done | bytes 1048608 | tf_op jit(solution)/shard_map/ppermute | solution.py:332
  246.2 11.1 %collective-permute-done.42 = f32[2,8,128,128]{3,2,1,0:T(8,128)S(1)} collective-permute-done((f32[2,8,128,128]{3,2,1,0:T(8,128)S(1)}, f32[2,8,128,128]{3,2,1,0:T(8,128)S(1)}, u32[]{:S(2)}, u32[]{:S(2)}) %collective-permute-start.42) | collective-permute-done | bytes 1048608 | tf_op jit(solution)/shard_map/ppermute | solution.py:332
  257.4 2.5 pad_maximum_fusion
  (164 shorter events, 64.3 us)
Async XLA Ops:
  1.3 17.0 %collective-permute-start.2 = (f32[2,64,128,128]{3,2,1,0:T(8,128)}, f32[2,64,128,128]{3,2,1,0:T(8,128)}, u32[]{:S(2)}, u32[]{:S(2)}) collective-permute-start(f32[2,64,128,128]{3,2,1,0:T(8,128)} %param.15), channel_id=1, source_target_pairs={{0,2},{1,3},{2,0},{3,1},{4,6},{5,7},{6,4},{7,5},{8,10},{9,11},{10,... | collective-permute-start | bytes 25165832 | tf_op jit(solution)/shard_map/ppermute | solution.py:332
  1.4 6.8 %collective-permute-start = (f32[2,1,4,128,128]{4,3,2,0,1:T(8,128)S(1)}, f32[2,1,4,128,128]{4,3,2,0,1:T(8,128)S(1)}, u32[]{:S(2)}, u32[]{:S(2)}) collective-permute-start(f32[2,1,4,128,128]{4,3,2,0,1:T(8,128)S(1)} %get-tuple-element.62), channel_id=1, source_target_pairs={{0,2},{1,3},{2,0},{3,1},{4,6},{5,7},{6,4},{7,5},{8,10},{9,11},{10,... | collective-permute-start | bytes 1572872 | tf_op jit(solution)/shard_map/ppermute | solution.py:332
  8.3 10.0 %collective-permute-start.1 = (f32[2,4,128,128]{3,2,1,0:T(8,128)S(1)}, f32[2,4,128,128]{3,2,1,0:T(8,128)S(1)}, u32[]{:S(2)}, u32[]{:S(2)}) collective-permute-start(f32[2,4,128,128]{3,2,1,0:T(8,128)S(1)} %select_bitcast_fusion.8.refs_0_), channel_id=1, source_target_pairs={{0,8},{1,9},{2,6},{3,7},{4,0},{5,1},{6,14},{7,15},{8,16},{9,17},{1... | collective-permute-start | bytes 1572872 | tf_op jit(solution)/shard_map/ppermute | solution.py:332
  11.4 50.1 %collective-permute-start.8 = (f32[64,128,128]{2,1,0:T(8,128)}, f32[64,128,128]{2,1,0:T(8,128)}, u32[]{:S(2)}, u32[]{:S(2)}) collective-permute-start(f32[64,128,128]{2,1,0:T(8,128)} %dynamic-slice_bitcast_fusion), channel_id=1, source_target_pairs={{1,2},{2,1},{5,6},{6,5},{9,10},{10,9},{13,14},{14,13},{17,18},{18,... | collective-permute-start | bytes 12582920 | tf_op jit(solution)/shard_map/ppermute | solution.py:332
  19.6 8.4 %collective-permute-start.3 = (f32[2,4,128,128]{3,2,1,0:T(8,128)S(1)}, f32[2,4,128,128]{3,2,1,0:T(8,128)S(1)}, u32[]{:S(2)}, u32[]{:S(2)}) collective-permute-start(f32[2,4,128,128]{3,2,1,0:T(8,128)S(1)} %fusion.8.refs_1_.refs_0_), channel_id=1, source_target_pairs={{0,8},{1,9},{2,6},{3,7},{4,0},{5,1},{6,14},{7,15},{8,16},{9,17},{1... | collective-permute-start | bytes 1572872 | tf_op jit(solution)/shard_map/ppermute | solution.py:332
  28.0 35.2 %copy-start.36 = (f32[2,4,128,128]{3,2,1,0:T(8,128)S(1)}, f32[2,4,128,128]{3,2,1,0:T(8,128)}, u32[]{:S(2)}) copy-start(f32[2,4,128,128]{3,2,1,0:T(8,128)} %get-tuple-element.69) | copy-start | bytes 1572868
  29.3 40.7 %copy-start.23 = (f32[2,4,128,128]{3,2,1,0:T(8,128)}, f32[2,4,128,128]{3,2,1,0:T(8,128)S(1)}, u32[]{:S(2)}) copy-start(f32[2,4,128,128]{3,2,1,0:T(8,128)S(1)} %fusion.1.refs_2_.refs_1_.refs_0_) | copy-start | bytes 1572868
  29.3 8.4 %collective-permute-start.4 = (f32[2,4,128,128]{3,2,1,0:T(8,128)S(1)}, f32[2,4,128,128]{3,2,1,0:T(8,128)S(1)}, u32[]{:S(2)}, u32[]{:S(2)}) collective-permute-start(f32[2,4,128,128]{3,2,1,0:T(8,128)S(1)} %fusion.1.refs_2_.refs_1_.refs_0_), channel_id=1, source_target_pairs={{0,8},{1,9},{2,6},{3,7},{4,0},{5,1},{6,14},{7,15},{8,16},{9,17},{1... | collective-permute-start | bytes 1572872 | tf_op jit(solution)/shard_map/ppermute | solution.py:332
  37.8 32.2 %copy-start.21 = (f32[2,4,128,128]{3,2,1,0:T(8,128)}, f32[2,4,128,128]{3,2,1,0:T(8,128)S(1)}, u32[]{:S(2)}) copy-start(f32[2,4,128,128]{3,2,1,0:T(8,128)S(1)} %broadcast_select_fusion.17.refs_3_.refs_2_.refs_1_.refs_0_) | copy-start | bytes 1572868
  37.8 8.4 %collective-permute-start.5 = (f32[2,4,128,128]{3,2,1,0:T(8,128)S(1)}, f32[2,4,128,128]{3,2,1,0:T(8,128)S(1)}, u32[]{:S(2)}, u32[]{:S(2)}) collective-permute-start(f32[2,4,128,128]{3,2,1,0:T(8,128)S(1)} %broadcast_select_fusion.17.refs_3_.refs_2_.refs_1_.refs_0_), channel_id=1, source_target_pairs={{0,8},{1,9},{2,6},{3,7},{4,0},{5,1},{6,14},{7,15},{8,16},{9,17},{1... | collective-permute-start | bytes 1572872 | tf_op jit(solution)/shard_map/ppermute | solution.py:332
  46.3 23.8 %copy-start.19 = (f32[2,4,128,128]{3,2,1,0:T(8,128)}, f32[2,4,128,128]{3,2,1,0:T(8,128)S(1)}, u32[]{:S(2)}) copy-start(f32[2,4,128,128]{3,2,1,0:T(8,128)S(1)} %broadcast_select_fusion.16.refs_4_.refs_3_.refs_2_.refs_1_.refs_0_) | copy-start | bytes 1572868
  46.3 8.4 %collective-permute-start.6 = (f32[2,4,128,128]{3,2,1,0:T(8,128)S(1)}, f32[2,4,128,128]{3,2,1,0:T(8,128)S(1)}, u32[]{:S(2)}, u32[]{:S(2)}) collective-permute-start(f32[2,4,128,128]{3,2,1,0:T(8,128)S(1)} %broadcast_select_fusion.16.refs_4_.refs_3_.refs_2_.refs_1_.refs_0_), channel_id=1, source_target_pairs={{0,8},{1,9},{2,6},{3,7},{4,0},{5,1},{6,14},{7,15},{8,16},{9,17},{1... | collective-permute-start | bytes 1572872 | tf_op jit(solution)/shard_map/ppermute | solution.py:332
  54.7 8.5 %collective-permute-start.7 = (f32[2,4,128,128]{3,2,1,0:T(8,128)S(1)}, f32[2,4,128,128]{3,2,1,0:T(8,128)}, u32[]{:S(2)}, u32[]{:S(2)}) collective-permute-start(f32[2,4,128,128]{3,2,1,0:T(8,128)S(1)} %broadcast_select_fusion.15.refs_5_.refs_4_.refs_3_.refs_2_.refs_1_.refs_0_), channel_id=1, source_target_pairs={{0,8},{1,9},{2,6},{3,7},{4,0},{5,1},{6,14},{7,15},{8,16},{9,17},{1... | collective-permute-start | bytes 1572872 | tf_op jit(solution)/shard_map/ppermute | solution.py:332
  64.3 8.4 %collective-permute-start.9 = (f32[2,4,128,128]{3,2,1,0:T(8,128)S(1)}, f32[2,4,128,128]{3,2,1,0:T(8,128)S(1)}, u32[]{:S(2)}, u32[]{:S(2)}) collective-permute-start(f32[2,4,128,128]{3,2,1,0:T(8,128)S(1)} %broadcast_select_fusion.14.refs_6_.refs_5_.refs_4_.refs_3_.refs_2_.refs_1_.refs_0_), channel_id=1, source_target_pairs={{0,8},{1,9},{2,6},{3,7},{4,0},{5,1},{6,14},{7,15},{8,16},{9,17},{1... | collective-permute-start | bytes 1572872 | tf_op jit(solution)/shard_map/ppermute | solution.py:332
  72.8 8.1 %collective-permute-start.10 = (f32[2,4,128,128]{3,2,1,0:T(8,128)S(1)}, f32[2,4,128,128]{3,2,1,0:T(8,128)S(1)}, u32[]{:S(2)}, u32[]{:S(2)}) collective-permute-start(f32[2,4,128,128]{3,2,1,0:T(8,128)S(1)} %broadcast_select_fusion.13.refs_7_.refs_6_.refs_5_.refs_4_.refs_3_.refs_2_.refs_1_.refs_0_), channel_id=1, source_target_pairs={{0,8},{1,9},{2,6},{3,7},{4,0},{5,1},{6,14},{7,15},{8,16},{9,17},{1... | collective-permute-start | bytes 1572872 | tf_op jit(solution)/shard_map/ppermute | solution.py:332
  76.1 10.1 %collective-permute-start.12 = (f32[2,4,128,128]{3,2,1,0:T(8,128)}, f32[2,4,128,128]{3,2,1,0:T(8,128)S(1)}, u32[]{:S(2)}, u32[]{:S(2)}) collective-permute-start(f32[2,4,128,128]{3,2,1,0:T(8,128)} %shard_map.145), channel_id=1, source_target_pairs={{0,1},{1,0},{2,3},{3,2},{4,5},{5,4},{6,7},{7,6},{8,9},{9,8},{10,11... | collective-permute-start | bytes 1572872 | tf_op jit(solution)/shard_map/ppermute | solution.py:332
  80.9 8.3 %collective-permute-start.11 = (f32[2,4,128,128]{3,2,1,0:T(8,128)S(1)}, f32[2,4,128,128]{3,2,1,0:T(8,128)S(1)}, u32[]{:S(2)}, u32[]{:S(2)}) collective-permute-start(f32[2,4,128,128]{3,2,1,0:T(8,128)S(1)} %collective-permute-done.10.refs_7_.refs_6_.refs_5_.refs_4_.refs_3_.refs_2_.refs_1_), channel_id=1, source_target_pairs={{0,8},{1,9},{2,6},{3,7},{4,0},{5,1},{6,14},{7,15},{8,16},{9,17},{1... | collective-permute-start | bytes 1572872 | tf_op jit(solution)/shard_map/ppermute | solution.py:332
  84.2 22.5 %copy-start.33 = (f32[2,4,128,128]{3,2,1,0:T(8,128)S(1)}, f32[2,4,128,128]{3,2,1,0:T(8,128)}, u32[]{:S(2)}) copy-start(f32[2,4,128,128]{3,2,1,0:T(8,128)} %shard_map.146) | copy-start | bytes 1572868
  84.2 18.9 %collective-permute-start.14 = (f32[2,4,128,128]{3,2,1,0:T(8,128)}, f32[2,4,128,128]{3,2,1,0:T(8,128)}, u32[]{:S(2)}, u32[]{:S(2)}) collective-permute-start(f32[2,4,128,128]{3,2,1,0:T(8,128)} %shard_map.146), channel_id=1, source_target_pairs={{0,1},{1,0},{2,3},{3,2},{4,5},{5,4},{6,7},{7,6},{8,9},{9,8},{10,11... | collective-permute-start | bytes 1572872 | tf_op jit(solution)/shard_map/ppermute | solution.py:332
  90.2 12.9 %collective-permute-start.15 = (f32[2,4,128,128]{3,2,1,0:T(8,128)}, f32[2,4,128,128]{3,2,1,0:T(8,128)}, u32[]{:S(2)}, u32[]{:S(2)}) collective-permute-start(f32[2,4,128,128]{3,2,1,0:T(8,128)} %get-tuple-element.135), channel_id=1, source_target_pairs={{0,2},{1,3},{2,0},{3,1},{4,6},{5,7},{6,4},{7,5},{8,10},{9,11},{10,... | collective-permute-start | bytes 1572872 | tf_op jit(solution)/shard_map/ppermute | solution.py:332
  98.3 8.3 %collective-permute-start.13 = (f32[2,4,128,128]{3,2,1,0:T(8,128)S(1)}, f32[2,4,128,128]{3,2,1,0:T(8,128)S(1)}, u32[]{:S(2)}, u32[]{:S(2)}) collective-permute-start(f32[2,4,128,128]{3,2,1,0:T(8,128)S(1)} %collective-permute-done.11.refs_7_.refs_6_.refs_5_.refs_4_.refs_3_.refs_2_), channel_id=1, source_target_pairs={{0,8},{1,9},{2,6},{3,7},{4,0},{5,1},{6,14},{7,15},{8,16},{9,17},{1... | collective-permute-start | bytes 1572872 | tf_op jit(solution)/shard_map/ppermute | solution.py:332
  101.8 12.9 %collective-permute-start.17 = (f32[2,4,128,128]{3,2,1,0:T(8,128)}, f32[2,4,128,128]{3,2,1,0:T(8,128)S(1)}, u32[]{:S(2)}, u32[]{:S(2)}) collective-permute-start(f32[2,4,128,128]{3,2,1,0:T(8,128)} %shard_map.147), channel_id=1, source_target_pairs={{0,1},{1,0},{2,3},{3,2},{4,5},{5,4},{6,7},{7,6},{8,9},{9,8},{10,11... | collective-permute-start | bytes 1572872 | tf_op jit(solution)/shard_map/ppermute | solution.py:332
  109.0 5.8 %collective-permute-start.18 = (f32[2,4,128,128]{3,2,1,0:T(8,128)}, f32[2,4,128,128]{3,2,1,0:T(8,128)}, u32[]{:S(2)}, u32[]{:S(2)}) collective-permute-start(f32[2,4,128,128]{3,2,1,0:T(8,128)} %get-tuple-element.137), channel_id=1, source_target_pairs={{0,2},{1,3},{2,0},{3,1},{4,6},{5,7},{6,4},{7,5},{8,10},{9,11},{10,... | collective-permute-start | bytes 1572872 | tf_op jit(solution)/shard_map/ppermute | solution.py:332
  109.9 8.4 %collective-permute-start.16 = (f32[2,4,128,128]{3,2,1,0:T(8,128)S(1)}, f32[2,4,128,128]{3,2,1,0:T(8,128)S(1)}, u32[]{:S(2)}, u32[]{:S(2)}) collective-permute-start(f32[2,4,128,128]{3,2,1,0:T(8,128)S(1)} %collective-permute-done.13.refs_7_.refs_6_.refs_5_.refs_4_.refs_3_), channel_id=1, source_target_pairs={{0,8},{1,9},{2,6},{3,7},{4,0},{5,1},{6,14},{7,15},{8,16},{9,17},{1... | collective-permute-start | bytes 1572872 | tf_op jit(solution)/shard_map/ppermute | solution.py:332
  113.3 13.1 %collective-permute-start.20 = (f32[2,4,128,128]{3,2,1,0:T(8,128)}, f32[2,4,128,128]{3,2,1,0:T(8,128)}, u32[]{:S(2)}, u32[]{:S(2)}) collective-permute-start(f32[2,4,128,128]{3,2,1,0:T(8,128)} %shard_map.148), channel_id=1, source_target_pairs={{0,1},{1,0},{2,3},{3,2},{4,5},{5,4},{6,7},{7,6},{8,9},{9,8},{10,11... | collective-permute-start | bytes 1572872 | tf_op jit(solution)/shard_map/ppermute | solution.py:332
  119.5 6.9 %collective-permute-start.21 = (f32[2,4,128,128]{3,2,1,0:T(8,128)}, f32[2,4,128,128]{3,2,1,0:T(8,128)}, u32[]{:S(2)}, u32[]{:S(2)}) collective-permute-start(f32[2,4,128,128]{3,2,1,0:T(8,128)} %get-tuple-element.139), channel_id=1, source_target_pairs={{0,2},{1,3},{2,0},{3,1},{4,6},{5,7},{6,4},{7,5},{8,10},{9,11},{10,... | collective-permute-start | bytes 1572872 | tf_op jit(solution)/shard_map/ppermute | solution.py:332
  120.2 8.3 %collective-permute-start.19 = (f32[2,4,128,128]{3,2,1,0:T(8,128)S(1)}, f32[2,4,128,128]{3,2,1,0:T(8,128)S(1)}, u32[]{:S(2)}, u32[]{:S(2)}) collective-permute-start(f32[2,4,128,128]{3,2,1,0:T(8,128)S(1)} %collective-permute-done.16.refs_7_.refs_6_.refs_5_.refs_4_), channel_id=1, source_target_pairs={{0,8},{1,9},{2,6},{3,7},{4,0},{5,1},{6,14},{7,15},{8,16},{9,17},{1... | collective-permute-start | bytes 1572872 | tf_op jit(solution)/shard_map/ppermute | solution.py:332
  123.7 14.3 %collective-permute-start.23 = (f32[2,4,128,128]{3,2,1,0:T(8,128)}, f32[2,4,128,128]{3,2,1,0:T(8,128)S(1)}, u32[]{:S(2)}, u32[]{:S(2)}) collective-permute-start(f32[2,4,128,128]{3,2,1,0:T(8,128)} %shard_map.149), channel_id=1, source_target_pairs={{0,1},{1,0},{2,3},{3,2},{4,5},{5,4},{6,7},{7,6},{8,9},{9,8},{10,11... | collective-permute-start | bytes 1572872 | tf_op jit(solution)/shard_map/ppermute | solution.py:332
  130.9 7.1 %collective-permute-start.24 = (f32[2,4,128,128]{3,2,1,0:T(8,128)}, f32[2,4,128,128]{3,2,1,0:T(8,128)}, u32[]{:S(2)}, u32[]{:S(2)}) collective-permute-start(f32[2,4,128,128]{3,2,1,0:T(8,128)} %get-tuple-element.132), channel_id=1, source_target_pairs={{0,2},{1,3},{2,0},{3,1},{4,6},{5,7},{6,4},{7,5},{8,10},{9,11},{10,... | collective-permute-start | bytes 1572872 | tf_op jit(solution)/shard_map/ppermute | solution.py:332
  131.8 8.4 %collective-permute-start.22 = (f32[2,4,128,128]{3,2,1,0:T(8,128)S(1)}, f32[2,4,128,128]{3,2,1,0:T(8,128)S(1)}, u32[]{:S(2)}, u32[]{:S(2)}) collective-permute-start(f32[2,4,128,128]{3,2,1,0:T(8,128)S(1)} %collective-permute-done.19.refs_7_.refs_6_.refs_5_), channel_id=1, source_target_pairs={{0,8},{1,9},{2,6},{3,7},{4,0},{5,1},{6,14},{7,15},{8,16},{9,17},{1... | collective-permute-start | bytes 1572872 | tf_op jit(solution)/shard_map/ppermute | solution.py:332
  135.2 14.2 %collective-permute-start.26 = (f32[2,4,128,128]{3,2,1,0:T(8,128)}, f32[2,4,128,128]{3,2,1,0:T(8,128)}, u32[]{:S(2)}, u32[]{:S(2)}) collective-permute-start(f32[2,4,128,128]{3,2,1,0:T(8,128)} %shard_map.151), channel_id=1, source_target_pairs={{0,1},{1,0},{2,3},{3,2},{4,5},{5,4},{6,7},{7,6},{8,9},{9,8},{10,11... | collective-permute-start | bytes 1572872 | tf_op jit(solution)/shard_map/ppermute | solution.py:332
  142.3 7.1 %collective-permute-start.27 = (f32[2,4,128,128]{3,2,1,0:T(8,128)}, f32[2,4,128,128]{3,2,1,0:T(8,128)}, u32[]{:S(2)}, u32[]{:S(2)}) collective-permute-start(f32[2,4,128,128]{3,2,1,0:T(8,128)} %get-tuple-element.131), channel_id=1, source_target_pairs={{0,2},{1,3},{2,0},{3,1},{4,6},{5,7},{6,4},{7,5},{8,10},{9,11},{10,... | collective-permute-start | bytes 1572872 | tf_op jit(solution)/shard_map/ppermute | solution.py:332
  143.1 8.4 %collective-permute-start.25 = (f32[2,4,128,128]{3,2,1,0:T(8,128)S(1)}, f32[2,4,128,128]{3,2,1,0:T(8,128)}, u32[]{:S(2)}, u32[]{:S(2)}) collective-permute-start(f32[2,4,128,128]{3,2,1,0:T(8,128)S(1)} %collective-permute-done.22.refs_7_.refs_6_), channel_id=1, source_target_pairs={{0,8},{1,9},{2,6},{3,7},{4,0},{5,1},{6,14},{7,15},{8,16},{9,17},{1... | collective-permute-start | bytes 1572872 | tf_op jit(solution)/shard_map/ppermute | solution.py:332
  146.6 13.9 %collective-permute-start.28 = (f32[2,4,128,128]{3,2,1,0:T(8,128)}, f32[2,4,128,128]{3,2,1,0:T(8,128)}, u32[]{:S(2)}, u32[]{:S(2)}) collective-permute-start(f32[2,4,128,128]{3,2,1,0:T(8,128)} %shard_map.152), channel_id=1, source_target_pairs={{0,1},{1,0},{2,3},{3,2},{4,5},{5,4},{6,7},{7,6},{8,9},{9,8},{10,11... | collective-permute-start | bytes 1572872 | tf_op jit(solution)/shard_map/ppermute | solution.py:332
  153.5 7.1 %collective-permute-start.29 = (f32[2,4,128,128]{3,2,1,0:T(8,128)}, f32[2,4,128,128]{3,2,1,0:T(8,128)}, u32[]{:S(2)}, u32[]{:S(2)}) collective-permute-start(f32[2,4,128,128]{3,2,1,0:T(8,128)} %get-tuple-element.128), channel_id=1, source_target_pairs={{0,2},{1,3},{2,0},{3,1},{4,6},{5,7},{6,4},{7,5},{8,10},{9,11},{10,... | collective-permute-start | bytes 1572872 | tf_op jit(solution)/shard_map/ppermute | solution.py:332
  156.9 18.7 %collective-permute-start.30 = (f32[2,4,128,128]{3,2,1,0:T(8,128)}, f32[2,4,128,128]{3,2,1,0:T(8,128)S(1)}, u32[]{:S(2)}, u32[]{:S(2)}) collective-permute-start(f32[2,4,128,128]{3,2,1,0:T(8,128)} %shard_map.154), channel_id=1, source_target_pairs={{0,1},{1,0},{2,3},{3,2},{4,5},{5,4},{6,7},{7,6},{8,9},{9,8},{10,11... | collective-permute-start | bytes 1572872 | tf_op jit(solution)/shard_map/ppermute | solution.py:332
  161.7 13.9 %collective-permute-start.31 = (f32[2,4,128,128]{3,2,1,0:T(8,128)S(1)}, f32[2,4,128,128]{3,2,1,0:T(8,128)S(1)}, u32[]{:S(2)}, u32[]{:S(2)}) collective-permute-start(f32[2,4,128,128]{3,2,1,0:T(8,128)S(1)} %get-tuple-element.127), channel_id=1, source_target_pairs={{0,2},{1,3},{2,0},{3,1},{4,6},{5,7},{6,4},{7,5},{8,10},{9,11},{10,... | collective-permute-start | bytes 1572872 | tf_op jit(solution)/shard_map/ppermute | solution.py:332
  175.5 11.2 %collective-permute-start.33 = (f32[2,64,32,128]{3,2,1,0:T(8,128)S(1)}, f32[2,64,32,128]{3,2,1,0:T(8,128)S(1)}, u32[]{:S(2)}, u32[]{:S(2)}) collective-permute-start(f32[2,64,32,128]{3,2,1,0:T(8,128)S(1)} %get-tuple-element.104), channel_id=1, source_target_pairs={{0,2},{1,3},{2,0},{3,1},{4,6},{5,7},{6,4},{7,5},{8,10},{9,11},{10,... | collective-permute-start | bytes 6291464 | tf_op jit(solution)/shard_map/ppermute | solution.py:332
  175.7 6.2 %collective-permute-start.32 = (f32[2,4,128,128]{3,2,1,0:T(8,128)S(1)}, f32[2,4,128,128]{3,2,1,0:T(8,128)S(1)}, u32[]{:S(2)}, u32[]{:S(2)}) collective-permute-start(f32[2,4,128,128]{3,2,1,0:T(8,128)S(1)} %get-tuple-element.124), channel_id=1, source_target_pairs={{0,2},{1,3},{2,0},{3,1},{4,6},{5,7},{6,4},{7,5},{8,10},{9,11},{10,... | collective-permute-start | bytes 1572872 | tf_op jit(solution)/shard_map/ppermute | solution.py:332
  181.7 5.0 %collective-permute-start.34 = (f32[2,64,16,128]{3,2,1,0:T(8,128)S(1)}, f32[2,64,16,128]{3,2,1,0:T(8,128)S(1)}, u32[]{:S(2)}, u32[]{:S(2)}) collective-permute-start(f32[2,64,16,128]{3,2,1,0:T(8,128)S(1)} %get-tuple-element.105), channel_id=1, source_target_pairs={{0,2},{1,3},{2,0},{3,1},{4,6},{5,7},{6,4},{7,5},{8,10},{9,11},{10,... | collective-permute-start | bytes 3145736 | tf_op jit(solution)/shard_map/ppermute | solution.py:332
  186.1 2.8 %collective-permute-start.35 = (f32[2,64,16,128]{3,2,1,0:T(8,128)S(1)}, f32[2,64,16,128]{3,2,1,0:T(8,128)S(1)}, u32[]{:S(2)}, u32[]{:S(2)}) collective-permute-start(f32[2,64,16,128]{3,2,1,0:T(8,128)S(1)} %get-tuple-element.106), channel_id=1, source_target_pairs={{0,2},{1,3},{2,0},{3,1},{4,6},{5,7},{6,4},{7,5},{8,10},{9,11},{10,... | collective-permute-start | bytes 3145736 | tf_op jit(solution)/shard_map/ppermute | solution.py:332
  199.7 4.2 %collective-permute-start.36 = (f32[2,64,32,128]{3,2,1,0:T(8,128)S(1)}, f32[2,64,32,128]{3,2,1,0:T(8,128)S(1)}, u32[]{:S(2)}, u32[]{:S(2)}) collective-permute-start(f32[2,64,32,128]{3,2,1,0:T(8,128)S(1)} %get-tuple-element.108), channel_id=1, source_target_pairs={{0,2},{1,3},{2,0},{3,1},{4,6},{5,7},{6,4},{7,5},{8,10},{9,11},{10,... | collective-permute-start | bytes 6291464 | tf_op jit(solution)/shard_map/ppermute | solution.py:332
  207.5 16.1 %collective-permute-start.37 = (f32[2,8,128,128]{3,2,1,0:T(8,128)S(1)}, f32[2,8,128,128]{3,2,1,0:T(8,128)S(1)}, u32[]{:S(2)}, u32[]{:S(2)}) collective-permute-start(f32[2,8,128,128]{3,2,1,0:T(8,128)S(1)} %shard_map.157), channel_id=1, source_target_pairs={{1,2},{2,1},{5,6},{6,5},{9,10},{10,9},{13,14},{14,13},{17,18},{18,... | collective-permute-start | bytes 3145736 | tf_op jit(solution)/shard_map/ppermute | solution.py:332
  210.9 12.7 %collective-permute-start.39 = (f32[2,64,16,128]{3,2,1,0:T(8,128)S(1)}, f32[2,64,16,128]{3,2,1,0:T(8,128)S(1)}, u32[]{:S(2)}, u32[]{:S(2)}) collective-permute-start(f32[2,64,16,128]{3,2,1,0:T(8,128)S(1)} %get-tuple-element.114), channel_id=1, source_target_pairs={{0,2},{1,3},{2,0},{3,1},{4,6},{5,7},{6,4},{7,5},{8,10},{9,11},{10,... | collective-permute-start | bytes 3145736 | tf_op jit(solution)/shard_map/ppermute | solution.py:332
  214.5 20.3 %collective-permute-start.38 = (f32[2,8,128,128]{3,2,1,0:T(8,128)S(1)}, f32[2,8,128,128]{3,2,1,0:T(8,128)S(1)}, u32[]{:S(2)}, u32[]{:S(2)}) collective-permute-start(f32[2,8,128,128]{3,2,1,0:T(8,128)S(1)} %shard_map.158), channel_id=1, source_target_pairs={{1,2},{2,1},{5,6},{6,5},{9,10},{10,9},{13,14},{14,13},{17,18},{18,... | collective-permute-start | bytes 3145736 | tf_op jit(solution)/shard_map/ppermute | solution.py:332
  216.7 18.1 %collective-permute-start.41 = (f32[2,64,16,128]{3,2,1,0:T(8,128)S(1)}, f32[2,64,16,128]{3,2,1,0:T(8,128)S(1)}, u32[]{:S(2)}, u32[]{:S(2)}) collective-permute-start(f32[2,64,16,128]{3,2,1,0:T(8,128)S(1)} %get-tuple-element.116), channel_id=1, source_target_pairs={{0,2},{1,3},{2,0},{3,1},{4,6},{5,7},{6,4},{7,5},{8,10},{9,11},{10,... | collective-permute-start | bytes 3145736 | tf_op jit(solution)/shard_map/ppermute | solution.py:332
  226.9 19.2 %collective-permute-start.40 = (f32[2,8,128,128]{3,2,1,0:T(8,128)S(1)}, f32[2,8,128,128]{3,2,1,0:T(8,128)S(1)}, u32[]{:S(2)}, u32[]{:S(2)}) collective-permute-start(f32[2,8,128,128]{3,2,1,0:T(8,128)S(1)} %shard_map.159), channel_id=1, source_target_pairs={{1,2},{2,1},{5,6},{6,5},{9,10},{10,9},{13,14},{14,13},{17,18},{18,... | collective-permute-start | bytes 3145736 | tf_op jit(solution)/shard_map/ppermute | solution.py:332
  238.1 19.2 %collective-permute-start.42 = (f32[2,8,128,128]{3,2,1,0:T(8,128)S(1)}, f32[2,8,128,128]{3,2,1,0:T(8,128)S(1)}, u32[]{:S(2)}, u32[]{:S(2)}) collective-permute-start(f32[2,8,128,128]{3,2,1,0:T(8,128)S(1)} %shard_map.160), channel_id=1, source_target_pairs={{1,2},{2,1},{5,6},{6,5},{9,10},{10,9},{13,14},{14,13},{17,18},{18,... | collective-permute-start | bytes 3145736 | tf_op jit(solution)/shard_map/ppermute | solution.py:332
  (34 other events, 301.1 us)

commit v4 on v3

--- a/solution.py
+++ b/solution.py
@@ -15,7 +15,7 @@
 ROWS = 8
 CHUNKS = 8
 UNITS = 2
-MIDDLE_ROWS = 16
+MIDDLE_ROWS = 32
 GROUPS = ((0, 4), (4, 6), (6, 8))
 TERM_GROUPS = ((0, 2), (2, 4), (4, 6), (6, 8))
 HOP_STEPS = 2

time: 261 us -> 260 us (level)
  starting transfers between devices: 61 us -> 64.9 us
  waiting for transfers between devices: 94.7 us -> 91.4 us
    ppermute x43, starting transfers between devices: 61 us -> 64.9 us  [move(): return lax.ppermute(value, axes, pairs)]
    ppermute x43, waiting for transfers between devices: 94.7 us -> 91.4 us  [move(): return lax.ppermute(value, axes, pairs)]
where the time goes in v4:
time: 260 us; the launch traced here: 259 us
  waiting for transfers between devices  91.4 us (35%)
  starting transfers between devices  64.9 us (25%)
  Pallas kernels  59.8 us (23%)
  other arithmetic  33.8 us (13%)
  local copies, waits for them, and re-layouts  6.96 us (3%)
    ppermute x43, waiting for transfers between devices, move(): return lax.ppermute(value, axes, pairs)  91.4 us
    ppermute x43, starting transfers between devices, move(): return lax.ppermute(value, axes, pairs)  64.9 us
    pallas_call x8, Pallas kernels, arrived(): pl.pallas_call(pick_body, in_specs=[pl.BlockSpec(memory_space=pltpu.SMEM)...  20.2 us
    pallas_call x3, Pallas kernels, paired(): call(forward_body, (hi - lo) // UNITS, [slab, pairs, pairs] + [whole(squa...  16.2 us
    pallas_call x4, Pallas kernels, paired(): call(backward_body, (hi - lo) // UNITS, [some_lines, some_lines, some_pai...  13.7 us
    pallas_call x1, Pallas kernels, paired(): call(middle_body, half // MIDDLE_ROWS, cols * 2 + [chosen(square)] * 4, c...  9.66 us
    another operation x8, other arithmetic, paired(): own = [jnp.stack(owns[lo:hi]) for lo, hi in GROUPS]  9.47 us
    select_n x1, other arithmetic, paired(): phi = jnp.where(home, chosen_orbital, values.pop())  5.29 us
  transfers between devices with their start and end apart: 43, of which 27 were waited for; matrix products, arithmetic and copies ran while one was open for 13% of the time, Pallas kernels for 18%

profile of v4, /device:TPU:1, one launch (start us, length us, event | category | flops | bytes accessed | tf_op | source)
XLA Modules:
  0.0 259.0 jit_solution(64510269049409406)
XLA Ops:
  3.2 4.7 %dynamic-slice_bitcast_fusion = f32[64,128,128]{2,1,0:T(8,128)} fusion(f32[2,64,128,128]{3,2,1,0:T(8,128)} %param.15, s32[]{:T(128)S(6)} %select_n.264), kind=kLoop, calls=%fused_computation.1 | loop fusion | bytes 8388612 | tf_op jit(solution)/shard_map/jit(dynamic_index_in_dim)/squeeze | solution.py:371
  8.3 3.1 %collective-permute-start.1 = (f32[2,4,128,128]{3,2,1,0:T(8,128)S(1)}, f32[2,4,128,128]{3,2,1,0:T(8,128)S(1)}, u32[]{:S(2)}, u32[]{:S(2)}) collective-permute-start(f32[2,4,128,128]{3,2,1,0:T(8,128)S(1)} %select_bitcast_fusion.8.refs_0_), channel_id=1, source_target_pairs={{0,8},{1,9},{2,6},{3,7},{4,0},{5,1},{6,14},{7,15},{8,16},{9,17},{1... | collective-permute-start | bytes 1572872 | tf_op jit(solution)/shard_map/ppermute | solution.py:332
  11.4 3.5 %collective-permute-start.8 = (f32[64,128,128]{2,1,0:T(8,128)}, f32[64,128,128]{2,1,0:T(8,128)}, u32[]{:S(2)}, u32[]{:S(2)}) collective-permute-start(f32[64,128,128]{2,1,0:T(8,128)} %dynamic-slice_bitcast_fusion), channel_id=1, source_target_pairs={{1,2},{2,1},{5,6},{6,5},{9,10},{10,9},{13,14},{14,13},{17,18},{18,... | collective-permute-start | bytes 12582920 | tf_op jit(solution)/shard_map/ppermute | solution.py:332
  15.6 2.7 %collective-permute-done.1 = f32[2,4,128,128]{3,2,1,0:T(8,128)S(1)} collective-permute-done((f32[2,4,128,128]{3,2,1,0:T(8,128)S(1)}, f32[2,4,128,128]{3,2,1,0:T(8,128)S(1)}, u32[]{:S(2)}, u32[]{:S(2)}) %collective-permute-start.1) | collective-permute-done | bytes 524320 | tf_op jit(solution)/shard_map/ppermute | solution.py:332
  21.1 3.7 %fusion.2 = (f32[2,4,128,128]{3,2,1,0:T(8,128)S(1)}, f32[2,4,128,128]{3,2,1,0:T(8,128)}, f32[2,4,128,128]{3,2,1,0:T(8,128)S(1)}, f32[2,4,128,128]{3,2,1,0:T(8,128)S(1)}, f32[2,4,128,128]{3,2,1,0:T(8,128)S(1)}) fusion(f32[2,2,32,128,128]{4,3,2,1,0:T(8,128)} %bitcast.7, s32[]{:T(128)S(6)} %select_n.263, pred[]{:T(512)S(6)} %eq.26, ...), kind=kLoop, calls=%fused_computation.13 | loop fusion | flops 655360 | bytes 7864325 | tf_op jit(solution)/shard_map/jit(_where)/select_n | solution.py:380
  24.8 3.2 %collective-permute-done.3 = f32[2,4,128,128]{3,2,1,0:T(8,128)S(1)} collective-permute-done((f32[2,4,128,128]{3,2,1,0:T(8,128)S(1)}, f32[2,4,128,128]{3,2,1,0:T(8,128)S(1)}, u32[]{:S(2)}, u32[]{:S(2)}) %collective-permute-start.3) | collective-permute-done | bytes 524320 | tf_op jit(solution)/shard_map/ppermute | solution.py:332
  30.8 6.9 %collective-permute-done.4 = f32[2,4,128,128]{3,2,1,0:T(8,128)S(1)} collective-permute-done((f32[2,4,128,128]{3,2,1,0:T(8,128)S(1)}, f32[2,4,128,128]{3,2,1,0:T(8,128)S(1)}, u32[]{:S(2)}, u32[]{:S(2)}) %collective-permute-start.4) | collective-permute-done | bytes 524320 | tf_op jit(solution)/shard_map/ppermute | solution.py:332
  39.3 6.9 %collective-permute-done.5 = f32[2,4,128,128]{3,2,1,0:T(8,128)S(1)} collective-permute-done((f32[2,4,128,128]{3,2,1,0:T(8,128)S(1)}, f32[2,4,128,128]{3,2,1,0:T(8,128)S(1)}, u32[]{:S(2)}, u32[]{:S(2)}) %collective-permute-start.5) | collective-permute-done | bytes 524320 | tf_op jit(solution)/shard_map/ppermute | solution.py:332
  47.7 6.9 %collective-permute-done.6 = f32[2,4,128,128]{3,2,1,0:T(8,128)S(1)} collective-permute-done((f32[2,4,128,128]{3,2,1,0:T(8,128)S(1)}, f32[2,4,128,128]{3,2,1,0:T(8,128)S(1)}, u32[]{:S(2)}, u32[]{:S(2)}) %collective-permute-start.6) | collective-permute-done | bytes 524320 | tf_op jit(solution)/shard_map/ppermute | solution.py:332
  56.2 5.3 %collective-permute-done.8 = f32[64,128,128]{2,1,0:T(8,128)} collective-permute-done((f32[64,128,128]{2,1,0:T(8,128)}, f32[64,128,128]{2,1,0:T(8,128)}, u32[]{:S(2)}, u32[]{:S(2)}) %collective-permute-start.8) | collective-permute-done | bytes 4194336 | tf_op jit(solution)/shard_map/ppermute | solution.py:332
  65.8 5.3 %broadcast_select_fusion = f32[64,128,128]{2,1,0:T(8,128)} fusion(f32[64,128,128]{2,1,0:T(8,128)} %dynamic-slice_bitcast_fusion, f32[64,128,128]{2,1,0:T(8,128)} %collective-permute-done.8, pred[]{:T(512)S(6)} %eq.25), kind=kLoop, calls=%fused_computation.4 | loop fusion | flops 1048576 | bytes 12582913 | tf_op jit(solution)/shard_map/jit(_where)/select_n | solution.py:423
  73.9 2.5 shard_map.145
  78.6 2.3 collective-permute-done.10.refs_7_.refs_6_.refs_5_.refs_4_.refs_3_.refs_2_.refs_1_
  82.0 2.5 shard_map.146
  84.5 2.1 collective-permute-start.14
  86.6 2.6 collective-permute-done.11.refs_7_.refs_6_.refs_5_.refs_4_.refs_3_.refs_2_
  90.2 7.8 %collective-permute-start.15 = (f32[2,4,128,128]{3,2,1,0:T(8,128)}, f32[2,4,128,128]{3,2,1,0:T(8,128)}, u32[]{:S(2)}, u32[]{:S(2)}) collective-permute-start(f32[2,4,128,128]{3,2,1,0:T(8,128)} %get-tuple-element.135), channel_id=1, source_target_pairs={{0,2},{1,3},{2,0},{3,1},{4,6},{5,7},{6,4},{7,5},{8,10},{9,11},{10,... | collective-permute-start | bytes 1572872 | tf_op jit(solution)/shard_map/ppermute | solution.py:332
  99.7 2.5 shard_map.147
  103.6 3.1 %collective-permute-done.13.refs_7_.refs_6_.refs_5_.refs_4_.refs_3_ = f32[2,4,128,128]{3,2,1,0:T(8,128)S(1)} collective-permute-done((f32[2,4,128,128]{3,2,1,0:T(8,128)S(1)}, f32[2,4,128,128]{3,2,1,0:T(8,128)S(1)}, u32[]{:S(2)}, u32[]{:S(2)}) %collective-permute-start.13) | collective-permute-done | bytes 524320 | tf_op jit(solution)/shard_map/ppermute | solution.py:332
  106.6 2.3 select_bitcast_fusion.6
  111.2 2.5 shard_map.148
  115.7 2.5 collective-permute-done.16.refs_7_.refs_6_.refs_5_.refs_4_
  121.6 2.5 shard_map.149
  128.6 2.3 broadcast_select_fusion.9
  133.1 2.5 shard_map.151
  140.2 2.1 select_bitcast_fusion.3
  144.5 2.5 shard_map.152
  154.4 2.5 shard_map.154
  158.3 3.2 %collective-permute-done.28 = f32[2,4,128,128]{3,2,1,0:T(8,128)} collective-permute-done((f32[2,4,128,128]{3,2,1,0:T(8,128)}, f32[2,4,128,128]{3,2,1,0:T(8,128)}, u32[]{:S(2)}, u32[]{:S(2)}) %collective-permute-start.28) | collective-permute-done | bytes 524320 | tf_op jit(solution)/shard_map/ppermute | solution.py:332
  167.4 8.0 %shard_map.150 = (f32[2,64,32,128]{3,2,1,0:T(8,128)S(1)}, f32[2,64,32,128]{3,2,1,0:T(8,128)S(1)}) custom-call(s32[2]{0:T(128)S(1)} %copy-done.13, f32[2,32,128,128]{3,2,1,0:T(8,128)S(1)} %bitcast.97, f32[4,2,4,128,128]{4,3,2,1,0:T(8,128)S(1)} %pad_maximum_fusion.1.own, f32[4,2,4,128,128]{4,3,2,1,0:T(8,128)S(1)} %pad_maximum_fusion.2.other, ...), custom_call_target="tpu_custom_call" | custom-call | tf_op jit(solution)/shard_map/pallas_call | solution.py:464
  177.6 4.1 %shard_map.153 = (f32[2,64,16,128]{3,2,1,0:T(8,128)S(1)}, f32[2,64,16,128]{3,2,1,0:T(8,128)S(1)}) custom-call(s32[2]{0:T(128)S(1)} %copy-done.13, f32[2,32,128,128]{3,2,1,0:T(8,128)S(1)} %bitcast.98, f32[2,2,4,128,128]{4,3,2,1,0:T(8,128)S(1)} %pad_maximum_fusion.3.own, f32[2,2,4,128,128]{4,3,2,1,0:T(8,128)S(1)} %pad_maximum_fusion.4.other, ...), custom_call_target="tpu_custom_call" | custom-call | tf_op jit(solution)/shard_map/pallas_call | solution.py:464
  182.0 4.1 %shard_map.155 = (f32[2,64,16,128]{3,2,1,0:T(8,128)S(1)}, f32[2,64,16,128]{3,2,1,0:T(8,128)S(1)}) custom-call(s32[2]{0:T(128)S(1)} %copy-done.13, f32[2,32,128,128]{3,2,1,0:T(8,128)S(1)} %bitcast.99, f32[2,2,4,128,128]{4,3,2,1,0:T(8,128)S(1)} %pad_maximum_fusion.5.own, f32[2,2,4,128,128]{4,3,2,1,0:T(8,128)S(1)} %pad_maximum_fusion.6.other, ...), custom_call_target="tpu_custom_call" | custom-call | tf_op jit(solution)/shard_map/pallas_call | solution.py:464
  186.7 2.3 collective-permute-done.35.refs_5_
  189.0 9.7 %shard_map.156 = (f32[2,64,32,128]{3,2,1,0:T(8,128)S(1)}, f32[2,64,16,128]{3,2,1,0:T(8,128)S(1)}, f32[2,64,16,128]{3,2,1,0:T(8,128)S(1)}, f32[2,64,32,128]{3,2,1...) custom-call(s32[2]{0:T(128)S(1)} %copy-done.13, ...), custom_call_target="tpu_custom_call" | custom-call | tf_op jit(solution)/shard_map/pallas_call | solution.py:479
  199.1 3.8 %collective-permute-done.36.recv = f32[2,64,32,128]{3,2,1,0:T(8,128)S(1)} collective-permute-done((f32[2,64,32,128]{3,2,1,0:T(8,128)S(1)}, f32[2,64,32,128]{3,2,1,0:T(8,128)S(1)}, u32[]{:S(2)}, u32[]{:S(2)}) %collective-permute-start.36) | collective-permute-done | bytes 2097184 | tf_op jit(solution)/shard_map/ppermute | solution.py:332
  202.9 3.6 %shard_map.157 = f32[2,8,128,128]{3,2,1,0:T(8,128)S(1)} custom-call(s32[2]{0:T(128)S(1)} %copy-done.13, f32[2,64,32,128]{3,2,1,0:T(8,128)S(1)} %get-tuple-element.107.keep, f32[2,64,32,128]{3,2,1,0:T(8,128)S(1)} %collective-permute-done.36.recv, f32[4,2,4,128,128]{4,3,2,1,0:T(8,128)S(1)} %pad_maximum_fusion.1.own, ...), custom_call_target="tpu_custom_call" | custom-call | tf_op jit(solution)/shard_map/pallas_call | solution.py:503
  206.5 3.4 %collective-permute-start.37 = (f32[2,8,128,128]{3,2,1,0:T(8,128)S(1)}, f32[2,8,128,128]{3,2,1,0:T(8,128)S(1)}, u32[]{:S(2)}, u32[]{:S(2)}) collective-permute-start(f32[2,8,128,128]{3,2,1,0:T(8,128)S(1)} %shard_map.157), channel_id=1, source_target_pairs={{1,2},{2,1},{5,6},{6,5},{9,10},{10,9},{13,14},{14,13},{17,18},{18,... | collective-permute-start | bytes 3145736 | tf_op jit(solution)/shard_map/ppermute | solution.py:332
  210.0 3.5 %shard_map.158 = f32[2,8,128,128]{3,2,1,0:T(8,128)S(1)} custom-call(s32[2]{0:T(128)S(1)} %copy-done.13, f32[2,64,32,128]{3,2,1,0:T(8,128)S(1)} %get-tuple-element.107.keep, f32[2,64,32,128]{3,2,1,0:T(8,128)S(1)} %collective-permute-done.36.recv, f32[4,2,4,128,128]{4,3,2,1,0:T(8,128)S(1)} %pad_maximum_fusion.1.own, ...), custom_call_target="tpu_custom_call" | custom-call | tf_op jit(solution)/shard_map/pallas_call | solution.py:503
  213.5 2.4 collective-permute-start.38
  216.0 6.6 %collective-permute-done.37 = f32[2,8,128,128]{3,2,1,0:T(8,128)S(1)} collective-permute-done((f32[2,8,128,128]{3,2,1,0:T(8,128)S(1)}, f32[2,8,128,128]{3,2,1,0:T(8,128)S(1)}, u32[]{:S(2)}, u32[]{:S(2)}) %collective-permute-start.37) | collective-permute-done | bytes 1048608 | tf_op jit(solution)/shard_map/ppermute | solution.py:332
  222.6 3.3 %shard_map.159 = f32[2,8,128,128]{3,2,1,0:T(8,128)S(1)} custom-call(s32[2]{0:T(128)S(1)} %copy-done.13, f32[2,64,16,128]{3,2,1,0:T(8,128)S(1)} %get-tuple-element.113.keep, f32[2,64,16,128]{3,2,1,0:T(8,128)S(1)} %collective-permute-done.39.recv, f32[2,2,4,128,128]{4,3,2,1,0:T(8,128)S(1)} %pad_maximum_fusion.3.own, ...), custom_call_target="tpu_custom_call" | custom-call | tf_op jit(solution)/shard_map/pallas_call | solution.py:503
  225.9 3.4 %collective-permute-start.40 = (f32[2,8,128,128]{3,2,1,0:T(8,128)S(1)}, f32[2,8,128,128]{3,2,1,0:T(8,128)S(1)}, u32[]{:S(2)}, u32[]{:S(2)}) collective-permute-start(f32[2,8,128,128]{3,2,1,0:T(8,128)S(1)} %shard_map.159), channel_id=1, source_target_pairs={{1,2},{2,1},{5,6},{6,5},{9,10},{10,9},{13,14},{14,13},{17,18},{18,... | collective-permute-start | bytes 3145736 | tf_op jit(solution)/shard_map/ppermute | solution.py:332
  229.3 4.6 %collective-permute-done.38 = f32[2,8,128,128]{3,2,1,0:T(8,128)S(1)} collective-permute-done((f32[2,8,128,128]{3,2,1,0:T(8,128)S(1)}, f32[2,8,128,128]{3,2,1,0:T(8,128)S(1)}, u32[]{:S(2)}, u32[]{:S(2)}) %collective-permute-start.38) | collective-permute-done | bytes 1048608 | tf_op jit(solution)/shard_map/ppermute | solution.py:332
  233.9 3.3 %shard_map.160 = f32[2,8,128,128]{3,2,1,0:T(8,128)S(1)} custom-call(s32[2]{0:T(128)S(1)} %copy-done.13, f32[2,64,16,128]{3,2,1,0:T(8,128)S(1)} %get-tuple-element.115.keep, f32[2,64,16,128]{3,2,1,0:T(8,128)S(1)} %collective-permute-done.41.recv, f32[2,2,4,128,128]{4,3,2,1,0:T(8,128)S(1)} %pad_maximum_fusion.5.own, ...), custom_call_target="tpu_custom_call" | custom-call | tf_op jit(solution)/shard_map/pallas_call | solution.py:503
  237.1 3.4 %collective-permute-start.42 = (f32[2,8,128,128]{3,2,1,0:T(8,128)S(1)}, f32[2,8,128,128]{3,2,1,0:T(8,128)S(1)}, u32[]{:S(2)}, u32[]{:S(2)}) collective-permute-start(f32[2,8,128,128]{3,2,1,0:T(8,128)S(1)} %shard_map.160), channel_id=1, source_target_pairs={{1,2},{2,1},{5,6},{6,5},{9,10},{10,9},{13,14},{14,13},{17,18},{18,... | collective-permute-start | bytes 3145736 | tf_op jit(solution)/shard_map/ppermute | solution.py:332
  240.8 4.3 %collective-permute-done.40 = f32[2,8,128,128]{3,2,1,0:T(8,128)S(1)} collective-permute-done((f32[2,8,128,128]{3,2,1,0:T(8,128)S(1)}, f32[2,8,128,128]{3,2,1,0:T(8,128)S(1)}, u32[]{:S(2)}, u32[]{:S(2)}) %collective-permute-start.40) | collective-permute-done | bytes 1048608 | tf_op jit(solution)/shard_map/ppermute | solution.py:332
  245.2 11.1 %collective-permute-done.42 = f32[2,8,128,128]{3,2,1,0:T(8,128)S(1)} collective-permute-done((f32[2,8,128,128]{3,2,1,0:T(8,128)S(1)}, f32[2,8,128,128]{3,2,1,0:T(8,128)S(1)}, u32[]{:S(2)}, u32[]{:S(2)}) %collective-permute-start.42) | collective-permute-done | bytes 1048608 | tf_op jit(solution)/shard_map/ppermute | solution.py:332
  256.4 2.5 pad_maximum_fusion
  (164 shorter events, 66.8 us)
Async XLA Ops:
  1.3 17.0 %collective-permute-start.2 = (f32[2,64,128,128]{3,2,1,0:T(8,128)}, f32[2,64,128,128]{3,2,1,0:T(8,128)}, u32[]{:S(2)}, u32[]{:S(2)}) collective-permute-start(f32[2,64,128,128]{3,2,1,0:T(8,128)} %param.15), channel_id=1, source_target_pairs={{0,2},{1,3},{2,0},{3,1},{4,6},{5,7},{6,4},{7,5},{8,10},{9,11},{10,... | collective-permute-start | bytes 25165832 | tf_op jit(solution)/shard_map/ppermute | solution.py:332
  1.4 6.8 %collective-permute-start = (f32[2,1,4,128,128]{4,3,2,0,1:T(8,128)S(1)}, f32[2,1,4,128,128]{4,3,2,0,1:T(8,128)S(1)}, u32[]{:S(2)}, u32[]{:S(2)}) collective-permute-start(f32[2,1,4,128,128]{4,3,2,0,1:T(8,128)S(1)} %get-tuple-element.62), channel_id=1, source_target_pairs={{0,2},{1,3},{2,0},{3,1},{4,6},{5,7},{6,4},{7,5},{8,10},{9,11},{10,... | collective-permute-start | bytes 1572872 | tf_op jit(solution)/shard_map/ppermute | solution.py:332
  8.3 10.0 %collective-permute-start.1 = (f32[2,4,128,128]{3,2,1,0:T(8,128)S(1)}, f32[2,4,128,128]{3,2,1,0:T(8,128)S(1)}, u32[]{:S(2)}, u32[]{:S(2)}) collective-permute-start(f32[2,4,128,128]{3,2,1,0:T(8,128)S(1)} %select_bitcast_fusion.8.refs_0_), channel_id=1, source_target_pairs={{0,8},{1,9},{2,6},{3,7},{4,0},{5,1},{6,14},{7,15},{8,16},{9,17},{1... | collective-permute-start | bytes 1572872 | tf_op jit(solution)/shard_map/ppermute | solution.py:332
  11.4 50.1 %collective-permute-start.8 = (f32[64,128,128]{2,1,0:T(8,128)}, f32[64,128,128]{2,1,0:T(8,128)}, u32[]{:S(2)}, u32[]{:S(2)}) collective-permute-start(f32[64,128,128]{2,1,0:T(8,128)} %dynamic-slice_bitcast_fusion), channel_id=1, source_target_pairs={{1,2},{2,1},{5,6},{6,5},{9,10},{10,9},{13,14},{14,13},{17,18},{18,... | collective-permute-start | bytes 12582920 | tf_op jit(solution)/shard_map/ppermute | solution.py:332
  19.6 8.4 %collective-permute-start.3 = (f32[2,4,128,128]{3,2,1,0:T(8,128)S(1)}, f32[2,4,128,128]{3,2,1,0:T(8,128)S(1)}, u32[]{:S(2)}, u32[]{:S(2)}) collective-permute-start(f32[2,4,128,128]{3,2,1,0:T(8,128)S(1)} %fusion.8.refs_1_.refs_0_), channel_id=1, source_target_pairs={{0,8},{1,9},{2,6},{3,7},{4,0},{5,1},{6,14},{7,15},{8,16},{9,17},{1... | collective-permute-start | bytes 1572872 | tf_op jit(solution)/shard_map/ppermute | solution.py:332
  28.0 35.2 %copy-start.36 = (f32[2,4,128,128]{3,2,1,0:T(8,128)S(1)}, f32[2,4,128,128]{3,2,1,0:T(8,128)}, u32[]{:S(2)}) copy-start(f32[2,4,128,128]{3,2,1,0:T(8,128)} %get-tuple-element.69) | copy-start | bytes 1572868
  29.3 41.7 %copy-start.23 = (f32[2,4,128,128]{3,2,1,0:T(8,128)}, f32[2,4,128,128]{3,2,1,0:T(8,128)S(1)}, u32[]{:S(2)}) copy-start(f32[2,4,128,128]{3,2,1,0:T(8,128)S(1)} %fusion.1.refs_2_.refs_1_.refs_0_) | copy-start | bytes 1572868
  29.3 8.4 %collective-permute-start.4 = (f32[2,4,128,128]{3,2,1,0:T(8,128)S(1)}, f32[2,4,128,128]{3,2,1,0:T(8,128)S(1)}, u32[]{:S(2)}, u32[]{:S(2)}) collective-permute-start(f32[2,4,128,128]{3,2,1,0:T(8,128)S(1)} %fusion.1.refs_2_.refs_1_.refs_0_), channel_id=1, source_target_pairs={{0,8},{1,9},{2,6},{3,7},{4,0},{5,1},{6,14},{7,15},{8,16},{9,17},{1... | collective-permute-start | bytes 1572872 | tf_op jit(solution)/shard_map/ppermute | solution.py:332
  37.8 33.3 %copy-start.21 = (f32[2,4,128,128]{3,2,1,0:T(8,128)}, f32[2,4,128,128]{3,2,1,0:T(8,128)S(1)}, u32[]{:S(2)}) copy-start(f32[2,4,128,128]{3,2,1,0:T(8,128)S(1)} %broadcast_select_fusion.17.refs_3_.refs_2_.refs_1_.refs_0_) | copy-start | bytes 1572868
  37.8 8.4 %collective-permute-start.5 = (f32[2,4,128,128]{3,2,1,0:T(8,128)S(1)}, f32[2,4,128,128]{3,2,1,0:T(8,128)S(1)}, u32[]{:S(2)}, u32[]{:S(2)}) collective-permute-start(f32[2,4,128,128]{3,2,1,0:T(8,128)S(1)} %broadcast_select_fusion.17.refs_3_.refs_2_.refs_1_.refs_0_), channel_id=1, source_target_pairs={{0,8},{1,9},{2,6},{3,7},{4,0},{5,1},{6,14},{7,15},{8,16},{9,17},{1... | collective-permute-start | bytes 1572872 | tf_op jit(solution)/shard_map/ppermute | solution.py:332
  46.3 24.8 %copy-start.19 = (f32[2,4,128,128]{3,2,1,0:T(8,128)}, f32[2,4,128,128]{3,2,1,0:T(8,128)S(1)}, u32[]{:S(2)}) copy-start(f32[2,4,128,128]{3,2,1,0:T(8,128)S(1)} %broadcast_select_fusion.16.refs_4_.refs_3_.refs_2_.refs_1_.refs_0_) | copy-start | bytes 1572868
  46.3 8.4 %collective-permute-start.6 = (f32[2,4,128,128]{3,2,1,0:T(8,128)S(1)}, f32[2,4,128,128]{3,2,1,0:T(8,128)S(1)}, u32[]{:S(2)}, u32[]{:S(2)}) collective-permute-start(f32[2,4,128,128]{3,2,1,0:T(8,128)S(1)} %broadcast_select_fusion.16.refs_4_.refs_3_.refs_2_.refs_1_.refs_0_), channel_id=1, source_target_pairs={{0,8},{1,9},{2,6},{3,7},{4,0},{5,1},{6,14},{7,15},{8,16},{9,17},{1... | collective-permute-start | bytes 1572872 | tf_op jit(solution)/shard_map/ppermute | solution.py:332
  54.7 8.5 %collective-permute-start.7 = (f32[2,4,128,128]{3,2,1,0:T(8,128)S(1)}, f32[2,4,128,128]{3,2,1,0:T(8,128)}, u32[]{:S(2)}, u32[]{:S(2)}) collective-permute-start(f32[2,4,128,128]{3,2,1,0:T(8,128)S(1)} %broadcast_select_fusion.15.refs_5_.refs_4_.refs_3_.refs_2_.refs_1_.refs_0_), channel_id=1, source_target_pairs={{0,8},{1,9},{2,6},{3,7},{4,0},{5,1},{6,14},{7,15},{8,16},{9,17},{1... | collective-permute-start | bytes 1572872 | tf_op jit(solution)/shard_map/ppermute | solution.py:332
  64.3 8.4 %collective-permute-start.9 = (f32[2,4,128,128]{3,2,1,0:T(8,128)S(1)}, f32[2,4,128,128]{3,2,1,0:T(8,128)S(1)}, u32[]{:S(2)}, u32[]{:S(2)}) collective-permute-start(f32[2,4,128,128]{3,2,1,0:T(8,128)S(1)} %broadcast_select_fusion.14.refs_6_.refs_5_.refs_4_.refs_3_.refs_2_.refs_1_.refs_0_), channel_id=1, source_target_pairs={{0,8},{1,9},{2,6},{3,7},{4,0},{5,1},{6,14},{7,15},{8,16},{9,17},{1... | collective-permute-start | bytes 1572872 | tf_op jit(solution)/shard_map/ppermute | solution.py:332
  72.8 8.1 %collective-permute-start.10 = (f32[2,4,128,128]{3,2,1,0:T(8,128)S(1)}, f32[2,4,128,128]{3,2,1,0:T(8,128)S(1)}, u32[]{:S(2)}, u32[]{:S(2)}) collective-permute-start(f32[2,4,128,128]{3,2,1,0:T(8,128)S(1)} %broadcast_select_fusion.13.refs_7_.refs_6_.refs_5_.refs_4_.refs_3_.refs_2_.refs_1_.refs_0_), channel_id=1, source_target_pairs={{0,8},{1,9},{2,6},{3,7},{4,0},{5,1},{6,14},{7,15},{8,16},{9,17},{1... | collective-permute-start | bytes 1572872 | tf_op jit(solution)/shard_map/ppermute | solution.py:332
  76.5 10.1 %collective-permute-start.12 = (f32[2,4,128,128]{3,2,1,0:T(8,128)}, f32[2,4,128,128]{3,2,1,0:T(8,128)S(1)}, u32[]{:S(2)}, u32[]{:S(2)}) collective-permute-start(f32[2,4,128,128]{3,2,1,0:T(8,128)} %shard_map.145), channel_id=1, source_target_pairs={{0,1},{1,0},{2,3},{3,2},{4,5},{5,4},{6,7},{7,6},{8,9},{9,8},{10,11... | collective-permute-start | bytes 1572872 | tf_op jit(solution)/shard_map/ppermute | solution.py:332
  80.9 8.3 %collective-permute-start.11 = (f32[2,4,128,128]{3,2,1,0:T(8,128)S(1)}, f32[2,4,128,128]{3,2,1,0:T(8,128)S(1)}, u32[]{:S(2)}, u32[]{:S(2)}) collective-permute-start(f32[2,4,128,128]{3,2,1,0:T(8,128)S(1)} %collective-permute-done.10.refs_7_.refs_6_.refs_5_.refs_4_.refs_3_.refs_2_.refs_1_), channel_id=1, source_target_pairs={{0,8},{1,9},{2,6},{3,7},{4,0},{5,1},{6,14},{7,15},{8,16},{9,17},{1... | collective-permute-start | bytes 1572872 | tf_op jit(solution)/shard_map/ppermute | solution.py:332
  84.5 22.1 %copy-start.33 = (f32[2,4,128,128]{3,2,1,0:T(8,128)S(1)}, f32[2,4,128,128]{3,2,1,0:T(8,128)}, u32[]{:S(2)}) copy-start(f32[2,4,128,128]{3,2,1,0:T(8,128)} %shard_map.146) | copy-start | bytes 1572868
  84.5 19.0 %collective-permute-start.14 = (f32[2,4,128,128]{3,2,1,0:T(8,128)}, f32[2,4,128,128]{3,2,1,0:T(8,128)}, u32[]{:S(2)}, u32[]{:S(2)}) collective-permute-start(f32[2,4,128,128]{3,2,1,0:T(8,128)} %shard_map.146), channel_id=1, source_target_pairs={{0,1},{1,0},{2,3},{3,2},{4,5},{5,4},{6,7},{7,6},{8,9},{9,8},{10,11... | collective-permute-start | bytes 1572872 | tf_op jit(solution)/shard_map/ppermute | solution.py:332
  90.2 13.4 %collective-permute-start.15 = (f32[2,4,128,128]{3,2,1,0:T(8,128)}, f32[2,4,128,128]{3,2,1,0:T(8,128)}, u32[]{:S(2)}, u32[]{:S(2)}) collective-permute-start(f32[2,4,128,128]{3,2,1,0:T(8,128)} %get-tuple-element.135), channel_id=1, source_target_pairs={{0,2},{1,3},{2,0},{3,1},{4,6},{5,7},{6,4},{7,5},{8,10},{9,11},{10,... | collective-permute-start | bytes 1572872 | tf_op jit(solution)/shard_map/ppermute | solution.py:332
  98.0 8.7 %collective-permute-start.13 = (f32[2,4,128,128]{3,2,1,0:T(8,128)S(1)}, f32[2,4,128,128]{3,2,1,0:T(8,128)S(1)}, u32[]{:S(2)}, u32[]{:S(2)}) collective-permute-start(f32[2,4,128,128]{3,2,1,0:T(8,128)S(1)} %collective-permute-done.11.refs_7_.refs_6_.refs_5_.refs_4_.refs_3_.refs_2_), channel_id=1, source_target_pairs={{0,8},{1,9},{2,6},{3,7},{4,0},{5,1},{6,14},{7,15},{8,16},{9,17},{1... | collective-permute-start | bytes 1572872 | tf_op jit(solution)/shard_map/ppermute | solution.py:332
  102.3 13.5 %collective-permute-start.17 = (f32[2,4,128,128]{3,2,1,0:T(8,128)}, f32[2,4,128,128]{3,2,1,0:T(8,128)S(1)}, u32[]{:S(2)}, u32[]{:S(2)}) collective-permute-start(f32[2,4,128,128]{3,2,1,0:T(8,128)} %shard_map.147), channel_id=1, source_target_pairs={{0,1},{1,0},{2,3},{3,2},{4,5},{5,4},{6,7},{7,6},{8,9},{9,8},{10,11... | collective-permute-start | bytes 1572872 | tf_op jit(solution)/shard_map/ppermute | solution.py:332
  109.0 6.7 %collective-permute-start.18 = (f32[2,4,128,128]{3,2,1,0:T(8,128)}, f32[2,4,128,128]{3,2,1,0:T(8,128)}, u32[]{:S(2)}, u32[]{:S(2)}) collective-permute-start(f32[2,4,128,128]{3,2,1,0:T(8,128)} %get-tuple-element.137), channel_id=1, source_target_pairs={{0,2},{1,3},{2,0},{3,1},{4,6},{5,7},{6,4},{7,5},{8,10},{9,11},{10,... | collective-permute-start | bytes 1572872 | tf_op jit(solution)/shard_map/ppermute | solution.py:332
  109.5 8.8 %collective-permute-start.16 = (f32[2,4,128,128]{3,2,1,0:T(8,128)S(1)}, f32[2,4,128,128]{3,2,1,0:T(8,128)S(1)}, u32[]{:S(2)}, u32[]{:S(2)}) collective-permute-start(f32[2,4,128,128]{3,2,1,0:T(8,128)S(1)} %collective-permute-done.13.refs_7_.refs_6_.refs_5_.refs_4_.refs_3_), channel_id=1, source_target_pairs={{0,8},{1,9},{2,6},{3,7},{4,0},{5,1},{6,14},{7,15},{8,16},{9,17},{1... | collective-permute-start | bytes 1572872 | tf_op jit(solution)/shard_map/ppermute | solution.py:332
  113.8 13.6 %collective-permute-start.20 = (f32[2,4,128,128]{3,2,1,0:T(8,128)}, f32[2,4,128,128]{3,2,1,0:T(8,128)}, u32[]{:S(2)}, u32[]{:S(2)}) collective-permute-start(f32[2,4,128,128]{3,2,1,0:T(8,128)} %shard_map.148), channel_id=1, source_target_pairs={{0,1},{1,0},{2,3},{3,2},{4,5},{5,4},{6,7},{7,6},{8,9},{9,8},{10,11... | collective-permute-start | bytes 1572872 | tf_op jit(solution)/shard_map/ppermute | solution.py:332
  119.5 7.9 %collective-permute-start.21 = (f32[2,4,128,128]{3,2,1,0:T(8,128)}, f32[2,4,128,128]{3,2,1,0:T(8,128)}, u32[]{:S(2)}, u32[]{:S(2)}) collective-permute-start(f32[2,4,128,128]{3,2,1,0:T(8,128)} %get-tuple-element.139), channel_id=1, source_target_pairs={{0,2},{1,3},{2,0},{3,1},{4,6},{5,7},{6,4},{7,5},{8,10},{9,11},{10,... | collective-permute-start | bytes 1572872 | tf_op jit(solution)/shard_map/ppermute | solution.py:332
  119.9 8.8 %collective-permute-start.19 = (f32[2,4,128,128]{3,2,1,0:T(8,128)S(1)}, f32[2,4,128,128]{3,2,1,0:T(8,128)S(1)}, u32[]{:S(2)}, u32[]{:S(2)}) collective-permute-start(f32[2,4,128,128]{3,2,1,0:T(8,128)S(1)} %collective-permute-done.16.refs_7_.refs_6_.refs_5_.refs_4_), channel_id=1, source_target_pairs={{0,8},{1,9},{2,6},{3,7},{4,0},{5,1},{6,14},{7,15},{8,16},{9,17},{1... | collective-permute-start | bytes 1572872 | tf_op jit(solution)/shard_map/ppermute | solution.py:332
  124.2 14.3 %collective-permute-start.23 = (f32[2,4,128,128]{3,2,1,0:T(8,128)}, f32[2,4,128,128]{3,2,1,0:T(8,128)S(1)}, u32[]{:S(2)}, u32[]{:S(2)}) collective-permute-start(f32[2,4,128,128]{3,2,1,0:T(8,128)} %shard_map.149), channel_id=1, source_target_pairs={{0,1},{1,0},{2,3},{3,2},{4,5},{5,4},{6,7},{7,6},{8,9},{9,8},{10,11... | collective-permute-start | bytes 1572872 | tf_op jit(solution)/shard_map/ppermute | solution.py:332
  131.0 7.5 %collective-permute-start.24 = (f32[2,4,128,128]{3,2,1,0:T(8,128)}, f32[2,4,128,128]{3,2,1,0:T(8,128)}, u32[]{:S(2)}, u32[]{:S(2)}) collective-permute-start(f32[2,4,128,128]{3,2,1,0:T(8,128)} %get-tuple-element.132), channel_id=1, source_target_pairs={{0,2},{1,3},{2,0},{3,1},{4,6},{5,7},{6,4},{7,5},{8,10},{9,11},{10,... | collective-permute-start | bytes 1572872 | tf_op jit(solution)/shard_map/ppermute | solution.py:332
  131.6 8.5 %collective-permute-start.22 = (f32[2,4,128,128]{3,2,1,0:T(8,128)S(1)}, f32[2,4,128,128]{3,2,1,0:T(8,128)S(1)}, u32[]{:S(2)}, u32[]{:S(2)}) collective-permute-start(f32[2,4,128,128]{3,2,1,0:T(8,128)S(1)} %collective-permute-done.19.refs_7_.refs_6_.refs_5_), channel_id=1, source_target_pairs={{0,8},{1,9},{2,6},{3,7},{4,0},{5,1},{6,14},{7,15},{8,16},{9,17},{1... | collective-permute-start | bytes 1572872 | tf_op jit(solution)/shard_map/ppermute | solution.py:332
  135.7 14.4 %collective-permute-start.26 = (f32[2,4,128,128]{3,2,1,0:T(8,128)}, f32[2,4,128,128]{3,2,1,0:T(8,128)}, u32[]{:S(2)}, u32[]{:S(2)}) collective-permute-start(f32[2,4,128,128]{3,2,1,0:T(8,128)} %shard_map.151), channel_id=1, source_target_pairs={{0,1},{1,0},{2,3},{3,2},{4,5},{5,4},{6,7},{7,6},{8,9},{9,8},{10,11... | collective-permute-start | bytes 1572872 | tf_op jit(solution)/shard_map/ppermute | solution.py:332
  142.3 7.7 %collective-permute-start.27 = (f32[2,4,128,128]{3,2,1,0:T(8,128)}, f32[2,4,128,128]{3,2,1,0:T(8,128)}, u32[]{:S(2)}, u32[]{:S(2)}) collective-permute-start(f32[2,4,128,128]{3,2,1,0:T(8,128)} %get-tuple-element.131), channel_id=1, source_target_pairs={{0,2},{1,3},{2,0},{3,1},{4,6},{5,7},{6,4},{7,5},{8,10},{9,11},{10,... | collective-permute-start | bytes 1572872 | tf_op jit(solution)/shard_map/ppermute | solution.py:332
  143.1 8.4 %collective-permute-start.25 = (f32[2,4,128,128]{3,2,1,0:T(8,128)S(1)}, f32[2,4,128,128]{3,2,1,0:T(8,128)}, u32[]{:S(2)}, u32[]{:S(2)}) collective-permute-start(f32[2,4,128,128]{3,2,1,0:T(8,128)S(1)} %collective-permute-done.22.refs_7_.refs_6_), channel_id=1, source_target_pairs={{0,8},{1,9},{2,6},{3,7},{4,0},{5,1},{6,14},{7,15},{8,16},{9,17},{1... | collective-permute-start | bytes 1572872 | tf_op jit(solution)/shard_map/ppermute | solution.py:332
  147.0 14.4 %collective-permute-start.28 = (f32[2,4,128,128]{3,2,1,0:T(8,128)}, f32[2,4,128,128]{3,2,1,0:T(8,128)}, u32[]{:S(2)}, u32[]{:S(2)}) collective-permute-start(f32[2,4,128,128]{3,2,1,0:T(8,128)} %shard_map.152), channel_id=1, source_target_pairs={{0,1},{1,0},{2,3},{3,2},{4,5},{5,4},{6,7},{7,6},{8,9},{9,8},{10,11... | collective-permute-start | bytes 1572872 | tf_op jit(solution)/shard_map/ppermute | solution.py:332
  153.5 7.9 %collective-permute-start.29 = (f32[2,4,128,128]{3,2,1,0:T(8,128)}, f32[2,4,128,128]{3,2,1,0:T(8,128)}, u32[]{:S(2)}, u32[]{:S(2)}) collective-permute-start(f32[2,4,128,128]{3,2,1,0:T(8,128)} %get-tuple-element.128), channel_id=1, source_target_pairs={{0,2},{1,3},{2,0},{3,1},{4,6},{5,7},{6,4},{7,5},{8,10},{9,11},{10,... | collective-permute-start | bytes 1572872 | tf_op jit(solution)/shard_map/ppermute | solution.py:332
  156.9 18.7 %collective-permute-start.30 = (f32[2,4,128,128]{3,2,1,0:T(8,128)}, f32[2,4,128,128]{3,2,1,0:T(8,128)S(1)}, u32[]{:S(2)}, u32[]{:S(2)}) collective-permute-start(f32[2,4,128,128]{3,2,1,0:T(8,128)} %shard_map.154), channel_id=1, source_target_pairs={{0,1},{1,0},{2,3},{3,2},{4,5},{5,4},{6,7},{7,6},{8,9},{9,8},{10,11... | collective-permute-start | bytes 1572872 | tf_op jit(solution)/shard_map/ppermute | solution.py:332
  162.6 13.0 %collective-permute-start.31 = (f32[2,4,128,128]{3,2,1,0:T(8,128)S(1)}, f32[2,4,128,128]{3,2,1,0:T(8,128)S(1)}, u32[]{:S(2)}, u32[]{:S(2)}) collective-permute-start(f32[2,4,128,128]{3,2,1,0:T(8,128)S(1)} %get-tuple-element.127), channel_id=1, source_target_pairs={{0,2},{1,3},{2,0},{3,1},{4,6},{5,7},{6,4},{7,5},{8,10},{9,11},{10,... | collective-permute-start | bytes 1572872 | tf_op jit(solution)/shard_map/ppermute | solution.py:332
  175.5 11.2 %collective-permute-start.33 = (f32[2,64,32,128]{3,2,1,0:T(8,128)S(1)}, f32[2,64,32,128]{3,2,1,0:T(8,128)S(1)}, u32[]{:S(2)}, u32[]{:S(2)}) collective-permute-start(f32[2,64,32,128]{3,2,1,0:T(8,128)S(1)} %get-tuple-element.104), channel_id=1, source_target_pairs={{0,2},{1,3},{2,0},{3,1},{4,6},{5,7},{6,4},{7,5},{8,10},{9,11},{10,... | collective-permute-start | bytes 6291464 | tf_op jit(solution)/shard_map/ppermute | solution.py:332
  175.7 6.2 %collective-permute-start.32 = (f32[2,4,128,128]{3,2,1,0:T(8,128)S(1)}, f32[2,4,128,128]{3,2,1,0:T(8,128)S(1)}, u32[]{:S(2)}, u32[]{:S(2)}) collective-permute-start(f32[2,4,128,128]{3,2,1,0:T(8,128)S(1)} %get-tuple-element.124), channel_id=1, source_target_pairs={{0,2},{1,3},{2,0},{3,1},{4,6},{5,7},{6,4},{7,5},{8,10},{9,11},{10,... | collective-permute-start | bytes 1572872 | tf_op jit(solution)/shard_map/ppermute | solution.py:332
  181.7 5.0 %collective-permute-start.34 = (f32[2,64,16,128]{3,2,1,0:T(8,128)S(1)}, f32[2,64,16,128]{3,2,1,0:T(8,128)S(1)}, u32[]{:S(2)}, u32[]{:S(2)}) collective-permute-start(f32[2,64,16,128]{3,2,1,0:T(8,128)S(1)} %get-tuple-element.105), channel_id=1, source_target_pairs={{0,2},{1,3},{2,0},{3,1},{4,6},{5,7},{6,4},{7,5},{8,10},{9,11},{10,... | collective-permute-start | bytes 3145736 | tf_op jit(solution)/shard_map/ppermute | solution.py:332
  186.1 2.8 %collective-permute-start.35 = (f32[2,64,16,128]{3,2,1,0:T(8,128)S(1)}, f32[2,64,16,128]{3,2,1,0:T(8,128)S(1)}, u32[]{:S(2)}, u32[]{:S(2)}) collective-permute-start(f32[2,64,16,128]{3,2,1,0:T(8,128)S(1)} %get-tuple-element.106), channel_id=1, source_target_pairs={{0,2},{1,3},{2,0},{3,1},{4,6},{5,7},{6,4},{7,5},{8,10},{9,11},{10,... | collective-permute-start | bytes 3145736 | tf_op jit(solution)/shard_map/ppermute | solution.py:332
  198.7 4.2 %collective-permute-start.36 = (f32[2,64,32,128]{3,2,1,0:T(8,128)S(1)}, f32[2,64,32,128]{3,2,1,0:T(8,128)S(1)}, u32[]{:S(2)}, u32[]{:S(2)}) collective-permute-start(f32[2,64,32,128]{3,2,1,0:T(8,128)S(1)} %get-tuple-element.108), channel_id=1, source_target_pairs={{0,2},{1,3},{2,0},{3,1},{4,6},{5,7},{6,4},{7,5},{8,10},{9,11},{10,... | collective-permute-start | bytes 6291464 | tf_op jit(solution)/shard_map/ppermute | solution.py:332
  206.5 16.1 %collective-permute-start.37 = (f32[2,8,128,128]{3,2,1,0:T(8,128)S(1)}, f32[2,8,128,128]{3,2,1,0:T(8,128)S(1)}, u32[]{:S(2)}, u32[]{:S(2)}) collective-permute-start(f32[2,8,128,128]{3,2,1,0:T(8,128)S(1)} %shard_map.157), channel_id=1, source_target_pairs={{1,2},{2,1},{5,6},{6,5},{9,10},{10,9},{13,14},{14,13},{17,18},{18,... | collective-permute-start | bytes 3145736 | tf_op jit(solution)/shard_map/ppermute | solution.py:332
  209.9 12.7 %collective-permute-start.39 = (f32[2,64,16,128]{3,2,1,0:T(8,128)S(1)}, f32[2,64,16,128]{3,2,1,0:T(8,128)S(1)}, u32[]{:S(2)}, u32[]{:S(2)}) collective-permute-start(f32[2,64,16,128]{3,2,1,0:T(8,128)S(1)} %get-tuple-element.114), channel_id=1, source_target_pairs={{0,2},{1,3},{2,0},{3,1},{4,6},{5,7},{6,4},{7,5},{8,10},{9,11},{10,... | collective-permute-start | bytes 3145736 | tf_op jit(solution)/shard_map/ppermute | solution.py:332
  213.5 20.3 %collective-permute-start.38 = (f32[2,8,128,128]{3,2,1,0:T(8,128)S(1)}, f32[2,8,128,128]{3,2,1,0:T(8,128)S(1)}, u32[]{:S(2)}, u32[]{:S(2)}) collective-permute-start(f32[2,8,128,128]{3,2,1,0:T(8,128)S(1)} %shard_map.158), channel_id=1, source_target_pairs={{1,2},{2,1},{5,6},{6,5},{9,10},{10,9},{13,14},{14,13},{17,18},{18,... | collective-permute-start | bytes 3145736 | tf_op jit(solution)/shard_map/ppermute | solution.py:332
  216.0 17.9 %collective-permute-start.41 = (f32[2,64,16,128]{3,2,1,0:T(8,128)S(1)}, f32[2,64,16,128]{3,2,1,0:T(8,128)S(1)}, u32[]{:S(2)}, u32[]{:S(2)}) collective-permute-start(f32[2,64,16,128]{3,2,1,0:T(8,128)S(1)} %get-tuple-element.116), channel_id=1, source_target_pairs={{0,2},{1,3},{2,0},{3,1},{4,6},{5,7},{6,4},{7,5},{8,10},{9,11},{10,... | collective-permute-start | bytes 3145736 | tf_op jit(solution)/shard_map/ppermute | solution.py:332
  225.9 19.2 %collective-permute-start.40 = (f32[2,8,128,128]{3,2,1,0:T(8,128)S(1)}, f32[2,8,128,128]{3,2,1,0:T(8,128)S(1)}, u32[]{:S(2)}, u32[]{:S(2)}) collective-permute-start(f32[2,8,128,128]{3,2,1,0:T(8,128)S(1)} %shard_map.159), channel_id=1, source_target_pairs={{1,2},{2,1},{5,6},{6,5},{9,10},{10,9},{13,14},{14,13},{17,18},{18,... | collective-permute-start | bytes 3145736 | tf_op jit(solution)/shard_map/ppermute | solution.py:332
  237.1 19.2 %collective-permute-start.42 = (f32[2,8,128,128]{3,2,1,0:T(8,128)S(1)}, f32[2,8,128,128]{3,2,1,0:T(8,128)S(1)}, u32[]{:S(2)}, u32[]{:S(2)}) collective-permute-start(f32[2,8,128,128]{3,2,1,0:T(8,128)S(1)} %shard_map.160), channel_id=1, source_target_pairs={{1,2},{2,1},{5,6},{6,5},{9,10},{10,9},{13,14},{14,13},{17,18},{18,... | collective-permute-start | bytes 3145736 | tf_op jit(solution)/shard_map/ppermute | solution.py:332
  (34 other events, 300.0 us)

commit v5 on v4

--- a/solution.py
+++ b/solution.py
@@ -183,20 +183,22 @@
     pltpu.make_async_copy(inputs[0], out, sem).wait()
 
 
-def forward_body(info, phi, own, other, wyh, wyl, wxh, wxl, keep, send):
+def forward_body(info, phi, *refs):
+    units = (len(refs) - 6) // 2
+    own, other = refs[:units], refs[units : 2 * units]
+    wyh, wyl, wxh, wxl, keep, send = refs[2 * units :]
     grid = phi.shape[-1]
     half = grid // 2
     part = phi.shape[1]
     rows = 2 * part
     core = info[0]
-    units = own.shape[0]
     part = part // units
     re, im = [], []
     for u in range(units):
         near = phi[core, u * part : (u + 1) * part]
         far = phi[1 - core, u * part : (u + 1) * part]
-        re += [near * own[u, 0], far * other[u, 0]]
-        im += [near * own[u, 1], far * other[u, 1]]
+        re += [near * own[u][0, 0], far * other[u][0, 0]]
+        im += [near * own[u][0, 1], far * other[u][0, 1]]
     re = jnp.concatenate(re, axis=0)
     im = jnp.concatenate(im, axis=0)
     data = jnp.concatenate([re, im], axis=-1).reshape(rows * grid, 2 * grid)
@@ -267,10 +269,12 @@
                     row += size
 
 
-def backward_body(info, keep, recv, own, other, wxh, wxl, wyh, wyl, out):
+def backward_body(info, keep, recv, *refs):
+    units = (len(refs) - 5) // 2
+    own, other = refs[:units], refs[units : 2 * units]
+    wxh, wxl, wyh, wyl, out = refs[2 * units :]
     grid = keep.shape[-1]
     rows = keep.shape[2]
-    units = own.shape[0]
     part = rows // 2 // units
     core = info[0]
     lines = []
@@ -294,8 +298,8 @@
         near = slice(2 * u * part, (2 * u + 1) * part)
         far = slice((2 * u + 1) * part, (2 * u + 2) * part)
         place = pl.ds(u * part, part)
-        out[core, place] = re[near] * own[u, 0] + im[near] * own[u, 1]
-        out[1 - core, place] = re[far] * other[u, 0] + im[far] * other[u, 1]
+        out[core, place] = re[near] * own[u][0, 0] + im[near] * own[u][0, 1]
+        out[1 - core, place] = re[far] * other[u][0, 0] + im[far] * other[u][0, 1]
 
 
 def call(body, grid_size, in_specs, out_specs, out_shape):
@@ -441,8 +445,14 @@
 
     planes = 2 * part
     phi = phi.reshape((2, half // 2, grid, grid))
-    own = [jnp.stack(owns[lo:hi]) for lo, hi in GROUPS]
-    other = [jnp.stack(others[lo:hi]) for lo, hi in GROUPS]
+
+    def by_unit(values, lo, hi):
+        if hi - lo == UNITS:
+            return [value[None] for value in values[lo:hi]]
+        return [jnp.stack(values[lo:hi])] * UNITS
+
+    own = [by_unit(owns, lo, hi) for lo, hi in GROUPS]
+    other = [by_unit(others, lo, hi) for lo, hi in GROUPS]
     table = tables(grid, part)
 
     def whole(shape):
@@ -453,7 +463,16 @@
 
     square = (2 * grid, 2 * grid)
 
-    pairs = pl.BlockSpec((UNITS,) + chunk_shape, lambda i, info: (i, 0, 0, 0, 0))
+
+    def unit_specs(shift):
+        return [
+            pl.BlockSpec(
+                (1,) + chunk_shape,
+                lambda i, info, u=u: ((shift + i) * UNITS + u if shift is not None else 0, 0, 0, 0, 0),
+            )
+            for u in range(UNITS)
+        ]
+
     lines = pl.BlockSpec((2, half, UNITS * planes, grid), lambda i, info: (0, 0, i, 0))
     keeps, sends = [], []
     for g, (lo, hi) in enumerate(GROUPS):
@@ -464,10 +483,10 @@
         keep, send = call(
             forward_body,
             (hi - lo) // UNITS,
-            [slab, pairs, pairs] + [whole(square)] * 2 + [chosen(square)] * 2,
+            [slab] + unit_specs(0 if hi - lo > UNITS else None) * 2 + [whole(square)] * 2 + [chosen(square)] * 2,
             [lines, lines],
             [spectrum, spectrum],
-        )(info, phi, own[g], other[g], *table["last_fwd"], *table["mid_fwd"])
+        )(info, phi, *own[g], *other[g], *table["last_fwd"], *table["mid_fwd"])
         keeps.append(keep)
         sends.append(send)
     recvs = [move(send, sibling) for send in sends]
@@ -497,18 +516,16 @@
         some_lines = pl.BlockSpec(
             (2, half, UNITS * planes, grid), lambda i, info, shift=shift: (0, 0, shift + i, 0)
         )
-        some_pairs = pl.BlockSpec(
-            (UNITS,) + chunk_shape, lambda i, info, shift=shift: (shift + i, 0, 0, 0, 0)
-        )
+        g_units = unit_specs(shift if GROUPS[g][1] - GROUPS[g][0] > UNITS else None)
         term = call(
             backward_body,
             (hi - lo) // UNITS,
-            [some_lines, some_lines, some_pairs, some_pairs]
+            [some_lines, some_lines] + g_units * 2
             + [chosen(square)] * 2
             + [whole(square)] * 2,
             pl.BlockSpec((2, UNITS * part, grid, grid), lambda i, info: (0, i, 0, 0)),
             jax.ShapeDtypeStruct((2, (hi - lo) * part, grid, grid), F32),
-        )(info, keep, recv, own[g], other[g], *table["mid_inv"], *table["last_inv"])
+        )(info, keep, recv, *own[g], *other[g], *table["mid_inv"], *table["last_inv"])
         terms.append((term, move(term, cross)))
     total = jnp.concatenate([jnp.where(home, *both) for both in terms], axis=1)
     return total.reshape((1, half, grid, grid))

time: 260 us -> 259 us (level)
    another operation x11 -> x5, other arithmetic: 12.8 us -> 8.1 us  [by_unit(): return [jnp.stack(values[lo:hi])] * UNITS]
    select_n x3 -> x5, other arithmetic: 4.35 us -> 7.45 us  [paired(): swapping.append((t + 1, move(jnp.where(home, got, mine), sibling)))]
where the time goes in v5:
time: 259 us; the launch traced here: 258 us
  waiting for transfers between devices  92.4 us (36%)
  starting transfers between devices  65.2 us (25%)
  Pallas kernels  59.7 us (23%)
  other arithmetic  32.2 us (12%)
  local copies, waits for them, and re-layouts  6.15 us (2%)
    ppermute x43, waiting for transfers between devices, move(): return lax.ppermute(value, axes, pairs)  92.4 us
    ppermute x43, starting transfers between devices, move(): return lax.ppermute(value, axes, pairs)  65.2 us
    pallas_call x8, Pallas kernels, arrived(): pl.pallas_call(pick_body, in_specs=[pl.BlockSpec(memory_space=pltpu.SMEM)...  20.2 us
    pallas_call x3, Pallas kernels, paired(): call(forward_body, (hi - lo) // UNITS, [slab] + unit_specs(0 if hi - lo >...  16.2 us
    pallas_call x4, Pallas kernels, paired(): call(backward_body, (hi - lo) // UNITS, [some_lines, some_lines] + g_unit...  13.6 us
    pallas_call x1, Pallas kernels, paired(): call(middle_body, half // MIDDLE_ROWS, cols * 2 + [chosen(square)] * 4, c...  9.67 us
    another operation x5, other arithmetic, by_unit(): return [jnp.stack(values[lo:hi])] * UNITS  8.1 us
    select_n x5, other arithmetic, paired(): swapping.append((t + 1, move(jnp.where(home, got, mine), sibling)))  7.45 us
  transfers between devices with their start and end apart: 43, of which 27 were waited for; matrix products, arithmetic and copies ran while one was open for 13% of the time, Pallas kernels for 18%

profile of v5, /device:TPU:1, one launch (start us, length us, event | category | flops | bytes accessed | tf_op | source)
XLA Modules:
  0.0 257.7 jit_solution(4243876904047532680)
XLA Ops:
  3.2 4.7 %dynamic-slice_bitcast_fusion = f32[64,128,128]{2,1,0:T(8,128)} fusion(f32[2,64,128,128]{3,2,1,0:T(8,128)} %param.15, s32[]{:T(128)S(6)} %select_n.264), kind=kLoop, calls=%fused_computation.1 | loop fusion | bytes 8388612 | tf_op jit(solution)/shard_map/jit(dynamic_index_in_dim)/squeeze | solution.py:375
  8.3 3.1 %collective-permute-start.1 = (f32[2,4,128,128]{3,2,1,0:T(8,128)S(1)}, f32[2,4,128,128]{3,2,1,0:T(8,128)S(1)}, u32[]{:S(2)}, u32[]{:S(2)}) collective-permute-start(f32[2,4,128,128]{3,2,1,0:T(8,128)S(1)} %select_bitcast_fusion.8.refs_0_), channel_id=1, source_target_pairs={{0,8},{1,9},{2,6},{3,7},{4,0},{5,1},{6,14},{7,15},{8,16},{9,17},{1... | collective-permute-start | bytes 1572872 | tf_op jit(solution)/shard_map/ppermute | solution.py:336
  11.4 3.5 %collective-permute-start.8 = (f32[64,128,128]{2,1,0:T(8,128)}, f32[64,128,128]{2,1,0:T(8,128)}, u32[]{:S(2)}, u32[]{:S(2)}) collective-permute-start(f32[64,128,128]{2,1,0:T(8,128)} %dynamic-slice_bitcast_fusion), channel_id=1, source_target_pairs={{1,2},{2,1},{5,6},{6,5},{9,10},{10,9},{13,14},{14,13},{17,18},{18,... | collective-permute-start | bytes 12582920 | tf_op jit(solution)/shard_map/ppermute | solution.py:336
  15.6 2.7 %collective-permute-done.1 = f32[2,4,128,128]{3,2,1,0:T(8,128)S(1)} collective-permute-done((f32[2,4,128,128]{3,2,1,0:T(8,128)S(1)}, f32[2,4,128,128]{3,2,1,0:T(8,128)S(1)}, u32[]{:S(2)}, u32[]{:S(2)}) %collective-permute-start.1) | collective-permute-done | bytes 524320 | tf_op jit(solution)/shard_map/ppermute | solution.py:336
  21.1 3.7 %fusion.2 = (f32[2,4,128,128]{3,2,1,0:T(8,128)S(1)}, f32[2,4,128,128]{3,2,1,0:T(8,128)}, f32[2,4,128,128]{3,2,1,0:T(8,128)S(1)}, f32[2,4,128,128]{3,2,1,0:T(8,128)S(1)}, f32[2,4,128,128]{3,2,1,0:T(8,128)S(1)}) fusion(f32[2,2,32,128,128]{4,3,2,1,0:T(8,128)} %bitcast.7, s32[]{:T(128)S(6)} %select_n.263, pred[]{:T(512)S(6)} %eq.26, ...), kind=kLoop, calls=%fused_computation.9 | loop fusion | flops 655360 | bytes 7864325 | tf_op jit(solution)/shard_map/jit(_where)/select_n | solution.py:384
  24.8 3.2 %collective-permute-done.3 = f32[2,4,128,128]{3,2,1,0:T(8,128)S(1)} collective-permute-done((f32[2,4,128,128]{3,2,1,0:T(8,128)S(1)}, f32[2,4,128,128]{3,2,1,0:T(8,128)S(1)}, u32[]{:S(2)}, u32[]{:S(2)}) %collective-permute-start.3) | collective-permute-done | bytes 524320 | tf_op jit(solution)/shard_map/ppermute | solution.py:336
  30.8 6.9 %collective-permute-done.4 = f32[2,4,128,128]{3,2,1,0:T(8,128)S(1)} collective-permute-done((f32[2,4,128,128]{3,2,1,0:T(8,128)S(1)}, f32[2,4,128,128]{3,2,1,0:T(8,128)S(1)}, u32[]{:S(2)}, u32[]{:S(2)}) %collective-permute-start.4) | collective-permute-done | bytes 524320 | tf_op jit(solution)/shard_map/ppermute | solution.py:336
  39.3 6.9 %collective-permute-done.5 = f32[2,4,128,128]{3,2,1,0:T(8,128)S(1)} collective-permute-done((f32[2,4,128,128]{3,2,1,0:T(8,128)S(1)}, f32[2,4,128,128]{3,2,1,0:T(8,128)S(1)}, u32[]{:S(2)}, u32[]{:S(2)}) %collective-permute-start.5) | collective-permute-done | bytes 524320 | tf_op jit(solution)/shard_map/ppermute | solution.py:336
  47.7 6.9 %collective-permute-done.6 = f32[2,4,128,128]{3,2,1,0:T(8,128)S(1)} collective-permute-done((f32[2,4,128,128]{3,2,1,0:T(8,128)S(1)}, f32[2,4,128,128]{3,2,1,0:T(8,128)S(1)}, u32[]{:S(2)}, u32[]{:S(2)}) %collective-permute-start.6) | collective-permute-done | bytes 524320 | tf_op jit(solution)/shard_map/ppermute | solution.py:336
  56.2 5.3 %collective-permute-done.8 = f32[64,128,128]{2,1,0:T(8,128)} collective-permute-done((f32[64,128,128]{2,1,0:T(8,128)}, f32[64,128,128]{2,1,0:T(8,128)}, u32[]{:S(2)}, u32[]{:S(2)}) %collective-permute-start.8) | collective-permute-done | bytes 4194336 | tf_op jit(solution)/shard_map/ppermute | solution.py:336
  65.8 5.3 %broadcast_select_fusion = f32[64,128,128]{2,1,0:T(8,128)} fusion(f32[64,128,128]{2,1,0:T(8,128)} %dynamic-slice_bitcast_fusion, f32[64,128,128]{2,1,0:T(8,128)} %collective-permute-done.8, pred[]{:T(512)S(6)} %eq.25), kind=kLoop, calls=%fused_computation.4 | loop fusion | flops 1048576 | bytes 12582913 | tf_op jit(solution)/shard_map/jit(_where)/select_n | solution.py:427
  73.9 2.5 shard_map.145
  78.6 2.3 collective-permute-done.10.refs_7_.refs_6_.refs_5_.refs_4_.refs_3_.refs_2_.refs_1_
  82.0 2.5 shard_map.146
  84.5 2.1 collective-permute-start.14
  86.6 2.6 collective-permute-done.11.refs_7_.refs_6_.refs_5_.refs_4_.refs_3_.refs_2_
  90.2 7.8 %collective-permute-start.15 = (f32[2,4,128,128]{3,2,1,0:T(8,128)}, f32[2,4,128,128]{3,2,1,0:T(8,128)}, u32[]{:S(2)}, u32[]{:S(2)}) collective-permute-start(f32[2,4,128,128]{3,2,1,0:T(8,128)} %get-tuple-element.135), channel_id=1, source_target_pairs={{0,2},{1,3},{2,0},{3,1},{4,6},{5,7},{6,4},{7,5},{8,10},{9,11},{10,... | collective-permute-start | bytes 1572872 | tf_op jit(solution)/shard_map/ppermute | solution.py:336
  99.7 2.5 shard_map.147
  103.5 3.1 %collective-permute-done.13.refs_7_.refs_6_.refs_5_.refs_4_.refs_3_ = f32[2,4,128,128]{3,2,1,0:T(8,128)S(1)} collective-permute-done((f32[2,4,128,128]{3,2,1,0:T(8,128)S(1)}, f32[2,4,128,128]{3,2,1,0:T(8,128)S(1)}, u32[]{:S(2)}, u32[]{:S(2)}) %collective-permute-start.13) | collective-permute-done | bytes 524320 | tf_op jit(solution)/shard_map/ppermute | solution.py:336
  106.6 2.4 select_bitcast_fusion.6
  111.3 2.6 shard_map.148
  115.7 2.6 %collective-permute-done.16.refs_7_.refs_6_.refs_5_.refs_4_ = f32[2,4,128,128]{3,2,1,0:T(8,128)S(1)} collective-permute-done((f32[2,4,128,128]{3,2,1,0:T(8,128)S(1)}, f32[2,4,128,128]{3,2,1,0:T(8,128)S(1)}, u32[]{:S(2)}, u32[]{:S(2)}) %collective-permute-start.16) | collective-permute-done | bytes 524320 | tf_op jit(solution)/shard_map/ppermute | solution.py:336
  121.7 2.5 shard_map.149
  128.7 2.2 broadcast_select_fusion.9
  133.1 2.5 shard_map.151
  140.2 2.1 broadcast_select_fusion.8
  144.4 2.5 shard_map.152
  154.3 2.5 shard_map.154
  158.2 3.1 %collective-permute-done.28 = f32[2,4,128,128]{3,2,1,0:T(8,128)} collective-permute-done((f32[2,4,128,128]{3,2,1,0:T(8,128)}, f32[2,4,128,128]{3,2,1,0:T(8,128)}, u32[]{:S(2)}, u32[]{:S(2)}) %collective-permute-start.28) | collective-permute-done | bytes 524320 | tf_op jit(solution)/shard_map/ppermute | solution.py:336
  167.8 8.0 %shard_map.150 = (f32[2,64,32,128]{3,2,1,0:T(8,128)S(1)}, f32[2,64,32,128]{3,2,1,0:T(8,128)S(1)}) custom-call(s32[2]{0:T(128)S(1)} %copy-done.13, f32[2,32,128,128]{3,2,1,0:T(8,128)S(1)} %bitcast.97, f32[4,2,4,128,128]{4,3,2,1,0:T(8,128)S(1)} %pad_maximum_fusion.1.refs_0_.refs_1_, f32[4,2,4,128,128]{4,3,2,1,0:T(8,128)S(1)} %pad_maximum_fusion.1.refs_0_.refs_1_, ...), custom_call_target="tpu_custom_call" | custom-call | tf_op jit(solution)/shard_map/pallas_call | solution.py:483
  176.6 4.1 %shard_map.153 = (f32[2,64,16,128]{3,2,1,0:T(8,128)S(1)}, f32[2,64,16,128]{3,2,1,0:T(8,128)S(1)}) custom-call(s32[2]{0:T(128)S(1)} %copy-done.13, f32[2,32,128,128]{3,2,1,0:T(8,128)S(1)} %bitcast.98, f32[1,2,4,128,128]{4,3,2,1,0:T(8,128)S(1)} %get-tuple-element.131.refs_0_, f32[1,2,4,128,128]{4,3,2,1,0:T(8,128)S(1)} %get-tuple-element.129.refs_1_, ...), custom_call_target="tpu_custom_call" | custom-call | tf_op jit(solution)/shard_map/pallas_call | solution.py:483
  180.8 4.1 %shard_map.155 = (f32[2,64,16,128]{3,2,1,0:T(8,128)S(1)}, f32[2,64,16,128]{3,2,1,0:T(8,128)S(1)}) custom-call(s32[2]{0:T(128)S(1)} %copy-done.13, f32[2,32,128,128]{3,2,1,0:T(8,128)S(1)} %bitcast.99, f32[1,2,4,128,128]{4,3,2,1,0:T(8,128)S(1)} %get-tuple-element.127.refs_0_, f32[1,2,4,128,128]{4,3,2,1,0:T(8,128)S(1)} %get-tuple-element.125.refs_1_, ...), custom_call_target="tpu_custom_call" | custom-call | tf_op jit(solution)/shard_map/pallas_call | solution.py:483
  185.5 2.3 collective-permute-done.35.refs_5_
  187.8 9.7 %shard_map.156 = (f32[2,64,32,128]{3,2,1,0:T(8,128)S(1)}, f32[2,64,16,128]{3,2,1,0:T(8,128)S(1)}, f32[2,64,16,128]{3,2,1,0:T(8,128)S(1)}, f32[2,64,32,128]{3,2,1...) custom-call(s32[2]{0:T(128)S(1)} %copy-done.13, ...), custom_call_target="tpu_custom_call" | custom-call | tf_op jit(solution)/shard_map/pallas_call | solution.py:498
  197.9 3.8 %collective-permute-done.36.recv = f32[2,64,32,128]{3,2,1,0:T(8,128)S(1)} collective-permute-done((f32[2,64,32,128]{3,2,1,0:T(8,128)S(1)}, f32[2,64,32,128]{3,2,1,0:T(8,128)S(1)}, u32[]{:S(2)}, u32[]{:S(2)}) %collective-permute-start.36) | collective-permute-done | bytes 2097184 | tf_op jit(solution)/shard_map/ppermute | solution.py:336
  201.7 3.6 %shard_map.157 = f32[2,8,128,128]{3,2,1,0:T(8,128)S(1)} custom-call(s32[2]{0:T(128)S(1)} %copy-done.13, f32[2,64,32,128]{3,2,1,0:T(8,128)S(1)} %get-tuple-element.107.keep, f32[2,64,32,128]{3,2,1,0:T(8,128)S(1)} %collective-permute-done.36.recv, f32[4,2,4,128,128]{4,3,2,1,0:T(8,128)S(1)} %pad_maximum_fusion.1.refs_0_.refs_1_, ...), custom_call_target="tpu_custom_call" | custom-call | tf_op jit(solution)/shard_map/pallas_call | solution.py:520
  205.3 3.4 %collective-permute-start.37 = (f32[2,8,128,128]{3,2,1,0:T(8,128)S(1)}, f32[2,8,128,128]{3,2,1,0:T(8,128)S(1)}, u32[]{:S(2)}, u32[]{:S(2)}) collective-permute-start(f32[2,8,128,128]{3,2,1,0:T(8,128)S(1)} %shard_map.157), channel_id=1, source_target_pairs={{1,2},{2,1},{5,6},{6,5},{9,10},{10,9},{13,14},{14,13},{17,18},{18,... | collective-permute-start | bytes 3145736 | tf_op jit(solution)/shard_map/ppermute | solution.py:336
  208.8 3.5 %shard_map.158 = f32[2,8,128,128]{3,2,1,0:T(8,128)S(1)} custom-call(s32[2]{0:T(128)S(1)} %copy-done.13, f32[2,64,32,128]{3,2,1,0:T(8,128)S(1)} %get-tuple-element.107.keep, f32[2,64,32,128]{3,2,1,0:T(8,128)S(1)} %collective-permute-done.36.recv, f32[4,2,4,128,128]{4,3,2,1,0:T(8,128)S(1)} %pad_maximum_fusion.1.refs_0_.refs_1_, ...), custom_call_target="tpu_custom_call" | custom-call | tf_op jit(solution)/shard_map/pallas_call | solution.py:520
  212.3 2.4 collective-permute-start.38
  214.8 6.6 %collective-permute-done.37 = f32[2,8,128,128]{3,2,1,0:T(8,128)S(1)} collective-permute-done((f32[2,8,128,128]{3,2,1,0:T(8,128)S(1)}, f32[2,8,128,128]{3,2,1,0:T(8,128)S(1)}, u32[]{:S(2)}, u32[]{:S(2)}) %collective-permute-start.37) | collective-permute-done | bytes 1048608 | tf_op jit(solution)/shard_map/ppermute | solution.py:336
  221.4 3.2 %shard_map.159 = f32[2,8,128,128]{3,2,1,0:T(8,128)S(1)} custom-call(s32[2]{0:T(128)S(1)} %copy-done.13, f32[2,64,16,128]{3,2,1,0:T(8,128)S(1)} %get-tuple-element.113.keep, f32[2,64,16,128]{3,2,1,0:T(8,128)S(1)} %collective-permute-done.39.recv, f32[1,2,4,128,128]{4,3,2,1,0:T(8,128)S(1)} %get-tuple-element.131.refs_0_, ...), custom_call_target="tpu_custom_call" | custom-call | tf_op jit(solution)/shard_map/pallas_call | solution.py:520
  224.7 3.4 %collective-permute-start.40 = (f32[2,8,128,128]{3,2,1,0:T(8,128)S(1)}, f32[2,8,128,128]{3,2,1,0:T(8,128)S(1)}, u32[]{:S(2)}, u32[]{:S(2)}) collective-permute-start(f32[2,8,128,128]{3,2,1,0:T(8,128)S(1)} %shard_map.159), channel_id=1, source_target_pairs={{1,2},{2,1},{5,6},{6,5},{9,10},{10,9},{13,14},{14,13},{17,18},{18,... | collective-permute-start | bytes 3145736 | tf_op jit(solution)/shard_map/ppermute | solution.py:336
  228.0 4.6 %collective-permute-done.38 = f32[2,8,128,128]{3,2,1,0:T(8,128)S(1)} collective-permute-done((f32[2,8,128,128]{3,2,1,0:T(8,128)S(1)}, f32[2,8,128,128]{3,2,1,0:T(8,128)S(1)}, u32[]{:S(2)}, u32[]{:S(2)}) %collective-permute-start.38) | collective-permute-done | bytes 1048608 | tf_op jit(solution)/shard_map/ppermute | solution.py:336
  232.6 3.3 %shard_map.160 = f32[2,8,128,128]{3,2,1,0:T(8,128)S(1)} custom-call(s32[2]{0:T(128)S(1)} %copy-done.13, f32[2,64,16,128]{3,2,1,0:T(8,128)S(1)} %get-tuple-element.115.keep, f32[2,64,16,128]{3,2,1,0:T(8,128)S(1)} %collective-permute-done.41.recv, f32[1,2,4,128,128]{4,3,2,1,0:T(8,128)S(1)} %get-tuple-element.127.refs_0_, ...), custom_call_target="tpu_custom_call" | custom-call | tf_op jit(solution)/shard_map/pallas_call | solution.py:520
  235.9 3.4 %collective-permute-start.42 = (f32[2,8,128,128]{3,2,1,0:T(8,128)S(1)}, f32[2,8,128,128]{3,2,1,0:T(8,128)S(1)}, u32[]{:S(2)}, u32[]{:S(2)}) collective-permute-start(f32[2,8,128,128]{3,2,1,0:T(8,128)S(1)} %shard_map.160), channel_id=1, source_target_pairs={{1,2},{2,1},{5,6},{6,5},{9,10},{10,9},{13,14},{14,13},{17,18},{18,... | collective-permute-start | bytes 3145736 | tf_op jit(solution)/shard_map/ppermute | solution.py:336
  239.6 4.3 %collective-permute-done.40 = f32[2,8,128,128]{3,2,1,0:T(8,128)S(1)} collective-permute-done((f32[2,8,128,128]{3,2,1,0:T(8,128)S(1)}, f32[2,8,128,128]{3,2,1,0:T(8,128)S(1)}, u32[]{:S(2)}, u32[]{:S(2)}) %collective-permute-start.40) | collective-permute-done | bytes 1048608 | tf_op jit(solution)/shard_map/ppermute | solution.py:336
  244.0 11.1 %collective-permute-done.42 = f32[2,8,128,128]{3,2,1,0:T(8,128)S(1)} collective-permute-done((f32[2,8,128,128]{3,2,1,0:T(8,128)S(1)}, f32[2,8,128,128]{3,2,1,0:T(8,128)S(1)}, u32[]{:S(2)}, u32[]{:S(2)}) %collective-permute-start.42) | collective-permute-done | bytes 1048608 | tf_op jit(solution)/shard_map/ppermute | solution.py:336
  255.2 2.5 pad_maximum_fusion
  (160 shorter events, 65.6 us)
Async XLA Ops:
  1.3 17.0 %collective-permute-start.2 = (f32[2,64,128,128]{3,2,1,0:T(8,128)}, f32[2,64,128,128]{3,2,1,0:T(8,128)}, u32[]{:S(2)}, u32[]{:S(2)}) collective-permute-start(f32[2,64,128,128]{3,2,1,0:T(8,128)} %param.15), channel_id=1, source_target_pairs={{0,2},{1,3},{2,0},{3,1},{4,6},{5,7},{6,4},{7,5},{8,10},{9,11},{10,... | collective-permute-start | bytes 25165832 | tf_op jit(solution)/shard_map/ppermute | solution.py:336
  1.4 6.8 %collective-permute-start = (f32[2,1,4,128,128]{4,3,2,0,1:T(8,128)S(1)}, f32[2,1,4,128,128]{4,3,2,0,1:T(8,128)S(1)}, u32[]{:S(2)}, u32[]{:S(2)}) collective-permute-start(f32[2,1,4,128,128]{4,3,2,0,1:T(8,128)S(1)} %get-tuple-element.62), channel_id=1, source_target_pairs={{0,2},{1,3},{2,0},{3,1},{4,6},{5,7},{6,4},{7,5},{8,10},{9,11},{10,... | collective-permute-start | bytes 1572872 | tf_op jit(solution)/shard_map/ppermute | solution.py:336
  8.3 10.0 %collective-permute-start.1 = (f32[2,4,128,128]{3,2,1,0:T(8,128)S(1)}, f32[2,4,128,128]{3,2,1,0:T(8,128)S(1)}, u32[]{:S(2)}, u32[]{:S(2)}) collective-permute-start(f32[2,4,128,128]{3,2,1,0:T(8,128)S(1)} %select_bitcast_fusion.8.refs_0_), channel_id=1, source_target_pairs={{0,8},{1,9},{2,6},{3,7},{4,0},{5,1},{6,14},{7,15},{8,16},{9,17},{1... | collective-permute-start | bytes 1572872 | tf_op jit(solution)/shard_map/ppermute | solution.py:336
  11.4 50.1 %collective-permute-start.8 = (f32[64,128,128]{2,1,0:T(8,128)}, f32[64,128,128]{2,1,0:T(8,128)}, u32[]{:S(2)}, u32[]{:S(2)}) collective-permute-start(f32[64,128,128]{2,1,0:T(8,128)} %dynamic-slice_bitcast_fusion), channel_id=1, source_target_pairs={{1,2},{2,1},{5,6},{6,5},{9,10},{10,9},{13,14},{14,13},{17,18},{18,... | collective-permute-start | bytes 12582920 | tf_op jit(solution)/shard_map/ppermute | solution.py:336
  19.6 8.4 %collective-permute-start.3 = (f32[2,4,128,128]{3,2,1,0:T(8,128)S(1)}, f32[2,4,128,128]{3,2,1,0:T(8,128)S(1)}, u32[]{:S(2)}, u32[]{:S(2)}) collective-permute-start(f32[2,4,128,128]{3,2,1,0:T(8,128)S(1)} %fusion.8.refs_1_.refs_0_), channel_id=1, source_target_pairs={{0,8},{1,9},{2,6},{3,7},{4,0},{5,1},{6,14},{7,15},{8,16},{9,17},{1... | collective-permute-start | bytes 1572872 | tf_op jit(solution)/shard_map/ppermute | solution.py:336
  28.0 35.2 %copy-start.36 = (f32[2,4,128,128]{3,2,1,0:T(8,128)S(1)}, f32[2,4,128,128]{3,2,1,0:T(8,128)}, u32[]{:S(2)}) copy-start(f32[2,4,128,128]{3,2,1,0:T(8,128)} %get-tuple-element.69) | copy-start | bytes 1572868
  29.3 41.7 %copy-start.23 = (f32[2,4,128,128]{3,2,1,0:T(8,128)}, f32[2,4,128,128]{3,2,1,0:T(8,128)S(1)}, u32[]{:S(2)}) copy-start(f32[2,4,128,128]{3,2,1,0:T(8,128)S(1)} %fusion.1.refs_2_.refs_1_.refs_0_) | copy-start | bytes 1572868
  29.3 8.4 %collective-permute-start.4 = (f32[2,4,128,128]{3,2,1,0:T(8,128)S(1)}, f32[2,4,128,128]{3,2,1,0:T(8,128)S(1)}, u32[]{:S(2)}, u32[]{:S(2)}) collective-permute-start(f32[2,4,128,128]{3,2,1,0:T(8,128)S(1)} %fusion.1.refs_2_.refs_1_.refs_0_), channel_id=1, source_target_pairs={{0,8},{1,9},{2,6},{3,7},{4,0},{5,1},{6,14},{7,15},{8,16},{9,17},{1... | collective-permute-start | bytes 1572872 | tf_op jit(solution)/shard_map/ppermute | solution.py:336
  37.8 33.3 %copy-start.21 = (f32[2,4,128,128]{3,2,1,0:T(8,128)}, f32[2,4,128,128]{3,2,1,0:T(8,128)S(1)}, u32[]{:S(2)}) copy-start(f32[2,4,128,128]{3,2,1,0:T(8,128)S(1)} %broadcast_select_fusion.17.refs_3_.refs_2_.refs_1_.refs_0_) | copy-start | bytes 1572868
  37.8 8.4 %collective-permute-start.5 = (f32[2,4,128,128]{3,2,1,0:T(8,128)S(1)}, f32[2,4,128,128]{3,2,1,0:T(8,128)S(1)}, u32[]{:S(2)}, u32[]{:S(2)}) collective-permute-start(f32[2,4,128,128]{3,2,1,0:T(8,128)S(1)} %broadcast_select_fusion.17.refs_3_.refs_2_.refs_1_.refs_0_), channel_id=1, source_target_pairs={{0,8},{1,9},{2,6},{3,7},{4,0},{5,1},{6,14},{7,15},{8,16},{9,17},{1... | collective-permute-start | bytes 1572872 | tf_op jit(solution)/shard_map/ppermute | solution.py:336
  46.3 24.8 %copy-start.19 = (f32[2,4,128,128]{3,2,1,0:T(8,128)}, f32[2,4,128,128]{3,2,1,0:T(8,128)S(1)}, u32[]{:S(2)}) copy-start(f32[2,4,128,128]{3,2,1,0:T(8,128)S(1)} %broadcast_select_fusion.16.refs_4_.refs_3_.refs_2_.refs_1_.refs_0_) | copy-start | bytes 1572868
  46.3 8.4 %collective-permute-start.6 = (f32[2,4,128,128]{3,2,1,0:T(8,128)S(1)}, f32[2,4,128,128]{3,2,1,0:T(8,128)S(1)}, u32[]{:S(2)}, u32[]{:S(2)}) collective-permute-start(f32[2,4,128,128]{3,2,1,0:T(8,128)S(1)} %broadcast_select_fusion.16.refs_4_.refs_3_.refs_2_.refs_1_.refs_0_), channel_id=1, source_target_pairs={{0,8},{1,9},{2,6},{3,7},{4,0},{5,1},{6,14},{7,15},{8,16},{9,17},{1... | collective-permute-start | bytes 1572872 | tf_op jit(solution)/shard_map/ppermute | solution.py:336
  54.7 8.5 %collective-permute-start.7 = (f32[2,4,128,128]{3,2,1,0:T(8,128)S(1)}, f32[2,4,128,128]{3,2,1,0:T(8,128)}, u32[]{:S(2)}, u32[]{:S(2)}) collective-permute-start(f32[2,4,128,128]{3,2,1,0:T(8,128)S(1)} %broadcast_select_fusion.15.refs_5_.refs_4_.refs_3_.refs_2_.refs_1_.refs_0_), channel_id=1, source_target_pairs={{0,8},{1,9},{2,6},{3,7},{4,0},{5,1},{6,14},{7,15},{8,16},{9,17},{1... | collective-permute-start | bytes 1572872 | tf_op jit(solution)/shard_map/ppermute | solution.py:336
  64.3 8.4 %collective-permute-start.9 = (f32[2,4,128,128]{3,2,1,0:T(8,128)S(1)}, f32[2,4,128,128]{3,2,1,0:T(8,128)S(1)}, u32[]{:S(2)}, u32[]{:S(2)}) collective-permute-start(f32[2,4,128,128]{3,2,1,0:T(8,128)S(1)} %broadcast_select_fusion.14.refs_6_.refs_5_.refs_4_.refs_3_.refs_2_.refs_1_.refs_0_), channel_id=1, source_target_pairs={{0,8},{1,9},{2,6},{3,7},{4,0},{5,1},{6,14},{7,15},{8,16},{9,17},{1... | collective-permute-start | bytes 1572872 | tf_op jit(solution)/shard_map/ppermute | solution.py:336
  72.8 8.1 %collective-permute-start.10 = (f32[2,4,128,128]{3,2,1,0:T(8,128)S(1)}, f32[2,4,128,128]{3,2,1,0:T(8,128)S(1)}, u32[]{:S(2)}, u32[]{:S(2)}) collective-permute-start(f32[2,4,128,128]{3,2,1,0:T(8,128)S(1)} %broadcast_select_fusion.13.refs_7_.refs_6_.refs_5_.refs_4_.refs_3_.refs_2_.refs_1_.refs_0_), channel_id=1, source_target_pairs={{0,8},{1,9},{2,6},{3,7},{4,0},{5,1},{6,14},{7,15},{8,16},{9,17},{1... | collective-permute-start | bytes 1572872 | tf_op jit(solution)/shard_map/ppermute | solution.py:336
  76.5 10.1 %collective-permute-start.12 = (f32[2,4,128,128]{3,2,1,0:T(8,128)}, f32[2,4,128,128]{3,2,1,0:T(8,128)S(1)}, u32[]{:S(2)}, u32[]{:S(2)}) collective-permute-start(f32[2,4,128,128]{3,2,1,0:T(8,128)} %shard_map.145), channel_id=1, source_target_pairs={{0,1},{1,0},{2,3},{3,2},{4,5},{5,4},{6,7},{7,6},{8,9},{9,8},{10,11... | collective-permute-start | bytes 1572872 | tf_op jit(solution)/shard_map/ppermute | solution.py:336
  80.9 8.3 %collective-permute-start.11 = (f32[2,4,128,128]{3,2,1,0:T(8,128)S(1)}, f32[2,4,128,128]{3,2,1,0:T(8,128)S(1)}, u32[]{:S(2)}, u32[]{:S(2)}) collective-permute-start(f32[2,4,128,128]{3,2,1,0:T(8,128)S(1)} %collective-permute-done.10.refs_7_.refs_6_.refs_5_.refs_4_.refs_3_.refs_2_.refs_1_), channel_id=1, source_target_pairs={{0,8},{1,9},{2,6},{3,7},{4,0},{5,1},{6,14},{7,15},{8,16},{9,17},{1... | collective-permute-start | bytes 1572872 | tf_op jit(solution)/shard_map/ppermute | solution.py:336
  84.5 22.1 %copy-start.33 = (f32[2,4,128,128]{3,2,1,0:T(8,128)S(1)}, f32[2,4,128,128]{3,2,1,0:T(8,128)}, u32[]{:S(2)}) copy-start(f32[2,4,128,128]{3,2,1,0:T(8,128)} %shard_map.146) | copy-start | bytes 1572868
  84.5 19.0 %collective-permute-start.14 = (f32[2,4,128,128]{3,2,1,0:T(8,128)}, f32[2,4,128,128]{3,2,1,0:T(8,128)}, u32[]{:S(2)}, u32[]{:S(2)}) collective-permute-start(f32[2,4,128,128]{3,2,1,0:T(8,128)} %shard_map.146), channel_id=1, source_target_pairs={{0,1},{1,0},{2,3},{3,2},{4,5},{5,4},{6,7},{7,6},{8,9},{9,8},{10,11... | collective-permute-start | bytes 1572872 | tf_op jit(solution)/shard_map/ppermute | solution.py:336
  90.2 13.4 %collective-permute-start.15 = (f32[2,4,128,128]{3,2,1,0:T(8,128)}, f32[2,4,128,128]{3,2,1,0:T(8,128)}, u32[]{:S(2)}, u32[]{:S(2)}) collective-permute-start(f32[2,4,128,128]{3,2,1,0:T(8,128)} %get-tuple-element.135), channel_id=1, source_target_pairs={{0,2},{1,3},{2,0},{3,1},{4,6},{5,7},{6,4},{7,5},{8,10},{9,11},{10,... | collective-permute-start | bytes 1572872 | tf_op jit(solution)/shard_map/ppermute | solution.py:336
  98.0 8.7 %collective-permute-start.13 = (f32[2,4,128,128]{3,2,1,0:T(8,128)S(1)}, f32[2,4,128,128]{3,2,1,0:T(8,128)S(1)}, u32[]{:S(2)}, u32[]{:S(2)}) collective-permute-start(f32[2,4,128,128]{3,2,1,0:T(8,128)S(1)} %collective-permute-done.11.refs_7_.refs_6_.refs_5_.refs_4_.refs_3_.refs_2_), channel_id=1, source_target_pairs={{0,8},{1,9},{2,6},{3,7},{4,0},{5,1},{6,14},{7,15},{8,16},{9,17},{1... | collective-permute-start | bytes 1572872 | tf_op jit(solution)/shard_map/ppermute | solution.py:336
  102.3 13.5 %collective-permute-start.17 = (f32[2,4,128,128]{3,2,1,0:T(8,128)}, f32[2,4,128,128]{3,2,1,0:T(8,128)S(1)}, u32[]{:S(2)}, u32[]{:S(2)}) collective-permute-start(f32[2,4,128,128]{3,2,1,0:T(8,128)} %shard_map.147), channel_id=1, source_target_pairs={{0,1},{1,0},{2,3},{3,2},{4,5},{5,4},{6,7},{7,6},{8,9},{9,8},{10,11... | collective-permute-start | bytes 1572872 | tf_op jit(solution)/shard_map/ppermute | solution.py:336
  109.1 6.6 %collective-permute-start.18 = (f32[2,4,128,128]{3,2,1,0:T(8,128)}, f32[2,4,128,128]{3,2,1,0:T(8,128)}, u32[]{:S(2)}, u32[]{:S(2)}) collective-permute-start(f32[2,4,128,128]{3,2,1,0:T(8,128)} %get-tuple-element.137), channel_id=1, source_target_pairs={{0,2},{1,3},{2,0},{3,1},{4,6},{5,7},{6,4},{7,5},{8,10},{9,11},{10,... | collective-permute-start | bytes 1572872 | tf_op jit(solution)/shard_map/ppermute | solution.py:336
  109.6 8.8 %collective-permute-start.16 = (f32[2,4,128,128]{3,2,1,0:T(8,128)S(1)}, f32[2,4,128,128]{3,2,1,0:T(8,128)S(1)}, u32[]{:S(2)}, u32[]{:S(2)}) collective-permute-start(f32[2,4,128,128]{3,2,1,0:T(8,128)S(1)} %collective-permute-done.13.refs_7_.refs_6_.refs_5_.refs_4_.refs_3_), channel_id=1, source_target_pairs={{0,8},{1,9},{2,6},{3,7},{4,0},{5,1},{6,14},{7,15},{8,16},{9,17},{1... | collective-permute-start | bytes 1572872 | tf_op jit(solution)/shard_map/ppermute | solution.py:336
  113.9 13.6 %collective-permute-start.20 = (f32[2,4,128,128]{3,2,1,0:T(8,128)}, f32[2,4,128,128]{3,2,1,0:T(8,128)}, u32[]{:S(2)}, u32[]{:S(2)}) collective-permute-start(f32[2,4,128,128]{3,2,1,0:T(8,128)} %shard_map.148), channel_id=1, source_target_pairs={{0,1},{1,0},{2,3},{3,2},{4,5},{5,4},{6,7},{7,6},{8,9},{9,8},{10,11... | collective-permute-start | bytes 1572872 | tf_op jit(solution)/shard_map/ppermute | solution.py:336
  119.5 7.9 %collective-permute-start.21 = (f32[2,4,128,128]{3,2,1,0:T(8,128)}, f32[2,4,128,128]{3,2,1,0:T(8,128)S(1)}, u32[]{:S(2)}, u32[]{:S(2)}) collective-permute-start(f32[2,4,128,128]{3,2,1,0:T(8,128)} %get-tuple-element.139), channel_id=1, source_target_pairs={{0,2},{1,3},{2,0},{3,1},{4,6},{5,7},{6,4},{7,5},{8,10},{9,11},{10,... | collective-permute-start | bytes 1572872 | tf_op jit(solution)/shard_map/ppermute | solution.py:336
  120.0 8.8 %collective-permute-start.19 = (f32[2,4,128,128]{3,2,1,0:T(8,128)S(1)}, f32[2,4,128,128]{3,2,1,0:T(8,128)S(1)}, u32[]{:S(2)}, u32[]{:S(2)}) collective-permute-start(f32[2,4,128,128]{3,2,1,0:T(8,128)S(1)} %collective-permute-done.16.refs_7_.refs_6_.refs_5_.refs_4_), channel_id=1, source_target_pairs={{0,8},{1,9},{2,6},{3,7},{4,0},{5,1},{6,14},{7,15},{8,16},{9,17},{1... | collective-permute-start | bytes 1572872 | tf_op jit(solution)/shard_map/ppermute | solution.py:336
  124.2 14.5 %collective-permute-start.23 = (f32[2,4,128,128]{3,2,1,0:T(8,128)}, f32[2,4,128,128]{3,2,1,0:T(8,128)}, u32[]{:S(2)}, u32[]{:S(2)}) collective-permute-start(f32[2,4,128,128]{3,2,1,0:T(8,128)} %shard_map.149), channel_id=1, source_target_pairs={{0,1},{1,0},{2,3},{3,2},{4,5},{5,4},{6,7},{7,6},{8,9},{9,8},{10,11... | collective-permute-start | bytes 1572872 | tf_op jit(solution)/shard_map/ppermute | solution.py:336
  130.9 7.8 %collective-permute-start.24 = (f32[2,4,128,128]{3,2,1,0:T(8,128)S(1)}, f32[2,4,128,128]{3,2,1,0:T(8,128)}, u32[]{:S(2)}, u32[]{:S(2)}) collective-permute-start(f32[2,4,128,128]{3,2,1,0:T(8,128)S(1)} %get-tuple-element.132), channel_id=1, source_target_pairs={{0,2},{1,3},{2,0},{3,1},{4,6},{5,7},{6,4},{7,5},{8,10},{9,11},{10,... | collective-permute-start | bytes 1572872 | tf_op jit(solution)/shard_map/ppermute | solution.py:336
  131.8 8.4 %collective-permute-start.22 = (f32[2,4,128,128]{3,2,1,0:T(8,128)S(1)}, f32[2,4,128,128]{3,2,1,0:T(8,128)S(1)}, u32[]{:S(2)}, u32[]{:S(2)}) collective-permute-start(f32[2,4,128,128]{3,2,1,0:T(8,128)S(1)} %collective-permute-done.19.refs_7_.refs_6_.refs_5_), channel_id=1, source_target_pairs={{0,8},{1,9},{2,6},{3,7},{4,0},{5,1},{6,14},{7,15},{8,16},{9,17},{1... | collective-permute-start | bytes 1572872 | tf_op jit(solution)/shard_map/ppermute | solution.py:336
  135.6 14.3 %collective-permute-start.26 = (f32[2,4,128,128]{3,2,1,0:T(8,128)}, f32[2,4,128,128]{3,2,1,0:T(8,128)}, u32[]{:S(2)}, u32[]{:S(2)}) collective-permute-start(f32[2,4,128,128]{3,2,1,0:T(8,128)} %shard_map.151), channel_id=1, source_target_pairs={{0,1},{1,0},{2,3},{3,2},{4,5},{5,4},{6,7},{7,6},{8,9},{9,8},{10,11... | collective-permute-start | bytes 1572872 | tf_op jit(solution)/shard_map/ppermute | solution.py:336
  142.4 7.6 %collective-permute-start.27 = (f32[2,4,128,128]{3,2,1,0:T(8,128)}, f32[2,4,128,128]{3,2,1,0:T(8,128)S(1)}, u32[]{:S(2)}, u32[]{:S(2)}) collective-permute-start(f32[2,4,128,128]{3,2,1,0:T(8,128)} %get-tuple-element.130), channel_id=1, source_target_pairs={{0,2},{1,3},{2,0},{3,1},{4,6},{5,7},{6,4},{7,5},{8,10},{9,11},{10,... | collective-permute-start | bytes 1572872 | tf_op jit(solution)/shard_map/ppermute | solution.py:336
  143.1 8.4 %collective-permute-start.25 = (f32[2,4,128,128]{3,2,1,0:T(8,128)S(1)}, f32[2,4,128,128]{3,2,1,0:T(8,128)}, u32[]{:S(2)}, u32[]{:S(2)}) collective-permute-start(f32[2,4,128,128]{3,2,1,0:T(8,128)S(1)} %collective-permute-done.22.refs_7_.refs_6_), channel_id=1, source_target_pairs={{0,8},{1,9},{2,6},{3,7},{4,0},{5,1},{6,14},{7,15},{8,16},{9,17},{1... | collective-permute-start | bytes 1572872 | tf_op jit(solution)/shard_map/ppermute | solution.py:336
  146.9 14.4 %collective-permute-start.28 = (f32[2,4,128,128]{3,2,1,0:T(8,128)}, f32[2,4,128,128]{3,2,1,0:T(8,128)}, u32[]{:S(2)}, u32[]{:S(2)}) collective-permute-start(f32[2,4,128,128]{3,2,1,0:T(8,128)} %shard_map.152), channel_id=1, source_target_pairs={{0,1},{1,0},{2,3},{3,2},{4,5},{5,4},{6,7},{7,6},{8,9},{9,8},{10,11... | collective-permute-start | bytes 1572872 | tf_op jit(solution)/shard_map/ppermute | solution.py:336
  153.5 7.8 %collective-permute-start.29 = (f32[2,4,128,128]{3,2,1,0:T(8,128)}, f32[2,4,128,128]{3,2,1,0:T(8,128)S(1)}, u32[]{:S(2)}, u32[]{:S(2)}) collective-permute-start(f32[2,4,128,128]{3,2,1,0:T(8,128)} %get-tuple-element.128), channel_id=1, source_target_pairs={{0,2},{1,3},{2,0},{3,1},{4,6},{5,7},{6,4},{7,5},{8,10},{9,11},{10,... | collective-permute-start | bytes 1572872 | tf_op jit(solution)/shard_map/ppermute | solution.py:336
  156.9 19.0 %collective-permute-start.30 = (f32[2,4,128,128]{3,2,1,0:T(8,128)}, f32[2,4,128,128]{3,2,1,0:T(8,128)S(1)}, u32[]{:S(2)}, u32[]{:S(2)}) collective-permute-start(f32[2,4,128,128]{3,2,1,0:T(8,128)} %shard_map.154), channel_id=1, source_target_pairs={{0,1},{1,0},{2,3},{3,2},{4,5},{5,4},{6,7},{7,6},{8,9},{9,8},{10,11... | collective-permute-start | bytes 1572872 | tf_op jit(solution)/shard_map/ppermute | solution.py:336
  162.4 13.5 %collective-permute-start.31 = (f32[2,4,128,128]{3,2,1,0:T(8,128)S(1)}, f32[2,4,128,128]{3,2,1,0:T(8,128)S(1)}, u32[]{:S(2)}, u32[]{:S(2)}) collective-permute-start(f32[2,4,128,128]{3,2,1,0:T(8,128)S(1)} %get-tuple-element.126), channel_id=1, source_target_pairs={{0,2},{1,3},{2,0},{3,1},{4,6},{5,7},{6,4},{7,5},{8,10},{9,11},{10,... | collective-permute-start | bytes 1572872 | tf_op jit(solution)/shard_map/ppermute | solution.py:336
  175.8 9.6 %collective-permute-start.33 = (f32[2,64,32,128]{3,2,1,0:T(8,128)S(1)}, f32[2,64,32,128]{3,2,1,0:T(8,128)S(1)}, u32[]{:S(2)}, u32[]{:S(2)}) collective-permute-start(f32[2,64,32,128]{3,2,1,0:T(8,128)S(1)} %get-tuple-element.104), channel_id=1, source_target_pairs={{0,2},{1,3},{2,0},{3,1},{4,6},{5,7},{6,4},{7,5},{8,10},{9,11},{10,... | collective-permute-start | bytes 6291464 | tf_op jit(solution)/shard_map/ppermute | solution.py:336
  176.1 4.8 %collective-permute-start.32 = (f32[2,4,128,128]{3,2,1,0:T(8,128)S(1)}, f32[2,4,128,128]{3,2,1,0:T(8,128)S(1)}, u32[]{:S(2)}, u32[]{:S(2)}) collective-permute-start(f32[2,4,128,128]{3,2,1,0:T(8,128)S(1)} %get-tuple-element.124), channel_id=1, source_target_pairs={{0,2},{1,3},{2,0},{3,1},{4,6},{5,7},{6,4},{7,5},{8,10},{9,11},{10,... | collective-permute-start | bytes 1572872 | tf_op jit(solution)/shard_map/ppermute | solution.py:336
  180.7 4.7 %collective-permute-start.34 = (f32[2,64,16,128]{3,2,1,0:T(8,128)S(1)}, f32[2,64,16,128]{3,2,1,0:T(8,128)S(1)}, u32[]{:S(2)}, u32[]{:S(2)}) collective-permute-start(f32[2,64,16,128]{3,2,1,0:T(8,128)S(1)} %get-tuple-element.105), channel_id=1, source_target_pairs={{0,2},{1,3},{2,0},{3,1},{4,6},{5,7},{6,4},{7,5},{8,10},{9,11},{10,... | collective-permute-start | bytes 3145736 | tf_op jit(solution)/shard_map/ppermute | solution.py:336
  184.9 2.8 %collective-permute-start.35 = (f32[2,64,16,128]{3,2,1,0:T(8,128)S(1)}, f32[2,64,16,128]{3,2,1,0:T(8,128)S(1)}, u32[]{:S(2)}, u32[]{:S(2)}) collective-permute-start(f32[2,64,16,128]{3,2,1,0:T(8,128)S(1)} %get-tuple-element.106), channel_id=1, source_target_pairs={{0,2},{1,3},{2,0},{3,1},{4,6},{5,7},{6,4},{7,5},{8,10},{9,11},{10,... | collective-permute-start | bytes 3145736 | tf_op jit(solution)/shard_map/ppermute | solution.py:336
  197.5 4.2 %collective-permute-start.36 = (f32[2,64,32,128]{3,2,1,0:T(8,128)S(1)}, f32[2,64,32,128]{3,2,1,0:T(8,128)S(1)}, u32[]{:S(2)}, u32[]{:S(2)}) collective-permute-start(f32[2,64,32,128]{3,2,1,0:T(8,128)S(1)} %get-tuple-element.108), channel_id=1, source_target_pairs={{0,2},{1,3},{2,0},{3,1},{4,6},{5,7},{6,4},{7,5},{8,10},{9,11},{10,... | collective-permute-start | bytes 6291464 | tf_op jit(solution)/shard_map/ppermute | solution.py:336
  205.3 16.1 %collective-permute-start.37 = (f32[2,8,128,128]{3,2,1,0:T(8,128)S(1)}, f32[2,8,128,128]{3,2,1,0:T(8,128)S(1)}, u32[]{:S(2)}, u32[]{:S(2)}) collective-permute-start(f32[2,8,128,128]{3,2,1,0:T(8,128)S(1)} %shard_map.157), channel_id=1, source_target_pairs={{1,2},{2,1},{5,6},{6,5},{9,10},{10,9},{13,14},{14,13},{17,18},{18,... | collective-permute-start | bytes 3145736 | tf_op jit(solution)/shard_map/ppermute | solution.py:336
  208.7 12.7 %collective-permute-start.39 = (f32[2,64,16,128]{3,2,1,0:T(8,128)S(1)}, f32[2,64,16,128]{3,2,1,0:T(8,128)S(1)}, u32[]{:S(2)}, u32[]{:S(2)}) collective-permute-start(f32[2,64,16,128]{3,2,1,0:T(8,128)S(1)} %get-tuple-element.114), channel_id=1, source_target_pairs={{0,2},{1,3},{2,0},{3,1},{4,6},{5,7},{6,4},{7,5},{8,10},{9,11},{10,... | collective-permute-start | bytes 3145736 | tf_op jit(solution)/shard_map/ppermute | solution.py:336
  212.3 20.3 %collective-permute-start.38 = (f32[2,8,128,128]{3,2,1,0:T(8,128)S(1)}, f32[2,8,128,128]{3,2,1,0:T(8,128)S(1)}, u32[]{:S(2)}, u32[]{:S(2)}) collective-permute-start(f32[2,8,128,128]{3,2,1,0:T(8,128)S(1)} %shard_map.158), channel_id=1, source_target_pairs={{1,2},{2,1},{5,6},{6,5},{9,10},{10,9},{13,14},{14,13},{17,18},{18,... | collective-permute-start | bytes 3145736 | tf_op jit(solution)/shard_map/ppermute | solution.py:336
  214.8 17.9 %collective-permute-start.41 = (f32[2,64,16,128]{3,2,1,0:T(8,128)S(1)}, f32[2,64,16,128]{3,2,1,0:T(8,128)S(1)}, u32[]{:S(2)}, u32[]{:S(2)}) collective-permute-start(f32[2,64,16,128]{3,2,1,0:T(8,128)S(1)} %get-tuple-element.116), channel_id=1, source_target_pairs={{0,2},{1,3},{2,0},{3,1},{4,6},{5,7},{6,4},{7,5},{8,10},{9,11},{10,... | collective-permute-start | bytes 3145736 | tf_op jit(solution)/shard_map/ppermute | solution.py:336
  224.7 19.2 %collective-permute-start.40 = (f32[2,8,128,128]{3,2,1,0:T(8,128)S(1)}, f32[2,8,128,128]{3,2,1,0:T(8,128)S(1)}, u32[]{:S(2)}, u32[]{:S(2)}) collective-permute-start(f32[2,8,128,128]{3,2,1,0:T(8,128)S(1)} %shard_map.159), channel_id=1, source_target_pairs={{1,2},{2,1},{5,6},{6,5},{9,10},{10,9},{13,14},{14,13},{17,18},{18,... | collective-permute-start | bytes 3145736 | tf_op jit(solution)/shard_map/ppermute | solution.py:336
  235.9 19.2 %collective-permute-start.42 = (f32[2,8,128,128]{3,2,1,0:T(8,128)S(1)}, f32[2,8,128,128]{3,2,1,0:T(8,128)S(1)}, u32[]{:S(2)}, u32[]{:S(2)}) collective-permute-start(f32[2,8,128,128]{3,2,1,0:T(8,128)S(1)} %shard_map.160), channel_id=1, source_target_pairs={{1,2},{2,1},{5,6},{6,5},{9,10},{10,9},{13,14},{14,13},{17,18},{18,... | collective-permute-start | bytes 3145736 | tf_op jit(solution)/shard_map/ppermute | solution.py:336
  (34 other events, 294.7 us)

commit v6 on v5

--- a/solution.py
+++ b/solution.py
@@ -19,7 +19,7 @@
 GROUPS = ((0, 4), (4, 6), (6, 8))
 TERM_GROUPS = ((0, 2), (2, 4), (4, 6), (6, 8))
 HOP_STEPS = 2
-PHI_STEP = 6
+PHI_STEP = 5
 
 
 def spread(shard, axis, root):

time: 259 us -> 263 us (1.015)
  waiting for transfers between devices: 92.4 us -> 104 us
  starting transfers between devices: 65.2 us -> 56.7 us
    ppermute x43, waiting for transfers between devices: 92.4 us -> 104 us  [move(): return lax.ppermute(value, axes, pairs)]
    ppermute x43, starting transfers between devices: 65.2 us -> 56.7 us  [move(): return lax.ppermute(value, axes, pairs)]
where the time goes in v6:
time: 263 us; the launch traced here: 262 us
  waiting for transfers between devices  104 us (40%)
  Pallas kernels  59.7 us (23%)
  starting transfers between devices  56.7 us (22%)
  other arithmetic  33.4 us (13%)
  local copies, waits for them, and re-layouts  6.98 us (3%)
    ppermute x43, waiting for transfers between devices, move(): return lax.ppermute(value, axes, pairs)  104 us
    ppermute x43, starting transfers between devices, move(): return lax.ppermute(value, axes, pairs)  56.7 us
    pallas_call x8, Pallas kernels, arrived(): pl.pallas_call(pick_body, in_specs=[pl.BlockSpec(memory_space=pltpu.SMEM)...  20.2 us
    pallas_call x3, Pallas kernels, paired(): call(forward_body, (hi - lo) // UNITS, [slab] + unit_specs(0 if hi - lo >...  16.2 us
    pallas_call x4, Pallas kernels, paired(): call(backward_body, (hi - lo) // UNITS, [some_lines, some_lines] + g_unit...  13.6 us
    pallas_call x1, Pallas kernels, paired(): call(middle_body, half // MIDDLE_ROWS, cols * 2 + [chosen(square)] * 4, c...  9.67 us
    another operation x5, other arithmetic, by_unit(): return [jnp.stack(values[lo:hi])] * UNITS  9.25 us
    select_n x5, other arithmetic, paired(): swapping.append((t + 1, move(jnp.where(home, got, mine), sibling)))  7.45 us
  transfers between devices with their start and end apart: 43, of which 27 were waited for; matrix products, arithmetic and copies ran while one was open for 13% of the time, Pallas kernels for 18%

profile of v6, /device:TPU:1, one launch (start us, length us, event | category | flops | bytes accessed | tf_op | source)
XLA Modules:
  0.0 262.2 jit_solution(7641831522134761113)
XLA Ops:
  2.5 4.7 %dynamic-slice_bitcast_fusion = f32[64,128,128]{2,1,0:T(8,128)} fusion(f32[2,64,128,128]{3,2,1,0:T(8,128)} %param.15, s32[]{:T(128)S(6)} %select_n.264), kind=kLoop, calls=%fused_computation.1 | loop fusion | bytes 8388612 | tf_op jit(solution)/shard_map/jit(dynamic_index_in_dim)/squeeze | solution.py:375
  8.2 4.9 %collective-permute-start.7 = (f32[64,128,128]{2,1,0:T(8,128)}, f32[64,128,128]{2,1,0:T(8,128)}, u32[]{:S(2)}, u32[]{:S(2)}) collective-permute-start(f32[64,128,128]{2,1,0:T(8,128)} %dynamic-slice_bitcast_fusion), channel_id=1, source_target_pairs={{1,2},{2,1},{5,6},{6,5},{9,10},{10,9},{13,14},{14,13},{17,18},{18,... | collective-permute-start | bytes 12582920 | tf_op jit(solution)/shard_map/ppermute | solution.py:336
  15.9 6.1 %collective-permute-done.1 = f32[2,4,128,128]{3,2,1,0:T(8,128)S(1)} collective-permute-done((f32[2,4,128,128]{3,2,1,0:T(8,128)S(1)}, f32[2,4,128,128]{3,2,1,0:T(8,128)S(1)}, u32[]{:S(2)}, u32[]{:S(2)}) %collective-permute-start.1) | collective-permute-done | bytes 524320 | tf_op jit(solution)/shard_map/ppermute | solution.py:336
  24.9 3.7 %fusion.2 = (f32[2,4,128,128]{3,2,1,0:T(8,128)S(1)}, f32[2,4,128,128]{3,2,1,0:T(8,128)S(1)}, f32[2,4,128,128]{3,2,1,0:T(8,128)}, f32[2,4,128,128]{3,2,1,0:T(8,128)S(1)}, f32[2,4,128,128]{3,2,1,0:T(8,128)S(1)}) fusion(f32[2,2,32,128,128]{4,3,2,1,0:T(8,128)} %bitcast.7, s32[]{:T(128)S(6)} %select_n.263, pred[]{:T(512)S(6)} %eq.26, ...), kind=kLoop, calls=%fused_computation.9 | loop fusion | flops 655360 | bytes 7864325 | tf_op jit(solution)/shard_map/jit(_where)/select_n | solution.py:384
  28.6 3.2 %collective-permute-done.3 = f32[2,4,128,128]{3,2,1,0:T(8,128)S(1)} collective-permute-done((f32[2,4,128,128]{3,2,1,0:T(8,128)S(1)}, f32[2,4,128,128]{3,2,1,0:T(8,128)S(1)}, u32[]{:S(2)}, u32[]{:S(2)}) %collective-permute-start.3) | collective-permute-done | bytes 524320 | tf_op jit(solution)/shard_map/ppermute | solution.py:336
  34.6 6.9 %collective-permute-done.4 = f32[2,4,128,128]{3,2,1,0:T(8,128)S(1)} collective-permute-done((f32[2,4,128,128]{3,2,1,0:T(8,128)S(1)}, f32[2,4,128,128]{3,2,1,0:T(8,128)S(1)}, u32[]{:S(2)}, u32[]{:S(2)}) %collective-permute-start.4) | collective-permute-done | bytes 524320 | tf_op jit(solution)/shard_map/ppermute | solution.py:336
  43.1 6.9 %collective-permute-done.5 = f32[2,4,128,128]{3,2,1,0:T(8,128)S(1)} collective-permute-done((f32[2,4,128,128]{3,2,1,0:T(8,128)S(1)}, f32[2,4,128,128]{3,2,1,0:T(8,128)S(1)}, u32[]{:S(2)}, u32[]{:S(2)}) %collective-permute-start.5) | collective-permute-done | bytes 524320 | tf_op jit(solution)/shard_map/ppermute | solution.py:336
  51.5 8.4 %collective-permute-done.7 = f32[64,128,128]{2,1,0:T(8,128)} collective-permute-done((f32[64,128,128]{2,1,0:T(8,128)}, f32[64,128,128]{2,1,0:T(8,128)}, u32[]{:S(2)}, u32[]{:S(2)}) %collective-permute-start.7) | collective-permute-done | bytes 4194336 | tf_op jit(solution)/shard_map/ppermute | solution.py:336
  62.9 5.3 %broadcast_select_fusion = f32[64,128,128]{2,1,0:T(8,128)} fusion(f32[64,128,128]{2,1,0:T(8,128)} %dynamic-slice_bitcast_fusion, f32[64,128,128]{2,1,0:T(8,128)} %collective-permute-done.7, pred[]{:T(512)S(6)} %eq.25), kind=kLoop, calls=%fused_computation.4 | loop fusion | flops 1048576 | bytes 12582913 | tf_op jit(solution)/shard_map/jit(_where)/select_n | solution.py:427
  71.3 6.9 %collective-permute-done.9 = f32[2,4,128,128]{3,2,1,0:T(8,128)S(1)} collective-permute-done((f32[2,4,128,128]{3,2,1,0:T(8,128)S(1)}, f32[2,4,128,128]{3,2,1,0:T(8,128)S(1)}, u32[]{:S(2)}, u32[]{:S(2)}) %collective-permute-start.9) | collective-permute-done | bytes 524320 | tf_op jit(solution)/shard_map/ppermute | solution.py:336
  79.8 2.5 shard_map.145
  82.4 4.3 %collective-permute-done.10.refs_7_.refs_6_.refs_5_.refs_4_.refs_3_.refs_2_.refs_1_ = f32[2,4,128,128]{3,2,1,0:T(8,128)S(1)} collective-permute-done((f32[2,4,128,128]{3,2,1,0:T(8,128)S(1)}, f32[2,4,128,128]{3,2,1,0:T(8,128)S(1)}, u32[]{:S(2)}, u32[]{:S(2)}) %collective-permute-start.10) | collective-permute-done | bytes 524320 | tf_op jit(solution)/shard_map/ppermute | solution.py:336
  88.1 2.5 shard_map.146
  92.5 2.5 collective-permute-done.11.refs_7_.refs_6_.refs_5_.refs_4_.refs_3_.refs_2_
  97.1 5.6 %collective-permute-start.15 = (f32[2,4,128,128]{3,2,1,0:T(8,128)}, f32[2,4,128,128]{3,2,1,0:T(8,128)}, u32[]{:S(2)}, u32[]{:S(2)}) collective-permute-start(f32[2,4,128,128]{3,2,1,0:T(8,128)} %get-tuple-element.135), channel_id=1, source_target_pairs={{0,2},{1,3},{2,0},{3,1},{4,6},{5,7},{6,4},{7,5},{8,10},{9,11},{10,... | collective-permute-start | bytes 1572872 | tf_op jit(solution)/shard_map/ppermute | solution.py:336
  104.3 2.5 shard_map.147
  107.8 3.4 %collective-permute-done.13.refs_7_.refs_6_.refs_5_.refs_4_.refs_3_ = f32[2,4,128,128]{3,2,1,0:T(8,128)S(1)} collective-permute-done((f32[2,4,128,128]{3,2,1,0:T(8,128)S(1)}, f32[2,4,128,128]{3,2,1,0:T(8,128)S(1)}, u32[]{:S(2)}, u32[]{:S(2)}) %collective-permute-start.13) | collective-permute-done | bytes 524320 | tf_op jit(solution)/shard_map/ppermute | solution.py:336
  111.2 2.4 select_bitcast_fusion.6
  115.9 2.6 shard_map.148
  120.3 2.6 collective-permute-done.16.refs_7_.refs_6_.refs_5_.refs_4_
  126.3 2.5 shard_map.149
  129.7 2.3 collective-permute-done.20
  133.3 2.2 broadcast_select_fusion.9
  137.6 2.5 shard_map.151
  144.8 2.1 broadcast_select_fusion.8
  149.0 2.5 shard_map.152
  152.4 2.1 collective-permute-done.26
  158.9 2.5 shard_map.154
  162.4 3.5 %collective-permute-done.28 = f32[2,4,128,128]{3,2,1,0:T(8,128)} collective-permute-done((f32[2,4,128,128]{3,2,1,0:T(8,128)}, f32[2,4,128,128]{3,2,1,0:T(8,128)}, u32[]{:S(2)}, u32[]{:S(2)}) %collective-permute-start.28) | collective-permute-done | bytes 524320 | tf_op jit(solution)/shard_map/ppermute | solution.py:336
  172.3 8.0 %shard_map.150 = (f32[2,64,32,128]{3,2,1,0:T(8,128)S(1)}, f32[2,64,32,128]{3,2,1,0:T(8,128)S(1)}) custom-call(s32[2]{0:T(128)S(1)} %copy-done.13, f32[2,32,128,128]{3,2,1,0:T(8,128)S(1)} %bitcast.97, f32[4,2,4,128,128]{4,3,2,1,0:T(8,128)S(1)} %pad_maximum_fusion.1.refs_0_.refs_1_, f32[4,2,4,128,128]{4,3,2,1,0:T(8,128)S(1)} %pad_maximum_fusion.1.refs_0_.refs_1_, ...), custom_call_target="tpu_custom_call" | custom-call | tf_op jit(solution)/shard_map/pallas_call | solution.py:483
  181.1 4.1 %shard_map.153 = (f32[2,64,16,128]{3,2,1,0:T(8,128)S(1)}, f32[2,64,16,128]{3,2,1,0:T(8,128)S(1)}) custom-call(s32[2]{0:T(128)S(1)} %copy-done.13, f32[2,32,128,128]{3,2,1,0:T(8,128)S(1)} %bitcast.98, f32[1,2,4,128,128]{4,3,2,1,0:T(8,128)S(1)} %get-tuple-element.131.refs_0_, f32[1,2,4,128,128]{4,3,2,1,0:T(8,128)S(1)} %get-tuple-element.129.refs_1_, ...), custom_call_target="tpu_custom_call" | custom-call | tf_op jit(solution)/shard_map/pallas_call | solution.py:483
  185.3 4.1 %shard_map.155 = (f32[2,64,16,128]{3,2,1,0:T(8,128)S(1)}, f32[2,64,16,128]{3,2,1,0:T(8,128)S(1)}) custom-call(s32[2]{0:T(128)S(1)} %copy-done.13, f32[2,32,128,128]{3,2,1,0:T(8,128)S(1)} %bitcast.99, f32[1,2,4,128,128]{4,3,2,1,0:T(8,128)S(1)} %get-tuple-element.127.refs_0_, f32[1,2,4,128,128]{4,3,2,1,0:T(8,128)S(1)} %get-tuple-element.125.refs_1_, ...), custom_call_target="tpu_custom_call" | custom-call | tf_op jit(solution)/shard_map/pallas_call | solution.py:483
  189.9 2.3 collective-permute-done.35.refs_5_
  192.3 9.7 %shard_map.156 = (f32[2,64,32,128]{3,2,1,0:T(8,128)S(1)}, f32[2,64,16,128]{3,2,1,0:T(8,128)S(1)}, f32[2,64,16,128]{3,2,1,0:T(8,128)S(1)}, f32[2,64,32,128]{3,2,1...) custom-call(s32[2]{0:T(128)S(1)} %copy-done.13, ...), custom_call_target="tpu_custom_call" | custom-call | tf_op jit(solution)/shard_map/pallas_call | solution.py:498
  202.4 3.8 %collective-permute-done.36.recv = f32[2,64,32,128]{3,2,1,0:T(8,128)S(1)} collective-permute-done((f32[2,64,32,128]{3,2,1,0:T(8,128)S(1)}, f32[2,64,32,128]{3,2,1,0:T(8,128)S(1)}, u32[]{:S(2)}, u32[]{:S(2)}) %collective-permute-start.36) | collective-permute-done | bytes 2097184 | tf_op jit(solution)/shard_map/ppermute | solution.py:336
  206.2 3.6 %shard_map.157 = f32[2,8,128,128]{3,2,1,0:T(8,128)S(1)} custom-call(s32[2]{0:T(128)S(1)} %copy-done.13, f32[2,64,32,128]{3,2,1,0:T(8,128)S(1)} %get-tuple-element.107.keep, f32[2,64,32,128]{3,2,1,0:T(8,128)S(1)} %collective-permute-done.36.recv, f32[4,2,4,128,128]{4,3,2,1,0:T(8,128)S(1)} %pad_maximum_fusion.1.refs_0_.refs_1_, ...), custom_call_target="tpu_custom_call" | custom-call | tf_op jit(solution)/shard_map/pallas_call | solution.py:520
  209.8 3.0 %collective-permute-start.37 = (f32[2,8,128,128]{3,2,1,0:T(8,128)S(1)}, f32[2,8,128,128]{3,2,1,0:T(8,128)S(1)}, u32[]{:S(2)}, u32[]{:S(2)}) collective-permute-start(f32[2,8,128,128]{3,2,1,0:T(8,128)S(1)} %shard_map.157), channel_id=1, source_target_pairs={{1,2},{2,1},{5,6},{6,5},{9,10},{10,9},{13,14},{14,13},{17,18},{18,... | collective-permute-start | bytes 3145736 | tf_op jit(solution)/shard_map/ppermute | solution.py:336
  212.9 3.5 %shard_map.158 = f32[2,8,128,128]{3,2,1,0:T(8,128)S(1)} custom-call(s32[2]{0:T(128)S(1)} %copy-done.13, f32[2,64,32,128]{3,2,1,0:T(8,128)S(1)} %get-tuple-element.107.keep, f32[2,64,32,128]{3,2,1,0:T(8,128)S(1)} %collective-permute-done.36.recv, f32[4,2,4,128,128]{4,3,2,1,0:T(8,128)S(1)} %pad_maximum_fusion.1.refs_0_.refs_1_, ...), custom_call_target="tpu_custom_call" | custom-call | tf_op jit(solution)/shard_map/pallas_call | solution.py:520
  216.4 2.8 %collective-permute-start.38 = (f32[2,8,128,128]{3,2,1,0:T(8,128)S(1)}, f32[2,8,128,128]{3,2,1,0:T(8,128)S(1)}, u32[]{:S(2)}, u32[]{:S(2)}) collective-permute-start(f32[2,8,128,128]{3,2,1,0:T(8,128)S(1)} %shard_map.158), channel_id=1, source_target_pairs={{1,2},{2,1},{5,6},{6,5},{9,10},{10,9},{13,14},{14,13},{17,18},{18,... | collective-permute-start | bytes 3145736 | tf_op jit(solution)/shard_map/ppermute | solution.py:336
  219.3 6.6 %collective-permute-done.37 = f32[2,8,128,128]{3,2,1,0:T(8,128)S(1)} collective-permute-done((f32[2,8,128,128]{3,2,1,0:T(8,128)S(1)}, f32[2,8,128,128]{3,2,1,0:T(8,128)S(1)}, u32[]{:S(2)}, u32[]{:S(2)}) %collective-permute-start.37) | collective-permute-done | bytes 1048608 | tf_op jit(solution)/shard_map/ppermute | solution.py:336
  225.9 3.2 %shard_map.159 = f32[2,8,128,128]{3,2,1,0:T(8,128)S(1)} custom-call(s32[2]{0:T(128)S(1)} %copy-done.13, f32[2,64,16,128]{3,2,1,0:T(8,128)S(1)} %get-tuple-element.113.keep, f32[2,64,16,128]{3,2,1,0:T(8,128)S(1)} %collective-permute-done.39.recv, f32[1,2,4,128,128]{4,3,2,1,0:T(8,128)S(1)} %get-tuple-element.131.refs_0_, ...), custom_call_target="tpu_custom_call" | custom-call | tf_op jit(solution)/shard_map/pallas_call | solution.py:520
  229.1 3.0 %collective-permute-start.40 = (f32[2,8,128,128]{3,2,1,0:T(8,128)S(1)}, f32[2,8,128,128]{3,2,1,0:T(8,128)S(1)}, u32[]{:S(2)}, u32[]{:S(2)}) collective-permute-start(f32[2,8,128,128]{3,2,1,0:T(8,128)S(1)} %shard_map.159), channel_id=1, source_target_pairs={{1,2},{2,1},{5,6},{6,5},{9,10},{10,9},{13,14},{14,13},{17,18},{18,... | collective-permute-start | bytes 3145736 | tf_op jit(solution)/shard_map/ppermute | solution.py:336
  232.2 4.9 %collective-permute-done.38 = f32[2,8,128,128]{3,2,1,0:T(8,128)S(1)} collective-permute-done((f32[2,8,128,128]{3,2,1,0:T(8,128)S(1)}, f32[2,8,128,128]{3,2,1,0:T(8,128)S(1)}, u32[]{:S(2)}, u32[]{:S(2)}) %collective-permute-start.38) | collective-permute-done | bytes 1048608 | tf_op jit(solution)/shard_map/ppermute | solution.py:336
  237.1 3.3 %shard_map.160 = f32[2,8,128,128]{3,2,1,0:T(8,128)S(1)} custom-call(s32[2]{0:T(128)S(1)} %copy-done.13, f32[2,64,16,128]{3,2,1,0:T(8,128)S(1)} %get-tuple-element.115.keep, f32[2,64,16,128]{3,2,1,0:T(8,128)S(1)} %collective-permute-done.41.recv, f32[1,2,4,128,128]{4,3,2,1,0:T(8,128)S(1)} %get-tuple-element.127.refs_0_, ...), custom_call_target="tpu_custom_call" | custom-call | tf_op jit(solution)/shard_map/pallas_call | solution.py:520
  240.4 3.0 %collective-permute-start.42 = (f32[2,8,128,128]{3,2,1,0:T(8,128)S(1)}, f32[2,8,128,128]{3,2,1,0:T(8,128)S(1)}, u32[]{:S(2)}, u32[]{:S(2)}) collective-permute-start(f32[2,8,128,128]{3,2,1,0:T(8,128)S(1)} %shard_map.160), channel_id=1, source_target_pairs={{1,2},{2,1},{5,6},{6,5},{9,10},{10,9},{13,14},{14,13},{17,18},{18,... | collective-permute-start | bytes 3145736 | tf_op jit(solution)/shard_map/ppermute | solution.py:336
  243.7 4.7 %collective-permute-done.40 = f32[2,8,128,128]{3,2,1,0:T(8,128)S(1)} collective-permute-done((f32[2,8,128,128]{3,2,1,0:T(8,128)S(1)}, f32[2,8,128,128]{3,2,1,0:T(8,128)S(1)}, u32[]{:S(2)}, u32[]{:S(2)}) %collective-permute-start.40) | collective-permute-done | bytes 1048608 | tf_op jit(solution)/shard_map/ppermute | solution.py:336
  248.5 11.1 %collective-permute-done.42 = f32[2,8,128,128]{3,2,1,0:T(8,128)S(1)} collective-permute-done((f32[2,8,128,128]{3,2,1,0:T(8,128)S(1)}, f32[2,8,128,128]{3,2,1,0:T(8,128)S(1)}, u32[]{:S(2)}, u32[]{:S(2)}) %collective-permute-start.42) | collective-permute-done | bytes 1048608 | tf_op jit(solution)/shard_map/ppermute | solution.py:336
  259.7 2.5 pad_maximum_fusion
  (162 shorter events, 62.5 us)
Async XLA Ops:
  1.3 20.7 %collective-permute-start.2 = (f32[2,64,128,128]{3,2,1,0:T(8,128)}, f32[2,64,128,128]{3,2,1,0:T(8,128)}, u32[]{:S(2)}, u32[]{:S(2)}) collective-permute-start(f32[2,64,128,128]{3,2,1,0:T(8,128)} %param.15), channel_id=1, source_target_pairs={{0,2},{1,3},{2,0},{3,1},{4,6},{5,7},{6,4},{7,5},{8,10},{9,11},{10,... | collective-permute-start | bytes 25165832 | tf_op jit(solution)/shard_map/ppermute | solution.py:336
  1.4 6.8 %collective-permute-start = (f32[2,1,4,128,128]{4,3,2,0,1:T(8,128)S(1)}, f32[2,1,4,128,128]{4,3,2,0,1:T(8,128)S(1)}, u32[]{:S(2)}, u32[]{:S(2)}) collective-permute-start(f32[2,1,4,128,128]{4,3,2,0,1:T(8,128)S(1)} %get-tuple-element.62), channel_id=1, source_target_pairs={{0,2},{1,3},{2,0},{3,1},{4,6},{5,7},{6,4},{7,5},{8,10},{9,11},{10,... | collective-permute-start | bytes 1572872 | tf_op jit(solution)/shard_map/ppermute | solution.py:336
  8.2 51.7 %collective-permute-start.7 = (f32[64,128,128]{2,1,0:T(8,128)}, f32[64,128,128]{2,1,0:T(8,128)}, u32[]{:S(2)}, u32[]{:S(2)}) collective-permute-start(f32[64,128,128]{2,1,0:T(8,128)} %dynamic-slice_bitcast_fusion), channel_id=1, source_target_pairs={{1,2},{2,1},{5,6},{6,5},{9,10},{10,9},{13,14},{14,13},{17,18},{18,... | collective-permute-start | bytes 12582920 | tf_op jit(solution)/shard_map/ppermute | solution.py:336
  13.9 8.1 %collective-permute-start.1 = (f32[2,4,128,128]{3,2,1,0:T(8,128)S(1)}, f32[2,4,128,128]{3,2,1,0:T(8,128)S(1)}, u32[]{:S(2)}, u32[]{:S(2)}) collective-permute-start(f32[2,4,128,128]{3,2,1,0:T(8,128)S(1)} %select_bitcast_fusion.8.refs_0_), channel_id=1, source_target_pairs={{0,8},{1,9},{2,6},{3,7},{4,0},{5,1},{6,14},{7,15},{8,16},{9,17},{1... | collective-permute-start | bytes 1572872 | tf_op jit(solution)/shard_map/ppermute | solution.py:336
  23.3 8.5 %collective-permute-start.3 = (f32[2,4,128,128]{3,2,1,0:T(8,128)S(1)}, f32[2,4,128,128]{3,2,1,0:T(8,128)S(1)}, u32[]{:S(2)}, u32[]{:S(2)}) collective-permute-start(f32[2,4,128,128]{3,2,1,0:T(8,128)S(1)} %fusion.8.refs_1_.refs_0_), channel_id=1, source_target_pairs={{0,8},{1,9},{2,6},{3,7},{4,0},{5,1},{6,14},{7,15},{8,16},{9,17},{1... | collective-permute-start | bytes 1572872 | tf_op jit(solution)/shard_map/ppermute | solution.py:336
  31.8 28.2 %copy-start.36 = (f32[2,4,128,128]{3,2,1,0:T(8,128)S(1)}, f32[2,4,128,128]{3,2,1,0:T(8,128)}, u32[]{:S(2)}) copy-start(f32[2,4,128,128]{3,2,1,0:T(8,128)} %get-tuple-element.69) | copy-start | bytes 1572868
  33.2 35.0 %copy-start.23 = (f32[2,4,128,128]{3,2,1,0:T(8,128)}, f32[2,4,128,128]{3,2,1,0:T(8,128)S(1)}, u32[]{:S(2)}) copy-start(f32[2,4,128,128]{3,2,1,0:T(8,128)S(1)} %fusion.1.refs_2_.refs_1_.refs_0_) | copy-start | bytes 1572868
  33.2 8.4 %collective-permute-start.4 = (f32[2,4,128,128]{3,2,1,0:T(8,128)S(1)}, f32[2,4,128,128]{3,2,1,0:T(8,128)S(1)}, u32[]{:S(2)}, u32[]{:S(2)}) collective-permute-start(f32[2,4,128,128]{3,2,1,0:T(8,128)S(1)} %fusion.1.refs_2_.refs_1_.refs_0_), channel_id=1, source_target_pairs={{0,8},{1,9},{2,6},{3,7},{4,0},{5,1},{6,14},{7,15},{8,16},{9,17},{1... | collective-permute-start | bytes 1572872 | tf_op jit(solution)/shard_map/ppermute | solution.py:336
  41.6 26.5 %copy-start.21 = (f32[2,4,128,128]{3,2,1,0:T(8,128)}, f32[2,4,128,128]{3,2,1,0:T(8,128)S(1)}, u32[]{:S(2)}) copy-start(f32[2,4,128,128]{3,2,1,0:T(8,128)S(1)} %broadcast_select_fusion.17.refs_3_.refs_2_.refs_1_.refs_0_) | copy-start | bytes 1572868
  41.6 8.4 %collective-permute-start.5 = (f32[2,4,128,128]{3,2,1,0:T(8,128)S(1)}, f32[2,4,128,128]{3,2,1,0:T(8,128)S(1)}, u32[]{:S(2)}, u32[]{:S(2)}) collective-permute-start(f32[2,4,128,128]{3,2,1,0:T(8,128)S(1)} %broadcast_select_fusion.17.refs_3_.refs_2_.refs_1_.refs_0_), channel_id=1, source_target_pairs={{0,8},{1,9},{2,6},{3,7},{4,0},{5,1},{6,14},{7,15},{8,16},{9,17},{1... | collective-permute-start | bytes 1572872 | tf_op jit(solution)/shard_map/ppermute | solution.py:336
  50.1 18.1 %copy-start.19 = (f32[2,4,128,128]{3,2,1,0:T(8,128)}, f32[2,4,128,128]{3,2,1,0:T(8,128)S(1)}, u32[]{:S(2)}) copy-start(f32[2,4,128,128]{3,2,1,0:T(8,128)S(1)} %broadcast_select_fusion.16.refs_4_.refs_3_.refs_2_.refs_1_.refs_0_) | copy-start | bytes 1572868
  50.1 9.9 %collective-permute-start.6 = (f32[2,4,128,128]{3,2,1,0:T(8,128)S(1)}, f32[2,4,128,128]{3,2,1,0:T(8,128)}, u32[]{:S(2)}, u32[]{:S(2)}) collective-permute-start(f32[2,4,128,128]{3,2,1,0:T(8,128)S(1)} %broadcast_select_fusion.16.refs_4_.refs_3_.refs_2_.refs_1_.refs_0_), channel_id=1, source_target_pairs={{0,8},{1,9},{2,6},{3,7},{4,0},{5,1},{6,14},{7,15},{8,16},{9,17},{1... | collective-permute-start | bytes 1572872 | tf_op jit(solution)/shard_map/ppermute | solution.py:336
  61.1 8.7 %collective-permute-start.8 = (f32[2,4,128,128]{3,2,1,0:T(8,128)S(1)}, f32[2,4,128,128]{3,2,1,0:T(8,128)S(1)}, u32[]{:S(2)}, u32[]{:S(2)}) collective-permute-start(f32[2,4,128,128]{3,2,1,0:T(8,128)S(1)} %broadcast_select_fusion.15.refs_5_.refs_4_.refs_3_.refs_2_.refs_1_.refs_0_), channel_id=1, source_target_pairs={{0,8},{1,9},{2,6},{3,7},{4,0},{5,1},{6,14},{7,15},{8,16},{9,17},{1... | collective-permute-start | bytes 1572872 | tf_op jit(solution)/shard_map/ppermute | solution.py:336
  69.9 8.4 %collective-permute-start.9 = (f32[2,4,128,128]{3,2,1,0:T(8,128)S(1)}, f32[2,4,128,128]{3,2,1,0:T(8,128)S(1)}, u32[]{:S(2)}, u32[]{:S(2)}) collective-permute-start(f32[2,4,128,128]{3,2,1,0:T(8,128)S(1)} %broadcast_select_fusion.14.refs_6_.refs_5_.refs_4_.refs_3_.refs_2_.refs_1_.refs_0_), channel_id=1, source_target_pairs={{0,8},{1,9},{2,6},{3,7},{4,0},{5,1},{6,14},{7,15},{8,16},{9,17},{1... | collective-permute-start | bytes 1572872 | tf_op jit(solution)/shard_map/ppermute | solution.py:336
  78.3 8.4 %collective-permute-start.10 = (f32[2,4,128,128]{3,2,1,0:T(8,128)S(1)}, f32[2,4,128,128]{3,2,1,0:T(8,128)S(1)}, u32[]{:S(2)}, u32[]{:S(2)}) collective-permute-start(f32[2,4,128,128]{3,2,1,0:T(8,128)S(1)} %broadcast_select_fusion.13.refs_7_.refs_6_.refs_5_.refs_4_.refs_3_.refs_2_.refs_1_.refs_0_), channel_id=1, source_target_pairs={{0,8},{1,9},{2,6},{3,7},{4,0},{5,1},{6,14},{7,15},{8,16},{9,17},{1... | collective-permute-start | bytes 1572872 | tf_op jit(solution)/shard_map/ppermute | solution.py:336
  82.3 9.3 %collective-permute-start.12 = (f32[2,4,128,128]{3,2,1,0:T(8,128)}, f32[2,4,128,128]{3,2,1,0:T(8,128)S(1)}, u32[]{:S(2)}, u32[]{:S(2)}) collective-permute-start(f32[2,4,128,128]{3,2,1,0:T(8,128)} %shard_map.145), channel_id=1, source_target_pairs={{0,1},{1,0},{2,3},{3,2},{4,5},{5,4},{6,7},{7,6},{8,9},{9,8},{10,11... | collective-permute-start | bytes 1572872 | tf_op jit(solution)/shard_map/ppermute | solution.py:336
  86.7 8.3 %collective-permute-start.11 = (f32[2,4,128,128]{3,2,1,0:T(8,128)S(1)}, f32[2,4,128,128]{3,2,1,0:T(8,128)S(1)}, u32[]{:S(2)}, u32[]{:S(2)}) collective-permute-start(f32[2,4,128,128]{3,2,1,0:T(8,128)S(1)} %collective-permute-done.10.refs_7_.refs_6_.refs_5_.refs_4_.refs_3_.refs_2_.refs_1_), channel_id=1, source_target_pairs={{0,8},{1,9},{2,6},{3,7},{4,0},{5,1},{6,14},{7,15},{8,16},{9,17},{1... | collective-permute-start | bytes 1572872 | tf_op jit(solution)/shard_map/ppermute | solution.py:336
  90.6 20.6 %copy-start.33 = (f32[2,4,128,128]{3,2,1,0:T(8,128)S(1)}, f32[2,4,128,128]{3,2,1,0:T(8,128)}, u32[]{:S(2)}) copy-start(f32[2,4,128,128]{3,2,1,0:T(8,128)} %shard_map.146) | copy-start | bytes 1572868
  90.6 17.1 %collective-permute-start.14 = (f32[2,4,128,128]{3,2,1,0:T(8,128)}, f32[2,4,128,128]{3,2,1,0:T(8,128)}, u32[]{:S(2)}, u32[]{:S(2)}) collective-permute-start(f32[2,4,128,128]{3,2,1,0:T(8,128)} %shard_map.146), channel_id=1, source_target_pairs={{0,1},{1,0},{2,3},{3,2},{4,5},{5,4},{6,7},{7,6},{8,9},{9,8},{10,11... | collective-permute-start | bytes 1572872 | tf_op jit(solution)/shard_map/ppermute | solution.py:336
  97.1 10.6 %collective-permute-start.15 = (f32[2,4,128,128]{3,2,1,0:T(8,128)}, f32[2,4,128,128]{3,2,1,0:T(8,128)}, u32[]{:S(2)}, u32[]{:S(2)}) collective-permute-start(f32[2,4,128,128]{3,2,1,0:T(8,128)} %get-tuple-element.135), channel_id=1, source_target_pairs={{0,2},{1,3},{2,0},{3,1},{4,6},{5,7},{6,4},{7,5},{8,10},{9,11},{10,... | collective-permute-start | bytes 1572872 | tf_op jit(solution)/shard_map/ppermute | solution.py:336
  102.7 8.5 %collective-permute-start.13 = (f32[2,4,128,128]{3,2,1,0:T(8,128)S(1)}, f32[2,4,128,128]{3,2,1,0:T(8,128)S(1)}, u32[]{:S(2)}, u32[]{:S(2)}) collective-permute-start(f32[2,4,128,128]{3,2,1,0:T(8,128)S(1)} %collective-permute-done.11.refs_7_.refs_6_.refs_5_.refs_4_.refs_3_.refs_2_), channel_id=1, source_target_pairs={{0,8},{1,9},{2,6},{3,7},{4,0},{5,1},{6,14},{7,15},{8,16},{9,17},{1... | collective-permute-start | bytes 1572872 | tf_op jit(solution)/shard_map/ppermute | solution.py:336
  106.8 13.5 %collective-permute-start.17 = (f32[2,4,128,128]{3,2,1,0:T(8,128)}, f32[2,4,128,128]{3,2,1,0:T(8,128)S(1)}, u32[]{:S(2)}, u32[]{:S(2)}) collective-permute-start(f32[2,4,128,128]{3,2,1,0:T(8,128)} %shard_map.147), channel_id=1, source_target_pairs={{0,1},{1,0},{2,3},{3,2},{4,5},{5,4},{6,7},{7,6},{8,9},{9,8},{10,11... | collective-permute-start | bytes 1572872 | tf_op jit(solution)/shard_map/ppermute | solution.py:336
  113.6 6.7 %collective-permute-start.18 = (f32[2,4,128,128]{3,2,1,0:T(8,128)}, f32[2,4,128,128]{3,2,1,0:T(8,128)}, u32[]{:S(2)}, u32[]{:S(2)}) collective-permute-start(f32[2,4,128,128]{3,2,1,0:T(8,128)} %get-tuple-element.137), channel_id=1, source_target_pairs={{0,2},{1,3},{2,0},{3,1},{4,6},{5,7},{6,4},{7,5},{8,10},{9,11},{10,... | collective-permute-start | bytes 1572872 | tf_op jit(solution)/shard_map/ppermute | solution.py:336
  114.3 8.6 %collective-permute-start.16 = (f32[2,4,128,128]{3,2,1,0:T(8,128)S(1)}, f32[2,4,128,128]{3,2,1,0:T(8,128)S(1)}, u32[]{:S(2)}, u32[]{:S(2)}) collective-permute-start(f32[2,4,128,128]{3,2,1,0:T(8,128)S(1)} %collective-permute-done.13.refs_7_.refs_6_.refs_5_.refs_4_.refs_3_), channel_id=1, source_target_pairs={{0,8},{1,9},{2,6},{3,7},{4,0},{5,1},{6,14},{7,15},{8,16},{9,17},{1... | collective-permute-start | bytes 1572872 | tf_op jit(solution)/shard_map/ppermute | solution.py:336
  118.5 13.6 %collective-permute-start.20 = (f32[2,4,128,128]{3,2,1,0:T(8,128)}, f32[2,4,128,128]{3,2,1,0:T(8,128)}, u32[]{:S(2)}, u32[]{:S(2)}) collective-permute-start(f32[2,4,128,128]{3,2,1,0:T(8,128)} %shard_map.148), channel_id=1, source_target_pairs={{0,1},{1,0},{2,3},{3,2},{4,5},{5,4},{6,7},{7,6},{8,9},{9,8},{10,11... | collective-permute-start | bytes 1572872 | tf_op jit(solution)/shard_map/ppermute | solution.py:336
  124.1 7.9 %collective-permute-start.21 = (f32[2,4,128,128]{3,2,1,0:T(8,128)}, f32[2,4,128,128]{3,2,1,0:T(8,128)S(1)}, u32[]{:S(2)}, u32[]{:S(2)}) collective-permute-start(f32[2,4,128,128]{3,2,1,0:T(8,128)} %get-tuple-element.139), channel_id=1, source_target_pairs={{0,2},{1,3},{2,0},{3,1},{4,6},{5,7},{6,4},{7,5},{8,10},{9,11},{10,... | collective-permute-start | bytes 1572872 | tf_op jit(solution)/shard_map/ppermute | solution.py:336
  124.7 8.6 %collective-permute-start.19 = (f32[2,4,128,128]{3,2,1,0:T(8,128)S(1)}, f32[2,4,128,128]{3,2,1,0:T(8,128)S(1)}, u32[]{:S(2)}, u32[]{:S(2)}) collective-permute-start(f32[2,4,128,128]{3,2,1,0:T(8,128)S(1)} %collective-permute-done.16.refs_7_.refs_6_.refs_5_.refs_4_), channel_id=1, source_target_pairs={{0,8},{1,9},{2,6},{3,7},{4,0},{5,1},{6,14},{7,15},{8,16},{9,17},{1... | collective-permute-start | bytes 1572872 | tf_op jit(solution)/shard_map/ppermute | solution.py:336
  128.8 14.4 %collective-permute-start.23 = (f32[2,4,128,128]{3,2,1,0:T(8,128)}, f32[2,4,128,128]{3,2,1,0:T(8,128)}, u32[]{:S(2)}, u32[]{:S(2)}) collective-permute-start(f32[2,4,128,128]{3,2,1,0:T(8,128)} %shard_map.149), channel_id=1, source_target_pairs={{0,1},{1,0},{2,3},{3,2},{4,5},{5,4},{6,7},{7,6},{8,9},{9,8},{10,11... | collective-permute-start | bytes 1572872 | tf_op jit(solution)/shard_map/ppermute | solution.py:336
  135.5 7.8 %collective-permute-start.24 = (f32[2,4,128,128]{3,2,1,0:T(8,128)S(1)}, f32[2,4,128,128]{3,2,1,0:T(8,128)}, u32[]{:S(2)}, u32[]{:S(2)}) collective-permute-start(f32[2,4,128,128]{3,2,1,0:T(8,128)S(1)} %get-tuple-element.132), channel_id=1, source_target_pairs={{0,2},{1,3},{2,0},{3,1},{4,6},{5,7},{6,4},{7,5},{8,10},{9,11},{10,... | collective-permute-start | bytes 1572872 | tf_op jit(solution)/shard_map/ppermute | solution.py:336
  136.3 8.4 %collective-permute-start.22 = (f32[2,4,128,128]{3,2,1,0:T(8,128)S(1)}, f32[2,4,128,128]{3,2,1,0:T(8,128)S(1)}, u32[]{:S(2)}, u32[]{:S(2)}) collective-permute-start(f32[2,4,128,128]{3,2,1,0:T(8,128)S(1)} %collective-permute-done.19.refs_7_.refs_6_.refs_5_), channel_id=1, source_target_pairs={{0,8},{1,9},{2,6},{3,7},{4,0},{5,1},{6,14},{7,15},{8,16},{9,17},{1... | collective-permute-start | bytes 1572872 | tf_op jit(solution)/shard_map/ppermute | solution.py:336
  140.2 14.4 %collective-permute-start.26 = (f32[2,4,128,128]{3,2,1,0:T(8,128)}, f32[2,4,128,128]{3,2,1,0:T(8,128)}, u32[]{:S(2)}, u32[]{:S(2)}) collective-permute-start(f32[2,4,128,128]{3,2,1,0:T(8,128)} %shard_map.151), channel_id=1, source_target_pairs={{0,1},{1,0},{2,3},{3,2},{4,5},{5,4},{6,7},{7,6},{8,9},{9,8},{10,11... | collective-permute-start | bytes 1572872 | tf_op jit(solution)/shard_map/ppermute | solution.py:336
  146.9 7.7 %collective-permute-start.27 = (f32[2,4,128,128]{3,2,1,0:T(8,128)}, f32[2,4,128,128]{3,2,1,0:T(8,128)S(1)}, u32[]{:S(2)}, u32[]{:S(2)}) collective-permute-start(f32[2,4,128,128]{3,2,1,0:T(8,128)} %get-tuple-element.130), channel_id=1, source_target_pairs={{0,2},{1,3},{2,0},{3,1},{4,6},{5,7},{6,4},{7,5},{8,10},{9,11},{10,... | collective-permute-start | bytes 1572872 | tf_op jit(solution)/shard_map/ppermute | solution.py:336
  147.6 8.4 %collective-permute-start.25 = (f32[2,4,128,128]{3,2,1,0:T(8,128)S(1)}, f32[2,4,128,128]{3,2,1,0:T(8,128)}, u32[]{:S(2)}, u32[]{:S(2)}) collective-permute-start(f32[2,4,128,128]{3,2,1,0:T(8,128)S(1)} %collective-permute-done.22.refs_7_.refs_6_), channel_id=1, source_target_pairs={{0,8},{1,9},{2,6},{3,7},{4,0},{5,1},{6,14},{7,15},{8,16},{9,17},{1... | collective-permute-start | bytes 1572872 | tf_op jit(solution)/shard_map/ppermute | solution.py:336
  151.5 14.4 %collective-permute-start.28 = (f32[2,4,128,128]{3,2,1,0:T(8,128)}, f32[2,4,128,128]{3,2,1,0:T(8,128)}, u32[]{:S(2)}, u32[]{:S(2)}) collective-permute-start(f32[2,4,128,128]{3,2,1,0:T(8,128)} %shard_map.152), channel_id=1, source_target_pairs={{0,1},{1,0},{2,3},{3,2},{4,5},{5,4},{6,7},{7,6},{8,9},{9,8},{10,11... | collective-permute-start | bytes 1572872 | tf_op jit(solution)/shard_map/ppermute | solution.py:336
  158.0 7.9 %collective-permute-start.29 = (f32[2,4,128,128]{3,2,1,0:T(8,128)}, f32[2,4,128,128]{3,2,1,0:T(8,128)S(1)}, u32[]{:S(2)}, u32[]{:S(2)}) collective-permute-start(f32[2,4,128,128]{3,2,1,0:T(8,128)} %get-tuple-element.128), channel_id=1, source_target_pairs={{0,2},{1,3},{2,0},{3,1},{4,6},{5,7},{6,4},{7,5},{8,10},{9,11},{10,... | collective-permute-start | bytes 1572872 | tf_op jit(solution)/shard_map/ppermute | solution.py:336
  161.4 19.0 %collective-permute-start.30 = (f32[2,4,128,128]{3,2,1,0:T(8,128)}, f32[2,4,128,128]{3,2,1,0:T(8,128)S(1)}, u32[]{:S(2)}, u32[]{:S(2)}) collective-permute-start(f32[2,4,128,128]{3,2,1,0:T(8,128)} %shard_map.154), channel_id=1, source_target_pairs={{0,1},{1,0},{2,3},{3,2},{4,5},{5,4},{6,7},{7,6},{8,9},{9,8},{10,11... | collective-permute-start | bytes 1572872 | tf_op jit(solution)/shard_map/ppermute | solution.py:336
  167.0 13.4 %collective-permute-start.31 = (f32[2,4,128,128]{3,2,1,0:T(8,128)S(1)}, f32[2,4,128,128]{3,2,1,0:T(8,128)S(1)}, u32[]{:S(2)}, u32[]{:S(2)}) collective-permute-start(f32[2,4,128,128]{3,2,1,0:T(8,128)S(1)} %get-tuple-element.126), channel_id=1, source_target_pairs={{0,2},{1,3},{2,0},{3,1},{4,6},{5,7},{6,4},{7,5},{8,10},{9,11},{10,... | collective-permute-start | bytes 1572872 | tf_op jit(solution)/shard_map/ppermute | solution.py:336
  180.3 9.6 %collective-permute-start.33 = (f32[2,64,32,128]{3,2,1,0:T(8,128)S(1)}, f32[2,64,32,128]{3,2,1,0:T(8,128)S(1)}, u32[]{:S(2)}, u32[]{:S(2)}) collective-permute-start(f32[2,64,32,128]{3,2,1,0:T(8,128)S(1)} %get-tuple-element.104), channel_id=1, source_target_pairs={{0,2},{1,3},{2,0},{3,1},{4,6},{5,7},{6,4},{7,5},{8,10},{9,11},{10,... | collective-permute-start | bytes 6291464 | tf_op jit(solution)/shard_map/ppermute | solution.py:336
  180.5 4.8 %collective-permute-start.32 = (f32[2,4,128,128]{3,2,1,0:T(8,128)S(1)}, f32[2,4,128,128]{3,2,1,0:T(8,128)S(1)}, u32[]{:S(2)}, u32[]{:S(2)}) collective-permute-start(f32[2,4,128,128]{3,2,1,0:T(8,128)S(1)} %get-tuple-element.124), channel_id=1, source_target_pairs={{0,2},{1,3},{2,0},{3,1},{4,6},{5,7},{6,4},{7,5},{8,10},{9,11},{10,... | collective-permute-start | bytes 1572872 | tf_op jit(solution)/shard_map/ppermute | solution.py:336
  185.2 4.7 %collective-permute-start.34 = (f32[2,64,16,128]{3,2,1,0:T(8,128)S(1)}, f32[2,64,16,128]{3,2,1,0:T(8,128)S(1)}, u32[]{:S(2)}, u32[]{:S(2)}) collective-permute-start(f32[2,64,16,128]{3,2,1,0:T(8,128)S(1)} %get-tuple-element.105), channel_id=1, source_target_pairs={{0,2},{1,3},{2,0},{3,1},{4,6},{5,7},{6,4},{7,5},{8,10},{9,11},{10,... | collective-permute-start | bytes 3145736 | tf_op jit(solution)/shard_map/ppermute | solution.py:336
  189.4 2.8 %collective-permute-start.35 = (f32[2,64,16,128]{3,2,1,0:T(8,128)S(1)}, f32[2,64,16,128]{3,2,1,0:T(8,128)S(1)}, u32[]{:S(2)}, u32[]{:S(2)}) collective-permute-start(f32[2,64,16,128]{3,2,1,0:T(8,128)S(1)} %get-tuple-element.106), channel_id=1, source_target_pairs={{0,2},{1,3},{2,0},{3,1},{4,6},{5,7},{6,4},{7,5},{8,10},{9,11},{10,... | collective-permute-start | bytes 3145736 | tf_op jit(solution)/shard_map/ppermute | solution.py:336
  202.0 4.2 %collective-permute-start.36 = (f32[2,64,32,128]{3,2,1,0:T(8,128)S(1)}, f32[2,64,32,128]{3,2,1,0:T(8,128)S(1)}, u32[]{:S(2)}, u32[]{:S(2)}) collective-permute-start(f32[2,64,32,128]{3,2,1,0:T(8,128)S(1)} %get-tuple-element.108), channel_id=1, source_target_pairs={{0,2},{1,3},{2,0},{3,1},{4,6},{5,7},{6,4},{7,5},{8,10},{9,11},{10,... | collective-permute-start | bytes 6291464 | tf_op jit(solution)/shard_map/ppermute | solution.py:336
  209.8 16.1 %collective-permute-start.37 = (f32[2,8,128,128]{3,2,1,0:T(8,128)S(1)}, f32[2,8,128,128]{3,2,1,0:T(8,128)S(1)}, u32[]{:S(2)}, u32[]{:S(2)}) collective-permute-start(f32[2,8,128,128]{3,2,1,0:T(8,128)S(1)} %shard_map.157), channel_id=1, source_target_pairs={{1,2},{2,1},{5,6},{6,5},{9,10},{10,9},{13,14},{14,13},{17,18},{18,... | collective-permute-start | bytes 3145736 | tf_op jit(solution)/shard_map/ppermute | solution.py:336
  212.8 13.1 %collective-permute-start.39 = (f32[2,64,16,128]{3,2,1,0:T(8,128)S(1)}, f32[2,64,16,128]{3,2,1,0:T(8,128)S(1)}, u32[]{:S(2)}, u32[]{:S(2)}) collective-permute-start(f32[2,64,16,128]{3,2,1,0:T(8,128)S(1)} %get-tuple-element.114), channel_id=1, source_target_pairs={{0,2},{1,3},{2,0},{3,1},{4,6},{5,7},{6,4},{7,5},{8,10},{9,11},{10,... | collective-permute-start | bytes 3145736 | tf_op jit(solution)/shard_map/ppermute | solution.py:336
  216.4 20.7 %collective-permute-start.38 = (f32[2,8,128,128]{3,2,1,0:T(8,128)S(1)}, f32[2,8,128,128]{3,2,1,0:T(8,128)S(1)}, u32[]{:S(2)}, u32[]{:S(2)}) collective-permute-start(f32[2,8,128,128]{3,2,1,0:T(8,128)S(1)} %shard_map.158), channel_id=1, source_target_pairs={{1,2},{2,1},{5,6},{6,5},{9,10},{10,9},{13,14},{14,13},{17,18},{18,... | collective-permute-start | bytes 3145736 | tf_op jit(solution)/shard_map/ppermute | solution.py:336
  219.2 17.9 %collective-permute-start.41 = (f32[2,64,16,128]{3,2,1,0:T(8,128)S(1)}, f32[2,64,16,128]{3,2,1,0:T(8,128)S(1)}, u32[]{:S(2)}, u32[]{:S(2)}) collective-permute-start(f32[2,64,16,128]{3,2,1,0:T(8,128)S(1)} %get-tuple-element.116), channel_id=1, source_target_pairs={{0,2},{1,3},{2,0},{3,1},{4,6},{5,7},{6,4},{7,5},{8,10},{9,11},{10,... | collective-permute-start | bytes 3145736 | tf_op jit(solution)/shard_map/ppermute | solution.py:336
  229.1 19.2 %collective-permute-start.40 = (f32[2,8,128,128]{3,2,1,0:T(8,128)S(1)}, f32[2,8,128,128]{3,2,1,0:T(8,128)S(1)}, u32[]{:S(2)}, u32[]{:S(2)}) collective-permute-start(f32[2,8,128,128]{3,2,1,0:T(8,128)S(1)} %shard_map.159), channel_id=1, source_target_pairs={{1,2},{2,1},{5,6},{6,5},{9,10},{10,9},{13,14},{14,13},{17,18},{18,... | collective-permute-start | bytes 3145736 | tf_op jit(solution)/shard_map/ppermute | solution.py:336
  240.4 19.2 %collective-permute-start.42 = (f32[2,8,128,128]{3,2,1,0:T(8,128)S(1)}, f32[2,8,128,128]{3,2,1,0:T(8,128)S(1)}, u32[]{:S(2)}, u32[]{:S(2)}) collective-permute-start(f32[2,8,128,128]{3,2,1,0:T(8,128)S(1)} %shard_map.160), channel_id=1, source_target_pairs={{1,2},{2,1},{5,6},{6,5},{9,10},{10,9},{13,14},{14,13},{17,18},{18,... | collective-permute-start | bytes 3145736 | tf_op jit(solution)/shard_map/ppermute | solution.py:336
  (35 other events, 287.1 us)
